TPU v7x, 32 devices: a whole 2x2x4 slice. The times are simulated.
32 devices in a mesh: row: 4 (over y, x), col: 8 (over z, core).
Axes of the slice: x: 2, y: 2, z: 4, core: 2. Of those that a mesh axis runs over, the one named last changes fastest.
Arguments:
- density: bfloat16 [2048, 2048], P('row', 'col'), as said below
- pattern: int32 [16, 16], replicated, may hold values from 0 to 1, as said below
Outputs:
- square: bfloat16 [2048, 2048], P('row', 'col')
- traces: float32 [2], replicated
Inputs may be any that keep to these rules, and one draw needn't show every extreme that they name: Every diagonal block of 128 x 128 entries of density is symmetric. `pattern`: block (0, 15) is always stored.
All inputs are finite; a program needn't handle non-finite values.
Results may differ from a plain program's by a relative error of at most 0.0013.
Values may be sent and summed in bfloat16 or wider, within the bound.
No kernel may reach another device: no remote copies, remote signals or barrier semaphores. Data moves between devices by JAX's collectives and lax.ppermute only.
A program may use at most 64 MiB of HBM per device.

v0:
```python
import jax
import jax.numpy as jnp
from jax import lax
from jax.sharding import PartitionSpec as P

BLK = 128


def spread(value, axis, source):
    kept = jnp.where(lax.axis_index(axis) == source, value, 0).astype(value.dtype)
    return lax.psum(kept, axis)


def block_masks(row_start, row_count, col_start, col_count, pattern):
    block_rows = row_start + jnp.arange(row_count)
    block_cols = col_start + jnp.arange(col_count)
    chosen = lax.dynamic_slice(
        pattern, (jnp.asarray(row_start), jnp.asarray(col_start)), (row_count, col_count)
    )
    diagonal_blk = block_rows[:, None] == block_cols[None, :]
    above = block_cols[None, :] >= block_rows[:, None]
    kept_blocks = ((chosen != 0) | diagonal_blk) & above
    strict_blocks = kept_blocks & jnp.logical_not(diagonal_blk)
    return (kept_blocks, strict_blocks)


def masked(values, block_mask):
    row_count, col_count = block_mask.shape
    shaped = values.reshape(row_count, BLK, col_count, BLK)
    kept = jnp.where(block_mask[:, None, :, None], shaped, jnp.zeros_like(shaped))
    return kept.reshape(values.shape)


def complete_panel(column, panel_rows, col_index, pattern):
    panel_width = column.shape[1]
    order_size = column.shape[0]
    col_blocks = panel_width // BLK
    panel_rows = panel_rows.reshape(panel_width, order_size)
    mirror_kept, mirror_strict = block_masks(
        col_index * col_blocks, col_blocks, jnp.int32(0), order_size // BLK, pattern
    )
    mirrored = masked(panel_rows, mirror_strict)
    full_column = column + mirrored.T
    return full_column


def per_device(density, pattern):
    n_row = lax.axis_size("row")
    n_col = lax.axis_size("col")
    sub_count = n_col // n_row
    row_index = lax.axis_index("row")
    col_index = lax.axis_index("col")
    panel_height, panel_width = density.shape
    order_size = panel_width * n_col
    row_blocks = panel_height // BLK
    col_blocks = panel_width // BLK
    kept_blocks, strict_blocks = block_masks(
        row_index * row_blocks, row_blocks, col_index * col_blocks, col_blocks, pattern
    )
    stored = masked(density, kept_blocks)
    column = lax.all_gather(stored, "row", axis=0, tiled=True)
    pieces = stored.reshape(sub_count, panel_width, panel_width)
    outgoing = jnp.tile(pieces, (n_col // sub_count, 1, 1))
    own_upper = lax.all_to_all(outgoing, "col", split_axis=0, concat_axis=2, tiled=True)
    panel_rows = spread(own_upper, "row", col_index // sub_count)
    full_column = complete_panel(column, panel_rows, col_index, pattern)
    own_rows = lax.dynamic_slice_in_dim(full_column, row_index * panel_height, panel_height, 0)
    global_rows = row_index * panel_height + jnp.arange(panel_height)[:, None]
    global_cols = col_index * panel_width + jnp.arange(panel_width)[None, :]
    on_diag = global_rows == global_cols
    trace_local = jnp.sum(jnp.where(on_diag, stored, jnp.zeros_like(stored)).astype(jnp.float32))
    product = jnp.dot(
        lax.all_gather(own_rows, "col", axis=1, tiled=True),
        full_column,
        preferred_element_type=jnp.float32,
    )
    trace_square = jnp.sum(jnp.where(on_diag, product, jnp.zeros_like(product)))
    trace_sums = lax.psum((trace_local, trace_square), ("row", "col"))
    square = masked(product, kept_blocks).astype(jnp.bfloat16)
    traces = jnp.stack([trace_sums[0], trace_sums[1]]) / order_size
    return (square, traces)


def solution(mesh):
    placed = (P("row", "col"), P())
    return jax.shard_map(
        per_device, mesh=mesh, in_specs=placed, out_specs=(P("row", "col"), P()), check_vma=False
    )
```

profile of v0, /device:TPU:0, one launch (start us, length us, event | category | flops | bytes accessed | tf_op | source)
XLA Modules:
  0.0 190.4 jit_solution(11425492436317604124)
XLA Ops:
  7.2 0.8 fusion.2
  8.0 0.2 broadcast_in_dim.58
  8.2 0.3 broadcast_in_dim.63
  8.5 1.0 broadcast_select_fusion.1
  9.5 0.0 copy-start.1
  9.5 0.1 copy.8
  9.7 1.1 tile.8
  10.8 6.3 %all-to-all-start = ((bf16[8,256,256]{1,2,0:T(8,128)(2,1)}), bf16[8,256,256]{1,2,0:T(8,128)(2,1)S(1)}, u32[]{:S(2)}, u32[]{:S(2)}) async-start(bf16[8,256,256]{1,2,0:T(8,128)(2,1)} %bitcast.1), calls=%async_computation | async-start | bytes 2097152 | tf_op jit(solution)/shard_map/all_to_all | solution.py:64
  17.1 0.0 all-gather.3.cloned.1.call-start
  17.1 0.0 copy-done.1
  17.1 0.8 bitcast_select_fusion
  17.9 0.0 all-gather.3.cloned.1.call-update
  17.9 0.0 all-reduce.3.cloned.1.call-start
  18.0 25.7 %all-to-all-done = bf16[8,256,256]{1,2,0:T(8,128)(2,1)S(1)} async-done(((bf16[8,256,256]{1,2,0:T(8,128)(2,1)}), bf16[8,256,256]{1,2,0:T(8,128)(2,1)S(1)}, u32[]{:S(2)}, u32[]{:S(2)}) %all-to-all-start) | async-done | bytes 1048608 | tf_op jit(solution)/shard_map/all_to_all | solution.py:64
  43.7 1.1 broadcast_select_fusion
  44.7 0.0 all-reduce.3.cloned.1.call-update
  44.8 0.0 all-gather.5.cloned.1.call-start
  44.8 0.8 not_and_fusion
  45.6 0.2 broadcast_in_dim.61
  45.8 0.3 copy.17
  46.1 1.0 copy.9
  47.1 0.8 all-gather.3.cloned.1.call-done
  47.9 55.6 %all-reduce.3.cloned.1.call-done = bf16[256,2048]{0,1:T(8,128)(2,1)} async-done(((bf16[256,2048]{0,1:T(8,128)(2,1)}), bf16[256,2048]{0,1:T(8,128)(2,1)}) %all-reduce.3.cloned.1.call-update) | async-done | bytes 1048592 | tf_op jit(solution)/shard_map/psum | solution.py:11
  103.5 1.7 bitcast_add_fusion
  105.2 0.7 constant_dynamic-slice_fusion
  105.9 0.0 all-gather.5.cloned.1.call-update
  106.0 0.0 copy-start
  106.0 30.9 %all-gather.5.cloned.1.call-done = bf16[512,2048]{1,0:T(8,128)(2,1)} async-done(((bf16[512,256]{1,0:T(8,128)(2,1)}), bf16[512,2048]{1,0:T(8,128)(2,1)}) %all-gather.5.cloned.1.call-update) | async-done | bytes 2097168 | tf_op jit(solution)/shard_map/all_gather | solution.py:73
  137.0 3.0 %select_convert_fusion = (bf16[512,256]{1,0:T(8,128)(2,1)}, f32[512,256]{1,0:T(8,128)S(1)}) fusion(pred[64,8,2,128]{3,2,1,0:T(4,128)(4,1)S(1)} %bitcast.25, bf16[512,2048]{1,0:T(8,128)(2,1)} %all-gather.5.cloned.1.call-done, bf16[2048,256]{1,0:T(8,128)(2,1)S(1)} %bitcast_add_fusion), kind=kOutput, calls=%fused_computation.7 | convolution fusion | flops 537001984 | bytes 4063232 | tf_op jit(solution)/shard_map/dot_general | solution.py:72
  140.0 0.0 copy-done
  140.0 0.8 convert_reduce_fusion
  140.8 41.2 %all-reduce = (f32[1]{0:T(128)}, f32[1]{0:T(128)}) all-reduce(f32[1]{0:T(128)} %bitcast.7, f32[1]{0:T(128)} %bitcast.6), channel_id=1, replica_groups=mesh['row'=4,'col'=8] {'row','col'}, use_global_device_ids=true, to_apply=%region_4.5 | all-reduce | flops 2 | bytes 16 | tf_op jit(solution)/shard_map/psum | solution.py:78
  182.0 1.8 maximum_multiply_fusion
  (4 shorter events, 0.0 us)
Async XLA Ops:
  9.5 7.6 %copy-start.1 = (bf16[512,256]{1,0:T(8,128)(2,1)S(1)}, bf16[512,256]{1,0:T(8,128)(2,1)}, u32[]{:S(2)}) copy-start(bf16[512,256]{1,0:T(8,128)(2,1)} %param.2) | copy-start | bytes 786436
  10.8 32.9 %all-to-all-start = ((bf16[8,256,256]{1,2,0:T(8,128)(2,1)}), bf16[8,256,256]{1,2,0:T(8,128)(2,1)S(1)}, u32[]{:S(2)}, u32[]{:S(2)}) async-start(bf16[8,256,256]{1,2,0:T(8,128)(2,1)} %bitcast.1), calls=%async_computation | async-start | bytes 2097152 | tf_op jit(solution)/shard_map/all_to_all | solution.py:64
  17.1 30.8 %all-gather.3.cloned.1.call-start = ((), (), s32[]{:S(2)}) async-start(), calls=%async_computation.1 | async-start | bytes 1310720 | tf_op jit(solution)/shard_map/all_gather | solution.py:61
  17.9 85.6 %all-reduce.3.cloned.1.call-start = ((), (), s32[]{:S(2)}) async-start(), calls=%async_computation.2 | async-start | bytes 2097152 | tf_op jit(solution)/shard_map/psum | solution.py:11
  44.8 92.2 %all-gather.5.cloned.1.call-start = ((), (), s32[]{:S(2)}) async-start(), calls=%async_computation.3 | async-start | bytes 2359296 | tf_op jit(solution)/shard_map/all_gather | solution.py:73
  106.0 34.0 %copy-start = (bf16[512,256]{1,0:T(8,128)(2,1)S(1)}, bf16[512,256]{1,0:T(8,128)(2,1)}, u32[]{:S(2)}) copy-start(bf16[512,256]{1,0:T(8,128)(2,1)} %bitcast_select_fusion) | copy-start | bytes 786436
Sparse Core Ops, SparseCore 0:
  19.8 28.0 all-gather.2
  50.9 52.5 all-reduce.2
  106.1 30.8 all-gather.4
where the time goes:
time: 191 us; the launch traced here: 190 us
  waiting for transfers between devices  113 us (59%)
  blocking collectives  41.2 us (22%)
  between operations  13.9 us (7%)
  other arithmetic  8.74 us (5%)
  starting transfers between devices  6.45 us (3%)
  local copies, waits for them, and re-layouts  3.99 us (2%)
  matrix products  3.01 us (2%)
    psum x1, waiting for transfers between devices, spread(): return lax.psum(kept, axis)  55.6 us
    psum x1, blocking collectives, per_device(): trace_sums = lax.psum((trace_local, trace_square), ('row', 'col'))  41.2 us
    all_gather x1, waiting for transfers between devices, per_device(): lax.all_gather(own_rows, 'col', axis=1, tiled=True)  30.9 us
    all_to_all x1, waiting for transfers between devices, per_device(): lax.all_to_all(outgoing, 'col', split_axis=0, concat_axis=2, tiled=True)  25.7 us
    all_to_all x1, starting transfers between devices, per_device(): lax.all_to_all(outgoing, 'col', split_axis=0, concat_axis=2, tiled=True)  6.33 us
  transfers between devices with their start and end apart: 4, of which 4 were waited for; matrix products, arithmetic and copies ran while one was open for 2% of the time, Pallas kernels for 0%

commit v1 on v0

v1 whole, which is shorter than its diff:
```python
import functools
import jax
import jax.numpy as jnp
from jax import lax
from jax.experimental import pallas as pl
from jax.experimental.pallas import tpu as pltpu
from jax.sharding import PartitionSpec as P

BLK = 128
VMEM = pl.BlockSpec(memory_space=pltpu.VMEM)
SMEM = pl.BlockSpec(memory_space=pltpu.SMEM)
PARAMS = pltpu.CompilerParams(vmem_limit_bytes=40 * 2**20)


def symmetric_kernel(sub, place, pattern, density, *rest):
    pieces, full = rest[:sub], rest[sub]
    row, col = place[0], place[1]
    height, width = density.shape
    per_piece = width // BLK
    row_blocks = height // BLK
    own_slot = lax.rem(col, sub)
    on_diagonal = row == col // sub
    for t in range(sub):
        slot = lax.rem(own_slot + sub - t, sub)
        for a in range(per_piece):
            i = slot * per_piece + a
            block_row = row * row_blocks + i
            rows = pl.ds(pl.multiple_of(i * BLK, BLK), BLK)
            for b in range(per_piece):
                block_col = col * per_piece + b
                cols = pl.ds(b * BLK, BLK)
                mirror = pieces[t][b * BLK : (b + 1) * BLK, a * BLK : (a + 1) * BLK]
                if t == 0:
                    start = pl.multiple_of((own_slot * per_piece + b) * BLK, BLK)
                    mine = density[pl.ds(start, BLK), a * BLK : (a + 1) * BLK]
                    mirror = jnp.where(on_diagonal, mine, mirror)
                chosen = pattern[jnp.minimum(block_row, block_col), jnp.maximum(block_row, block_col)] != 0
                upper = (block_row == block_col) | ((block_row < block_col) & chosen)
                lower = (block_row > block_col) & chosen
                zero = jnp.zeros((BLK, BLK), full.dtype)
                value = jnp.where(lower, mirror.T, zero)
                full[rows, cols] = jnp.where(upper, density[rows, cols], value)


def product_kernel(lines, planes, place, pattern, *refs):
    left = refs[: 2 * lines]
    right = refs[2 * lines : 2 * lines + planes]
    out, panel = refs[2 * lines + planes :]
    row, col = place[0], place[1]
    height, width = out.shape
    core, line = lax.rem(col, 2), col // 2
    for d in range(planes):
        start = pl.multiple_of((row ^ d) * height, height)
        panel[pl.ds(start, height), :] = right[d][...]
    total = jnp.zeros((height, width), jnp.float32)
    for e in range(lines):
        for s in range(2):
            start = pl.multiple_of(((line ^ e) * 2 + (core ^ s)) * width, width)
            total += jnp.dot(
                left[2 * e + s][...],
                panel[pl.ds(start, width), :],
                preferred_element_type=jnp.float32,
            )
    for i in range(height // BLK):
        for j in range(width // BLK):
            block_row = row * (height // BLK) + i
            block_col = col * (width // BLK) + j
            kept = (block_row == block_col) | ((block_row < block_col) & (pattern[block_row, block_col] != 0))
            block = total[i * BLK : (i + 1) * BLK, j * BLK : (j + 1) * BLK]
            out[i * BLK : (i + 1) * BLK, j * BLK : (j + 1) * BLK] = jnp.where(
                kept, block, jnp.zeros_like(block)
            ).astype(out.dtype)


def block_weights(pattern, row, col, row_blocks, col_blocks):
    block_rows = row * row_blocks + jnp.arange(row_blocks)
    block_cols = col * col_blocks + jnp.arange(col_blocks)
    chosen = lax.dynamic_slice(pattern, (row * row_blocks, col * col_blocks), (row_blocks, col_blocks))
    diagonal = block_rows[:, None] == block_cols[None, :]
    strict = (block_cols[None, :] > block_rows[:, None]) & (chosen != 0)
    return jnp.where(diagonal, 1.0, jnp.where(strict, 2.0, 0.0)).astype(jnp.float32)


def any_mesh(density, pattern):
    n_row = lax.axis_size("row")
    n_col = lax.axis_size("col")
    sub = n_col // n_row
    row = lax.axis_index("row")
    col = lax.axis_index("col")
    height, width = density.shape
    order_size = width * n_col
    place = jnp.stack([row, col]).astype(jnp.int32)

    pieces = []
    for t in range(sub):
        pairs = []
        for q in range(n_row):
            for c in range(n_col):
                p = (c + t) % sub
                if c > q * sub + p:
                    pairs.append((q * n_col + c, (c // sub) * n_col + q * sub + p))
        start = lax.rem(col + t, sub) * width
        piece = lax.dynamic_slice_in_dim(density, start, width, 0)
        pieces.append(lax.ppermute(piece, ("row", "col"), pairs))
    full = pl.pallas_call(
        functools.partial(symmetric_kernel, sub),
        out_shape=jax.ShapeDtypeStruct(density.shape, density.dtype),
        in_specs=[SMEM, SMEM] + [VMEM] * (sub + 1),
        out_specs=VMEM,
        compiler_params=PARAMS,
    )(place, pattern, density, *pieces)

    weights = block_weights(pattern, row, col, height // BLK, width // BLK)
    values = density.astype(jnp.float32).reshape(height // BLK, BLK, width // BLK, BLK)
    squares = jnp.sum(values * values, axis=(1, 3))
    rows_at = row * height + jnp.arange(height)[:, None]
    cols_at = col * width + jnp.arange(width)[None, :]
    diagonal = jnp.where(rows_at == cols_at, density.astype(jnp.float32), 0.0)
    sums = jnp.stack([jnp.sum(diagonal), jnp.sum(jnp.where(weights > 0, weights * squares, 0.0))])
    step = 1
    while step < n_row:
        sums = sums + lax.ppermute(sums, "row", [(i, i ^ step) for i in range(n_row)])
        step *= 2
    step = 1
    while step < n_col:
        sums = sums + lax.ppermute(sums, "col", [(i, i ^ step) for i in range(n_col)])
        step *= 2
    traces = sums / order_size

    right = [full]
    for d in range(1, n_row):
        right.append(lax.ppermute(full, "row", [(i, i ^ d) for i in range(n_row)]))
    left = []
    for e in range(n_col // 2):
        shard = full
        if e > 0:
            shard = lax.ppermute(full, "col", [(i, i ^ (2 * e)) for i in range(n_col)])
        other = lax.ppermute(shard, "col", [(i, i ^ 1) for i in range(n_col)])
        left += [shard, other]
    square = pl.pallas_call(
        functools.partial(product_kernel, n_col // 2, n_row),
        out_shape=jax.ShapeDtypeStruct(density.shape, density.dtype),
        in_specs=[SMEM, SMEM] + [VMEM] * (len(left) + len(right)),
        out_specs=VMEM,
        scratch_shapes=[pltpu.VMEM((order_size, width), density.dtype)],
        compiler_params=PARAMS,
    )(place, pattern, *left, *right)
    return (square, traces)

GRID_PARAMS = pltpu.CompilerParams(vmem_limit_bytes=14 * 2**20)
USES = 8
FIRST = 5
SECOND = 3
SUMS = 2 + SECOND
BASE = SUMS + 2 * FIRST
SEEN = ((), (0,), (1, 3), (2,))

MESSAGES = (
    (0, (0, 0), 1, (0, 0, 1), (0, 3, 1)),
    (0, (0, 2), 0, (0, 1, 0), (0, 0, 0)),
    (0, (0, 1), 1, (0, 1, 1), (1, 2, 0)),
    (0, (0, 1), 0, (0, 2, 0), (0, 3, 0)),
    (0, (2, 3), 0, (0, 3, 0), (1, 3, 1)),
    (0, (2, 3), 1, (0, 3, 1), (1, 2, 1)),
    (0, (1, 3), 1, (1, 2, 1), (0, 1, 1)),
    (0, (1, 3), 0, (1, 3, 0), (0, 1, 0)),
    (0, (1, 2), 1, (1, 3, 1), (2, 3, 0)),
    (0, (0, 3), 0, (2, 3, 0), (3, 3, 0)),
    (0, (0, 3), 1, (2, 3, 1), (3, 3, 1)),
    (0, (1, 1), 0, (3, 1, 0), (1, 3, 0)),
    (0, (1, 2), 0, (3, 2, 0), (2, 2, 0)),
    (0, (1, 3), 0, (3, 3, 0), (1, 1, 1)),
    (0, (1, 3), 1, (3, 3, 1), (2, 3, 1)),
    (1, (0, 3), 1, (0, 2, 1), (0, 1, 0)),
    (1, (1, 3), 0, (0, 3, 0), (2, 3, 0)),
    (1, (2, 3), 1, (0, 3, 1), (0, 2, 0)),
    (1, (0, 0), 1, (1, 0, 1), (0, 2, 1)),
    (1, (0, 1), 0, (1, 1, 0), (1, 3, 0)),
    (1, (1, 1), 1, (1, 2, 1), (1, 3, 1)),
    (1, (3, 3), 0, (1, 3, 0), (0, 3, 0)),
    (1, (1, 2), 1, (1, 3, 1), (2, 2, 1)),
    (1, (0, 1), 0, (2, 1, 0), (1, 2, 0)),
    (1, (0, 2), 0, (2, 2, 0), (2, 3, 1)),
    (1, (0, 2), 1, (2, 2, 1), (0, 0, 1)),
    (1, (0, 3), 0, (2, 3, 0), (0, 1, 1)),
    (1, (3, 3), 1, (2, 3, 1), (0, 3, 1)),
    (1, (2, 2), 1, (3, 2, 1), (1, 2, 1)),
    (2, (0, 0), 0, (0, 0, 0), (0, 3, 1)),
    (2, (2, 2), 0, (0, 2, 0), (1, 2, 0)),
    (2, (0, 3), 1, (0, 2, 1), (0, 0, 1)),
    (2, (0, 3), 0, (0, 3, 0), (0, 0, 0)),
    (2, (0, 2), 1, (0, 3, 1), (2, 3, 1)),
    (2, (1, 2), 0, (1, 1, 0), (0, 1, 1)),
    (2, (0, 1), 1, (1, 1, 1), (1, 3, 0)),
    (2, (1, 3), 1, (1, 2, 1), (1, 1, 1)),
    (2, (1, 2), 0, (1, 3, 0), (2, 3, 0)),
    (2, (0, 0), 0, (2, 0, 0), (0, 2, 0)),
    (2, (0, 1), 1, (2, 1, 1), (0, 3, 0)),
    (2, (2, 3), 0, (2, 2, 0), (0, 2, 1)),
    (2, (2, 3), 1, (2, 3, 1), (1, 3, 1)),
    (2, (1, 2), 1, (3, 2, 1), (0, 1, 0)),
    (2, (2, 3), 0, (3, 3, 0), (1, 2, 1)),
)


def wanted(r, z):
    if r > z:
        return [None] * USES
    return [(min(r, j), max(r, j)) for j in range(4)] + [(min(z, j), max(z, j)) for j in range(4)]


def first_round(devices):
    def ring(r, z, k, up):
        step = 1 if (k == 0) == up else -1
        return (r, z + step, k) if 0 <= z + step < 4 else (r, z, 1 - k)

    return [[(d, ring(*d, up)) for d in devices] for up in (True, False)] + [
        [((r, z, k), (r ^ bit, z, k)) for r, z, k in devices] for bit in (1, 2)
    ]


def closed(pairs, devices):
    def hops(a, b):
        return abs(a[1] - b[1]) + bin(a[0] ^ b[0]).count("1")

    sends, receives = {a for a, _ in pairs}, {b for _, b in pairs}
    free = sorted((hops(a, b), a, b) for a in devices for b in devices if a not in sends and b not in receives and a != b)
    extra = []
    for _, a, b in free:
        if a not in sends and b not in receives:
            sends.add(a)
            receives.add(b)
            extra.append((a, b))
    return pairs + extra


def schedule():
    devices = [(r, z, k) for r in range(4) for z in range(4) for k in range(2)]
    first = first_round(devices)
    held = {d: [((d[0], d[1]), d[2])] for d in devices}
    for pairs in first:
        for a, b in pairs:
            held[b].append(((a[0], a[1]), a[2]))
    second = [[] for _ in range(SECOND)]
    later = {d: [None] * SECOND for d in devices}
    sends = {d: [-1] * SECOND for d in devices}
    for i, tile, half, a, b in MESSAGES:
        second[i].append((a, b))
        sends[a][i] = held[a].index((tile, half))
        later[b][i] = (tile, half)
    second = [closed(pairs, devices) for pairs in second]
    rows = []
    for r, z, k in devices:
        row = [r, 2 * z + k] + sends[r, z, k]
        added = {(r, z), (r ^ 1, z), (r ^ 2, z)} | {(r, j) for j in SEEN[z]}
        for s, (tile, half) in enumerate(held[r, z, k]):
            ours = tile in added and half == k and (s == 0 or tile != (r, z))
            row += [tile[0], 2 * tile[1] + half] if ours else [-1, -1]
        taken = set()
        for shards in (held, later):
            here = shards[r, z, k] + shards[r, z, 1 - k]
            halves = [[], []]
            for u, tile in enumerate(wanted(r, z)):
                found = tile and u not in taken and (tile, 0) in here and (tile, 1) in here
                if found:
                    taken.add(u)
                for h in range(2):
                    halves[h].append(here.index((tile, h)) if found else -1)
            row += halves[0] + halves[1]
        assert r > z or len(taken) == USES
        rows.append(row)

    def flat(pairs):
        assert len({a for a, _ in pairs}) == len({b for _, b in pairs}) == len(devices)
        return [(8 * a[0] + 2 * a[1] + a[2], 8 * b[0] + 2 * b[1] + b[2]) for a, b in pairs]

    return [flat(p) for p in first], [flat(p) for p in second], rows


class Scalars:
    def __init__(self, info, rows):
        self.info, self.rows, self.width = info, rows, info.shape[1]

    def plan(self, i):
        return self.info[i // self.width, i % self.width] if isinstance(i, int) else self.info[
            lax.div(i, self.width), lax.rem(i, self.width)
        ]

    def kept(self, i, j):
        low, high = jnp.minimum(i, j), jnp.maximum(i, j)
        return (low == high) | (self.info[self.rows + low, high] != 0)


def partial_kernel(rows, info, *refs):
    scalars = Scalars(info, rows)
    shards, out, squares, diagonals = refs[:FIRST], refs[FIRST], refs[FIRST + 1], refs[FIRST + 2]
    squares[...] = jnp.zeros_like(squares)
    diagonals[...] = jnp.zeros_like(diagonals)
    for s, ref in enumerate(shards):
        row, col = scalars.plan(SUMS + 2 * s), scalars.plan(SUMS + 2 * s + 1)
        row_blocks, col_blocks = ref.shape[0] // BLK, ref.shape[1] // BLK

        @pl.when((row >= 0) & (row <= col // 2))
        def _():
            zero = jnp.zeros((BLK, BLK), jnp.float32)
            total = zero
            for a in range(row_blocks):
                for b in range(col_blocks):
                    i, j = row * row_blocks + a, col * col_blocks + b
                    block = ref[a * BLK : (a + 1) * BLK, b * BLK : (b + 1) * BLK].astype(jnp.float32)
                    block = jnp.where((i <= j) & scalars.kept(i, j), block, zero)
                    total += jnp.where(i == j, 1.0, 2.0) * (block * block)
            squares[...] += total

            @pl.when(row == col // 2)
            def _():
                rows_at = lax.broadcasted_iota(jnp.int32, (BLK, BLK), 0)
                cols_at = lax.broadcasted_iota(jnp.int32, (BLK, BLK), 1)
                for b in range(col_blocks):
                    start = pl.multiple_of((lax.rem(col, 2) * col_blocks + b) * BLK, BLK)
                    block = ref[pl.ds(start, BLK), b * BLK : (b + 1) * BLK].astype(jnp.float32)
                    diagonals[...] += jnp.where(rows_at == cols_at, block, zero)

    at_col = lax.broadcasted_iota(jnp.int32, out.shape, 1)
    out[...] = jnp.where(
        at_col == 0, jnp.sum(diagonals[...]), jnp.where(at_col == 1, jnp.sum(squares[...]), 0.0)
    )


def choose_kernel(rows, info, *refs):
    scalars = Scalars(info, rows)
    held, outs = refs[:FIRST], refs[FIRST:]
    for c, out in enumerate(outs):
        for s, ref in enumerate(held):
            @pl.when(scalars.plan(2 + c) == s)
            def _():
                out[...] = ref[...]


def copy_kernel(source, out):
    out[...] = source[...]


def pack_kernel(*refs):
    out = refs[-1]
    for i, ref in enumerate(refs[:-1]):
        out[i] = ref[...]


def copy_kernel(source, out):
    out[...] = source[...]


def pack_kernel(*refs):
    out = refs[-1]
    for i, ref in enumerate(refs[:-1]):
        out[i] = ref[...]


def choose_kernel(rows, info, *refs):
    scalars = Scalars(info, rows)
    held, outs = refs[:FIRST], refs[FIRST:]
    for c, out in enumerate(outs):
        for s, ref in enumerate(held):
            @pl.when(scalars.plan(2 + c) == s)
            def _():
                out[...] = ref[...]


def place_tiles(base, scalars, shards, left, right, raw):
    row, col = scalars.plan(0), scalars.plan(1)
    line, core = col // 2, lax.rem(col, 2)
    tile = left.shape[1]
    width = right.shape[2]
    blocks, half = tile // BLK, width // BLK
    zero = jnp.zeros((BLK, BLK), left.dtype)

    def stored(a, b):
        start = pl.multiple_of((b // 2) * tile + a * BLK, BLK)
        cols = pl.ds(pl.multiple_of(lax.rem(b, 2) * BLK, BLK), BLK) if not isinstance(b, int) else pl.ds((b % 2) * BLK, BLK)
        return raw[pl.ds(start, BLK), cols]

    def fetch(use):
        for half in range(2):
            for s, ref in enumerate(shards):
                @pl.when(scalars.plan(base + half * USES + use) == s)
                def _():
                    raw[half * tile : (half + 1) * tile, :] = ref[...]

    def left_tile(j, carry):
        slot = scalars.plan(base + j)

        @pl.when(slot >= 0)
        def _():
            fetch(j)

            def fill(block_of):
                for a in range(blocks):
                    for b in range(blocks):
                        keep = scalars.kept(row * blocks + a, j * blocks + b)
                        left[j, a * BLK : (a + 1) * BLK, b * BLK : (b + 1) * BLK] = jnp.where(keep, block_of(a, b), zero)

            @pl.when(j > row)
            def _():
                fill(stored)

            @pl.when(j < row)
            def _():
                fill(lambda a, b: stored(b, a).T)

            @pl.when(j == row)
            def _():
                fill(lambda a, b: stored(a, b) if a <= b else stored(b, a).T)

        return carry

    def right_tile(j, carry):
        slot = scalars.plan(base + 4 + j)

        @pl.when(slot >= 0)
        def _():
            fetch(4 + j)

            def fill(block_of):
                for a in range(blocks):
                    for b in range(half):
                        keep = scalars.kept(j * blocks + a, col * half + b)
                        right[j, a * BLK : (a + 1) * BLK, b * BLK : (b + 1) * BLK] = jnp.where(keep, block_of(a, b), zero)

            def direct(a, b):
                start = pl.multiple_of(core * tile + a * BLK, BLK)
                return raw[pl.ds(start, BLK), b * BLK : (b + 1) * BLK]

            def mirrored(a, b):
                start = pl.multiple_of((a // 2) * tile + (core * half + b) * BLK, BLK)
                return raw[pl.ds(start, BLK), (a % 2) * BLK : (a % 2 + 1) * BLK].T

            @pl.when(j < line)
            def _():
                fill(direct)

            @pl.when(j > line)
            def _():
                fill(mirrored)

            @pl.when(j == line)
            def _():
                fill(lambda a, b: jnp.where(a <= core * half + b, direct(a, b), mirrored(a, b)))

        return carry

    lax.fori_loop(0, 4, left_tile, 0)
    lax.fori_loop(0, 4, right_tile, 0)


def panels_kernel(base, count, rows, info, *refs):
    packed, left, right, raw = refs[count:]
    shards = list(refs[:count]) + [packed.at[i] for i in range(count)]
    place_tiles(base, Scalars(info, rows), shards, left, right, raw)


def grid_product_kernel(base, count, rows, info, *refs):
    left, right, out, raw = refs[2 * count + 2 :]
    scalars = Scalars(info, rows)
    place_tiles(base, scalars, refs[: 2 * count], left, right, raw)
    row, col = scalars.plan(0), scalars.plan(1)
    height, width = out.shape
    blocks, half = height // BLK, width // BLK

    @pl.when(row <= col // 2)
    def _():
        total = jnp.zeros((height, width), jnp.float32)
        for j in range(4):
            total += jnp.dot(left[j], right[j], preferred_element_type=jnp.float32)
        for a in range(blocks):
            for b in range(half):
                i, j = row * blocks + a, col * half + b
                keep = (i <= j) & scalars.kept(i, j)
                block = total[a * BLK : (a + 1) * BLK, b * BLK : (b + 1) * BLK]
                out[a * BLK : (a + 1) * BLK, b * BLK : (b + 1) * BLK] = jnp.where(
                    keep, block, jnp.zeros_like(block)
                ).astype(out.dtype)

    @pl.when(row > col // 2)
    def _():
        out[...] = jnp.zeros_like(out)


def chip_grid(density, pattern):
    height, width = density.shape
    n_col = lax.axis_size("col")
    n_devices = lax.axis_size("row") * n_col
    order_size = width * lax.axis_size("col")
    dtype = density.dtype
    axes = ("row", "col")
    first, second, rows = schedule()
    me = lax.axis_index("row") * lax.axis_size("col") + lax.axis_index("col")
    lanes = pattern.shape[1]
    plan_rows = -(-len(rows[0]) // lanes)
    table = jnp.asarray([row + [0] * (plan_rows * lanes - len(row)) for row in rows], jnp.int32)
    plan = lax.dynamic_index_in_dim(table.reshape(n_devices, plan_rows, lanes), me, 0, keepdims=False)
    plan = jnp.concatenate([plan, pattern], axis=0)
    shard = jax.ShapeDtypeStruct(density.shape, dtype)
    raw = pltpu.VMEM((2 * height, width), dtype)
    panels = [
        jax.ShapeDtypeStruct((4, height, height), dtype),
        jax.ShapeDtypeStruct((4, height, width), dtype),
    ]

    def call(kernel, out_shape, smem, args, scratch=(), out_specs=VMEM, aliases=None, flops=0):
        return pl.pallas_call(
            kernel,
            out_shape=out_shape,
            in_specs=[SMEM] * smem + [VMEM] * (len(args) - smem),
            out_specs=out_specs,
            scratch_shapes=list(scratch),
            input_output_aliases=aliases or {},
            compiler_params=GRID_PARAMS,
            cost_estimate=pl.CostEstimate(flops=flops, bytes_accessed=2**23, transcendentals=0) if flops else None,
        )(*args)

    def share(value):
        return lax.ppermute(value, axes, [(d, d ^ 1) for d in range(n_devices)])

    def part_from(parts, row_bits, col_bits):
        return lax.ppermute(parts, axes, [(d, d ^ (row_bits * n_col + col_bits)) for d in range(n_devices)])

    came = [lax.ppermute(density, axes, pairs) for pairs in first]
    came[-1], own = lax.optimization_barrier((came[-1], call(copy_kernel, shard, 0, [density])))
    held = [own] + came
    chosen = call(
        functools.partial(choose_kernel, plan_rows), [shard] * SECOND, 1, [plan] + held, (), [VMEM] * SECOND
    )
    tied = lax.optimization_barrier((*chosen, *held))
    chosen, held = tied[:SECOND], list(tied[SECOND:])
    later = [lax.ppermute(value, axes, pairs) for value, pairs in zip(chosen, second)]
    packed = share(call(pack_kernel, jax.ShapeDtypeStruct((FIRST, height, width), dtype), 0, held))
    parts = call(
        functools.partial(partial_kernel, plan_rows),
        jax.ShapeDtypeStruct((8, 128), jnp.float32),
        1,
        [plan] + held,
        [pltpu.VMEM((BLK, BLK), jnp.float32)] * 2,
    )
    packed, parts = lax.optimization_barrier((packed, parts + part_from(parts, 0, 1)))
    received = part_from(parts, 3, 2)
    left, right = call(
        functools.partial(panels_kernel, BASE, FIRST, plan_rows),
        panels,
        1,
        [plan] + held + [packed],
        [raw],
        [VMEM] * 2,
        flops=2**31,
    )
    *later, left, right, received = lax.optimization_barrier((*later, left, right, received))
    parts = parts + received
    received = part_from(parts, 0, 4)
    inputs = [plan] + later + [share(value) for value in later] + [left, right]
    square = call(
        functools.partial(grid_product_kernel, BASE + 2 * USES, SECOND, plan_rows),
        panels + [shard],
        1,
        inputs,
        [raw],
        [VMEM] * 3,
        {len(inputs) - 2: 0, len(inputs) - 1: 1},
        flops=2**31,
    )[2]
    square, received = lax.optimization_barrier((square, received))
    traces = (parts + received)[0, :2] / order_size
    return (square, traces)


def per_device(density, pattern):
    if lax.axis_size("row") == 4 and lax.axis_size("col") == 8 and density.shape[0] == 2 * density.shape[1]:
        return chip_grid(density, pattern)
    return any_mesh(density, pattern)


def solution(mesh):
    placed = (P("row", "col"), P())
    return jax.shard_map(
        per_device, mesh=mesh, in_specs=placed, out_specs=(P("row", "col"), P()), check_vma=False
    )
```

time: 191 us -> 34.1 us (0.18)
  waiting for transfers between devices: 113 us -> 8.4 us
  blocking collectives: 41.2 us -> 0 us
  between operations: 13.9 us -> 0.72 us
  Pallas kernels: 0 us -> 7.64 us
  other arithmetic: 8.74 us -> 1.23 us
  starting transfers between devices: 6.45 us -> 13.9 us
  matrix products: 3.01 us -> 0 us
  local copies, waits for them, and re-layouts: 3.99 us -> 1.67 us
    psum x1 -> x0, waiting for transfers between devices: 55.6 us -> none  [spread(): return lax.psum(kept, axis)]
    psum x1 -> x0, blocking collectives: 41.2 us -> none  [per_device(): trace_sums = lax.psum((trace_local, trace_square), ('row', 'col'))]
    all_gather x2 -> x0, waiting for transfers between devices: 31.7 us -> none  [the longest x1 30.9 us: per_device(): lax.all_gather(own_rows, 'col', axis=1, tiled=True)]
    all_to_all x1 -> x0, waiting for transfers between devices: 25.7 us -> none  [per_device(): lax.all_to_all(outgoing, 'col', split_axis=0, concat_axis=2, tiled=True)]
    ppermute x0 -> x14, starting transfers between devices: none -> 13.9 us  [the longest x4 6.1 us: chip_grid(): came = [lax.ppermute(density, axes, pairs) for pairs in first]]
    ppermute x0 -> x14, waiting for transfers between devices: none -> 8.4 us  [the longest x4 4.18 us: chip_grid(): came = [lax.ppermute(density, axes, pairs) for pairs in first]]
    pallas_call x0 -> x6, Pallas kernels: none -> 7.64 us  [call(): pl.pallas_call(kernel, out_shape=out_shape, in_specs=[SMEM] * smem + [VME...]
    all_to_all x1 -> x0, starting transfers between devices: 6.33 us -> none  [per_device(): lax.all_to_all(outgoing, 'col', split_axis=0, concat_axis=2, tiled=True)]
  transfers between devices with their start and end apart: 4 -> 14, of which waited for: 4 -> 7; matrix products, arithmetic and copies ran while one was open for 2% -> 4% of each run, Pallas kernels for 0% -> 20%
where the time goes in v1:
time: 34.1 us; the launch traced here: 33.5 us
  starting transfers between devices  13.9 us (41%)
  waiting for transfers between devices  8.4 us (25%)
  Pallas kernels  7.64 us (22%)
  local copies, waits for them, and re-layouts  1.67 us (5%)
  other arithmetic  1.23 us (4%)
  between operations  0.72 us (2%)
    pallas_call x6, Pallas kernels, call(): pl.pallas_call(kernel, out_shape=out_shape, in_specs=[SMEM] * smem + [VME...  7.64 us
    ppermute x4, starting transfers between devices, chip_grid(): came = [lax.ppermute(density, axes, pairs) for pairs in first]  6.1 us
    ppermute x3, starting transfers between devices, chip_grid(): lax.ppermute(value, axes, pairs)  5.15 us
    ppermute x4, waiting for transfers between devices, chip_grid(): came = [lax.ppermute(density, axes, pairs) for pairs in first]  4.18 us
    ppermute x3, waiting for transfers between devices, chip_grid(): lax.ppermute(value, axes, pairs)  2.63 us
    ppermute x3, starting transfers between devices, part_from(): lax.ppermute(parts, axes, [(d, d ^ row_bits * n_col + col_bits) for d in...  1.78 us
    ppermute x3, waiting for transfers between devices, part_from(): lax.ppermute(parts, axes, [(d, d ^ row_bits * n_col + col_bits) for d in...  1.58 us
    unnamed x2, local copies, waits for them, and re-layouts  0.98 us
  transfers between devices with their start and end apart: 14, of which 7 were waited for; matrix products, arithmetic and copies ran while one was open for 4% of the time, Pallas kernels for 20%

profile of v1, /device:TPU:0, one launch (start us, length us, event | category | flops | bytes accessed | tf_op | source)
XLA Modules:
  0.0 33.5 jit_solution(15221594324717386246)
XLA Ops:
  0.6 3.0 %collective-permute-start = (bf16[512,256]{1,0:T(8,128)(2,1)}, bf16[512,256]{1,0:T(8,128)(2,1)S(1)}, u32[]{:S(2)}, u32[]{:S(2)}) collective-permute-start(bf16[512,256]{1,0:T(8,128)(2,1)} %source.1), channel_id=1, source_target_pairs={{0,16},{1,17},{2,18},{3,19},{4,20},{5,21},{6,22},{7,23},{8,24},{9,... | collective-permute-start | bytes 786440 | tf_op jit(solution)/shard_map/ppermute | solution.py:528
  3.7 1.6 %collective-permute-start.1 = (bf16[512,256]{1,0:T(8,128)(2,1)}, bf16[512,256]{1,0:T(8,128)(2,1)S(1)}, u32[]{:S(2)}, u32[]{:S(2)}) collective-permute-start(bf16[512,256]{1,0:T(8,128)(2,1)} %source.1), channel_id=1, source_target_pairs={{0,2},{1,0},{2,4},{3,1},{4,6},{5,3},{6,7},{7,5},{8,10},{9,8},{10,1... | collective-permute-start | bytes 786440 | tf_op jit(solution)/shard_map/ppermute | solution.py:528
  5.2 1.5 %collective-permute-start.3 = (bf16[512,256]{1,0:T(8,128)(2,1)}, bf16[512,256]{1,0:T(8,128)(2,1)S(1)}, u32[]{:S(2)}, u32[]{:S(2)}) collective-permute-start(bf16[512,256]{1,0:T(8,128)(2,1)} %source.1), channel_id=1, source_target_pairs={{0,8},{1,9},{2,10},{3,11},{4,12},{5,13},{6,14},{7,15},{8,0},{9,1},... | collective-permute-start | bytes 786440 | tf_op jit(solution)/shard_map/ppermute | solution.py:528
  6.7 0.0 collective-permute-start.2
  6.7 0.0 copy-start
  6.7 1.0 %copy-done = bf16[512,256]{1,0:T(8,128)(2,1)S(1)} copy-done((bf16[512,256]{1,0:T(8,128)(2,1)S(1)}, bf16[512,256]{1,0:T(8,128)(2,1)}, u32[]{:S(2)}) %copy-start) | copy-done | bytes 262168
  7.7 0.7 %dynamic-slice_bitcast_fusion = s32[3,16]{1,0:T(4,128)S(1)} fusion(s32[32,3,16]{2,1,0:T(4,128)} %constant.22, s32[]{:T(128)S(6)} %select_n.4), kind=kLoop, calls=%fused_computation.1 | loop fusion | bytes 388 | tf_op jit(solution)/shard_map/jit(dynamic_index_in_dim)/squeeze | solution.py:501
  8.4 0.7 %pad_add_fusion.info = s32[19,16]{1,0:T(8,128)S(1)} fusion(s32[16,16]{1,0:T(8,128)} %param.4, s32[3,16]{1,0:T(4,128)S(1)} %dynamic-slice_bitcast_fusion), kind=kLoop, calls=%fused_computation | loop fusion | flops 304 | bytes 2432 | tf_op jit(solution)/shard_map/concatenate | solution.py:502
  9.1 1.0 %collective-permute-done.refs_4_ = bf16[512,256]{1,0:T(8,128)(2,1)S(1)} collective-permute-done((bf16[512,256]{1,0:T(8,128)(2,1)}, bf16[512,256]{1,0:T(8,128)(2,1)S(1)}, u32[]{:S(2)}, u32[]{:S(2)}) %collective-permute-start) | collective-permute-done | bytes 262176 | tf_op jit(solution)/shard_map/ppermute | solution.py:528
  10.2 2.0 %collective-permute-done.1.refs_1_ = bf16[512,256]{1,0:T(8,128)(2,1)S(1)} collective-permute-done((bf16[512,256]{1,0:T(8,128)(2,1)}, bf16[512,256]{1,0:T(8,128)(2,1)S(1)}, u32[]{:S(2)}, u32[]{:S(2)}) %collective-permute-start.1) | collective-permute-done | bytes 262176 | tf_op jit(solution)/shard_map/ppermute | solution.py:528
  12.2 0.4 %collective-permute-done.3.refs_3_ = bf16[512,256]{1,0:T(8,128)(2,1)S(1)} collective-permute-done((bf16[512,256]{1,0:T(8,128)(2,1)}, bf16[512,256]{1,0:T(8,128)(2,1)S(1)}, u32[]{:S(2)}, u32[]{:S(2)}) %collective-permute-start.3) | collective-permute-done | bytes 262176 | tf_op jit(solution)/shard_map/ppermute | solution.py:528
  12.6 0.7 %collective-permute-done.2.refs_2_ = bf16[512,256]{1,0:T(8,128)(2,1)S(1)} collective-permute-done((bf16[512,256]{1,0:T(8,128)(2,1)}, bf16[512,256]{1,0:T(8,128)(2,1)S(1)}, u32[]{:S(2)}, u32[]{:S(2)}) %collective-permute-start.2) | collective-permute-done | bytes 262176 | tf_op jit(solution)/shard_map/ppermute | solution.py:528
  13.3 0.9 %shard_map.51 = (bf16[512,256]{1,0:T(8,128)(2,1)S(1)}, bf16[512,256]{1,0:T(8,128)(2,1)S(1)}, bf16[512,256]{1,0:T(8,128)(2,1)S(1)}) custom-call(s32[19,16]{1,0:T(8,128)S(1)} %pad_add_fusion.info, bf16[512,256]{1,0:T(8,128)(2,1)S(1)} %shard_map.50.refs_0_, bf16[512,256]{1,0:T(8,128)(2,1)S(1)} %collective-permute-done.1.refs_1_, ...), custom_call_target="tpu_custom_call" | custom-call | tf_op jit(solution)/shard_map/pallas_call | solution.py:511
  14.2 0.1 shard_map.52
  14.3 0.1 collective-permute-start.7
  14.4 0.5 %collective-permute-start.4 = (bf16[512,256]{1,0:T(8,128)(2,1)S(1)}, bf16[512,256]{1,0:T(8,128)(2,1)S(1)}, u32[]{:S(2)}, u32[]{:S(2)}) collective-permute-start(bf16[512,256]{1,0:T(8,128)(2,1)S(1)} %get-tuple-element.33), channel_id=1, source_target_pairs={{1,7},{2,0},{3,12},{4,6},{6,15},{7,13},{13,3},{14,2},{15,22},{22,3... | collective-permute-start | bytes 786440 | tf_op jit(solution)/shard_map/ppermute | solution.py:536
  14.9 0.8 %collective-permute-start.5 = (bf16[512,256]{1,0:T(8,128)(2,1)S(1)}, bf16[512,256]{1,0:T(8,128)(2,1)S(1)}, u32[]{:S(2)}, u32[]{:S(2)}) collective-permute-start(bf16[512,256]{1,0:T(8,128)(2,1)S(1)} %get-tuple-element.34), channel_id=1, source_target_pairs={{5,2},{6,22},{7,4},{9,5},{10,14},{13,15},{14,6},{15,21},{18,12},{2... | collective-permute-start | bytes 786440 | tf_op jit(solution)/shard_map/ppermute | solution.py:536
  15.6 3.9 %collective-permute-start.6 = (bf16[512,256]{1,0:T(8,128)(2,1)S(1)}, bf16[512,256]{1,0:T(8,128)(2,1)S(1)}, u32[]{:S(2)}, u32[]{:S(2)}) collective-permute-start(bf16[512,256]{1,0:T(8,128)(2,1)S(1)} %get-tuple-element.35), channel_id=1, source_target_pairs={{0,7},{4,12},{5,1},{6,0},{7,23},{10,3},{11,14},{13,11},{14,22},{16... | collective-permute-start | bytes 786440 | tf_op jit(solution)/shard_map/ppermute | solution.py:536
  19.5 1.1 %shard_map.53 = f32[8,128]{1,0:T(8,128)S(1)} custom-call(s32[19,16]{1,0:T(8,128)S(1)} %pad_add_fusion.info, bf16[512,256]{1,0:T(8,128)(2,1)S(1)} %shard_map.50.refs_0_, bf16[512,256]{1,0:T(8,128)(2,1)S(1)} %collective-permute-done.1.refs_1_, bf16[512,256]{1,0:T(8,128)(2,1)S(1)} %collective-permute-done.2.refs_2_, ...), custom_call_target="tpu_custom_call" | custom-call | tf_op jit(solution)/shard_map/pallas_call | solution.py:511
  20.6 0.1 collective-permute-start.8
  20.7 1.2 %collective-permute-done.8 = f32[8,128]{1,0:T(8,128)S(1)} collective-permute-done((f32[8,128]{1,0:T(8,128)S(1)}, f32[8,128]{1,0:T(8,128)S(1)}, u32[]{:S(2)}, u32[]{:S(2)}) %collective-permute-start.8) | collective-permute-done | bytes 4128 | tf_op jit(solution)/shard_map/ppermute | solution.py:526
  21.8 0.0 collective-permute-done.7.refs_5_
  21.8 0.2 collective-permute-start.9
  22.0 2.2 %shard_map.54 = (bf16[4,512,512]{2,1,0:T(8,128)(2,1)S(1)}, bf16[4,512,256]{2,1,0:T(8,128)(2,1)S(1)}) custom-call(s32[19,16]{1,0:T(8,128)S(1)} %pad_add_fusion.info, bf16[512,256]{1,0:T(8,128)(2,1)S(1)} %shard_map.50.refs_0_, bf16[512,256]{1,0:T(8,128)(2,1)S(1)} %collective-permute-done.1.refs_1_, bf16[512,256]{1,0:T(8,128)(2,1)S(1)} %collective-permute-done.2.refs_2_, ...), custom_call_target="tpu_custom_call" | custom-call | flops 2147483648 | bytes 8388608 | tf_op jit(solution)/shard_map/pallas_call | solution.py:511
  24.2 0.0 collective-permute-done.4.refs_0_
  24.2 0.0 collective-permute-done.5.refs_1_
  24.3 2.6 %collective-permute-done.6.refs_2_ = bf16[512,256]{1,0:T(8,128)(2,1)S(1)} collective-permute-done((bf16[512,256]{1,0:T(8,128)(2,1)S(1)}, bf16[512,256]{1,0:T(8,128)(2,1)S(1)}, u32[]{:S(2)}, u32[]{:S(2)}) %collective-permute-start.6) | collective-permute-done | bytes 262176 | tf_op jit(solution)/shard_map/ppermute | solution.py:536
  26.9 0.4 %collective-permute-done.9 = f32[8,128]{1,0:T(8,128)S(1)} collective-permute-done((f32[8,128]{1,0:T(8,128)S(1)}, f32[8,128]{1,0:T(8,128)S(1)}, u32[]{:S(2)}, u32[]{:S(2)}) %collective-permute-start.9) | collective-permute-done | bytes 4128 | tf_op jit(solution)/shard_map/ppermute | solution.py:526
  27.3 0.3 collective-permute-start.10
  27.6 0.2 collective-permute-start.11
  27.8 0.3 collective-permute-start.12
  28.1 1.5 %collective-permute-start.13 = (f32[8,128]{1,0:T(8,128)S(1)}, f32[8,128]{1,0:T(8,128)S(1)}, u32[]{:S(2)}, u32[]{:S(2)}) collective-permute-start(f32[8,128]{1,0:T(8,128)S(1)} %add.19), channel_id=1, source_target_pairs={{0,4},{1,5},{2,6},{3,7},{4,0},{5,1},{6,2},{7,3},{8,12},{9,13},{10,... | collective-permute-start | bytes 12296 | tf_op jit(solution)/shard_map/ppermute | solution.py:526
  29.6 0.0 collective-permute-done.10.refs_3_
  29.6 0.0 collective-permute-done.11.refs_4_
  29.6 0.0 collective-permute-done.12.refs_5_
  29.6 3.4 %shard_map.55 = (bf16[4,512,512]{2,1,0:T(8,128)(2,1)S(1)}, bf16[4,512,256]{2,1,0:T(8,128)(2,1)S(1)}, bf16[512,256]{1,0:T(8,128)(2,1)}) custom-call(s32[19,16]{1,0:T(8,128)S(1)} %pad_add_fusion.info, bf16[512,256]{1,0:T(8,128)(2,1)S(1)} %collective-permute-done.4.refs_0_, ...), custom_call_target="tpu_custom_call", output_to_operand_aliasing={{0}: (7, {}), {1}: (8, {})} | custom-call | flops 2147483648 | bytes 8388608 | tf_op jit(solution)/shard_map/pallas_call | solution.py:511
  33.0 0.0 collective-permute-done.13
  33.0 0.5 %multiply_bitcast_fusion = f32[2]{0:T(128)} fusion(f32[8,128]{1,0:T(8,128)S(1)} %add.20), kind=kLoop, calls=%fused_computation.2 | loop fusion | flops 2 | bytes 16 | tf_op jit(solution)/shard_map/div | solution.py:571
  (4 shorter events, 0.0 us)
Async XLA Ops:
  0.6 9.5 %collective-permute-start = (bf16[512,256]{1,0:T(8,128)(2,1)}, bf16[512,256]{1,0:T(8,128)(2,1)S(1)}, u32[]{:S(2)}, u32[]{:S(2)}) collective-permute-start(bf16[512,256]{1,0:T(8,128)(2,1)} %source.1), channel_id=1, source_target_pairs={{0,16},{1,17},{2,18},{3,19},{4,20},{5,21},{6,22},{7,23},{8,24},{9,... | collective-permute-start | bytes 786440 | tf_op jit(solution)/shard_map/ppermute | solution.py:528
  3.7 8.6 %collective-permute-start.1 = (bf16[512,256]{1,0:T(8,128)(2,1)}, bf16[512,256]{1,0:T(8,128)(2,1)S(1)}, u32[]{:S(2)}, u32[]{:S(2)}) collective-permute-start(bf16[512,256]{1,0:T(8,128)(2,1)} %source.1), channel_id=1, source_target_pairs={{0,2},{1,0},{2,4},{3,1},{4,6},{5,3},{6,7},{7,5},{8,10},{9,8},{10,1... | collective-permute-start | bytes 786440 | tf_op jit(solution)/shard_map/ppermute | solution.py:528
  5.2 7.4 %collective-permute-start.3 = (bf16[512,256]{1,0:T(8,128)(2,1)}, bf16[512,256]{1,0:T(8,128)(2,1)S(1)}, u32[]{:S(2)}, u32[]{:S(2)}) collective-permute-start(bf16[512,256]{1,0:T(8,128)(2,1)} %source.1), channel_id=1, source_target_pairs={{0,8},{1,9},{2,10},{3,11},{4,12},{5,13},{6,14},{7,15},{8,0},{9,1},... | collective-permute-start | bytes 786440 | tf_op jit(solution)/shard_map/ppermute | solution.py:528
  6.7 6.6 %collective-permute-start.2 = (bf16[512,256]{1,0:T(8,128)(2,1)}, bf16[512,256]{1,0:T(8,128)(2,1)S(1)}, u32[]{:S(2)}, u32[]{:S(2)}) collective-permute-start(bf16[512,256]{1,0:T(8,128)(2,1)} %source.1), channel_id=1, source_target_pairs={{0,1},{1,3},{2,0},{3,5},{4,2},{5,7},{6,4},{7,6},{8,9},{9,11},{10,8... | collective-permute-start | bytes 786440 | tf_op jit(solution)/shard_map/ppermute | solution.py:528
  6.7 1.0 %copy-start = (bf16[512,256]{1,0:T(8,128)(2,1)S(1)}, bf16[512,256]{1,0:T(8,128)(2,1)}, u32[]{:S(2)}) copy-start(bf16[512,256]{1,0:T(8,128)(2,1)} %source.1) | copy-start | bytes 786436
  14.3 7.5 %collective-permute-start.7 = (bf16[5,512,256]{2,1,0:T(8,128)(2,1)S(1)}, bf16[5,512,256]{2,1,0:T(8,128)(2,1)S(1)}, u32[]{:S(2)}, u32[]{:S(2)}) collective-permute-start(bf16[5,512,256]{2,1,0:T(8,128)(2,1)S(1)} %shard_map.52), channel_id=1, source_target_pairs={{0,1},{1,0},{2,3},{3,2},{4,5},{5,4},{6,7},{7,6},{8,9},{9,8},{10,11... | collective-permute-start | bytes 3932168 | tf_op jit(solution)/shard_map/ppermute | solution.py:523
  14.4 9.9 %collective-permute-start.4 = (bf16[512,256]{1,0:T(8,128)(2,1)S(1)}, bf16[512,256]{1,0:T(8,128)(2,1)S(1)}, u32[]{:S(2)}, u32[]{:S(2)}) collective-permute-start(bf16[512,256]{1,0:T(8,128)(2,1)S(1)} %get-tuple-element.33), channel_id=1, source_target_pairs={{1,7},{2,0},{3,12},{4,6},{6,15},{7,13},{13,3},{14,2},{15,22},{22,3... | collective-permute-start | bytes 786440 | tf_op jit(solution)/shard_map/ppermute | solution.py:536
  14.9 9.4 %collective-permute-start.5 = (bf16[512,256]{1,0:T(8,128)(2,1)S(1)}, bf16[512,256]{1,0:T(8,128)(2,1)S(1)}, u32[]{:S(2)}, u32[]{:S(2)}) collective-permute-start(bf16[512,256]{1,0:T(8,128)(2,1)S(1)} %get-tuple-element.34), channel_id=1, source_target_pairs={{5,2},{6,22},{7,4},{9,5},{10,14},{13,15},{14,6},{15,21},{18,12},{2... | collective-permute-start | bytes 786440 | tf_op jit(solution)/shard_map/ppermute | solution.py:536
  15.6 11.3 %collective-permute-start.6 = (bf16[512,256]{1,0:T(8,128)(2,1)S(1)}, bf16[512,256]{1,0:T(8,128)(2,1)S(1)}, u32[]{:S(2)}, u32[]{:S(2)}) collective-permute-start(bf16[512,256]{1,0:T(8,128)(2,1)S(1)} %get-tuple-element.35), channel_id=1, source_target_pairs={{0,7},{4,12},{5,1},{6,0},{7,23},{10,3},{11,14},{13,11},{14,22},{16... | collective-permute-start | bytes 786440 | tf_op jit(solution)/shard_map/ppermute | solution.py:536
  20.6 1.2 %collective-permute-start.8 = (f32[8,128]{1,0:T(8,128)S(1)}, f32[8,128]{1,0:T(8,128)S(1)}, u32[]{:S(2)}, u32[]{:S(2)}) collective-permute-start(f32[8,128]{1,0:T(8,128)S(1)} %shard_map.53), channel_id=1, source_target_pairs={{0,1},{1,0},{2,3},{3,2},{4,5},{5,4},{6,7},{7,6},{8,9},{9,8},{10,11... | collective-permute-start | bytes 12296 | tf_op jit(solution)/shard_map/ppermute | solution.py:526
  21.8 5.5 %collective-permute-start.9 = (f32[8,128]{1,0:T(8,128)S(1)}, f32[8,128]{1,0:T(8,128)S(1)}, u32[]{:S(2)}, u32[]{:S(2)}) collective-permute-start(f32[8,128]{1,0:T(8,128)S(1)} %add.18), channel_id=1, source_target_pairs={{0,26},{1,27},{2,24},{3,25},{4,30},{5,31},{6,28},{7,29},{8,18},{9,... | collective-permute-start | bytes 12296 | tf_op jit(solution)/shard_map/ppermute | solution.py:526
  27.3 2.3 %collective-permute-start.10 = (bf16[512,256]{1,0:T(8,128)(2,1)S(1)}, bf16[512,256]{1,0:T(8,128)(2,1)S(1)}, u32[]{:S(2)}, u32[]{:S(2)}) collective-permute-start(bf16[512,256]{1,0:T(8,128)(2,1)S(1)} %collective-permute-done.4.refs_0_), channel_id=1, source_target_pairs={{0,1},{1,0},{2,3},{3,2},{4,5},{5,4},{6,7},{7,6},{8,9},{9,8},{10,11... | collective-permute-start | bytes 786440 | tf_op jit(solution)/shard_map/ppermute | solution.py:523
  27.6 2.0 %collective-permute-start.11 = (bf16[512,256]{1,0:T(8,128)(2,1)S(1)}, bf16[512,256]{1,0:T(8,128)(2,1)S(1)}, u32[]{:S(2)}, u32[]{:S(2)}) collective-permute-start(bf16[512,256]{1,0:T(8,128)(2,1)S(1)} %collective-permute-done.5.refs_1_), channel_id=1, source_target_pairs={{0,1},{1,0},{2,3},{3,2},{4,5},{5,4},{6,7},{7,6},{8,9},{9,8},{10,11... | collective-permute-start | bytes 786440 | tf_op jit(solution)/shard_map/ppermute | solution.py:523
  27.8 1.8 %collective-permute-start.12 = (bf16[512,256]{1,0:T(8,128)(2,1)S(1)}, bf16[512,256]{1,0:T(8,128)(2,1)S(1)}, u32[]{:S(2)}, u32[]{:S(2)}) collective-permute-start(bf16[512,256]{1,0:T(8,128)(2,1)S(1)} %collective-permute-done.6.refs_2_), channel_id=1, source_target_pairs={{0,1},{1,0},{2,3},{3,2},{4,5},{5,4},{6,7},{7,6},{8,9},{9,8},{10,11... | collective-permute-start | bytes 786440 | tf_op jit(solution)/shard_map/ppermute | solution.py:523
  28.1 4.9 %collective-permute-start.13 = (f32[8,128]{1,0:T(8,128)S(1)}, f32[8,128]{1,0:T(8,128)S(1)}, u32[]{:S(2)}, u32[]{:S(2)}) collective-permute-start(f32[8,128]{1,0:T(8,128)S(1)} %add.19), channel_id=1, source_target_pairs={{0,4},{1,5},{2,6},{3,7},{4,0},{5,1},{6,2},{7,3},{8,12},{9,13},{10,... | collective-permute-start | bytes 12296 | tf_op jit(solution)/shard_map/ppermute | solution.py:526

commit v2 on v1

v2 whole, which is shorter than its diff:
```python
import functools
import jax
import jax.numpy as jnp
from jax import lax
from jax.experimental import pallas as pl
from jax.experimental.pallas import tpu as pltpu
from jax.sharding import PartitionSpec as P

BLK = 128
VMEM = pl.BlockSpec(memory_space=pltpu.VMEM)
SMEM = pl.BlockSpec(memory_space=pltpu.SMEM)
PARAMS = pltpu.CompilerParams(vmem_limit_bytes=40 * 2**20)


def symmetric_kernel(sub, place, pattern, density, *rest):
    pieces, full = rest[:sub], rest[sub]
    row, col = place[0], place[1]
    height, width = density.shape
    per_piece = width // BLK
    row_blocks = height // BLK
    own_slot = lax.rem(col, sub)
    on_diagonal = row == col // sub
    for t in range(sub):
        slot = lax.rem(own_slot + sub - t, sub)
        for a in range(per_piece):
            i = slot * per_piece + a
            block_row = row * row_blocks + i
            rows = pl.ds(pl.multiple_of(i * BLK, BLK), BLK)
            for b in range(per_piece):
                block_col = col * per_piece + b
                cols = pl.ds(b * BLK, BLK)
                mirror = pieces[t][b * BLK : (b + 1) * BLK, a * BLK : (a + 1) * BLK]
                if t == 0:
                    start = pl.multiple_of((own_slot * per_piece + b) * BLK, BLK)
                    mine = density[pl.ds(start, BLK), a * BLK : (a + 1) * BLK]
                    mirror = jnp.where(on_diagonal, mine, mirror)
                chosen = pattern[jnp.minimum(block_row, block_col), jnp.maximum(block_row, block_col)] != 0
                upper = (block_row == block_col) | ((block_row < block_col) & chosen)
                lower = (block_row > block_col) & chosen
                zero = jnp.zeros((BLK, BLK), full.dtype)
                value = jnp.where(lower, mirror.T, zero)
                full[rows, cols] = jnp.where(upper, density[rows, cols], value)


def product_kernel(lines, planes, place, pattern, *refs):
    left = refs[: 2 * lines]
    right = refs[2 * lines : 2 * lines + planes]
    out, panel = refs[2 * lines + planes :]
    row, col = place[0], place[1]
    height, width = out.shape
    core, line = lax.rem(col, 2), col // 2
    for d in range(planes):
        start = pl.multiple_of((row ^ d) * height, height)
        panel[pl.ds(start, height), :] = right[d][...]
    total = jnp.zeros((height, width), jnp.float32)
    for e in range(lines):
        for s in range(2):
            start = pl.multiple_of(((line ^ e) * 2 + (core ^ s)) * width, width)
            total += jnp.dot(
                left[2 * e + s][...],
                panel[pl.ds(start, width), :],
                preferred_element_type=jnp.float32,
            )
    for i in range(height // BLK):
        for j in range(width // BLK):
            block_row = row * (height // BLK) + i
            block_col = col * (width // BLK) + j
            kept = (block_row == block_col) | ((block_row < block_col) & (pattern[block_row, block_col] != 0))
            block = total[i * BLK : (i + 1) * BLK, j * BLK : (j + 1) * BLK]
            out[i * BLK : (i + 1) * BLK, j * BLK : (j + 1) * BLK] = jnp.where(
                kept, block, jnp.zeros_like(block)
            ).astype(out.dtype)


def block_weights(pattern, row, col, row_blocks, col_blocks):
    block_rows = row * row_blocks + jnp.arange(row_blocks)
    block_cols = col * col_blocks + jnp.arange(col_blocks)
    chosen = lax.dynamic_slice(pattern, (row * row_blocks, col * col_blocks), (row_blocks, col_blocks))
    diagonal = block_rows[:, None] == block_cols[None, :]
    strict = (block_cols[None, :] > block_rows[:, None]) & (chosen != 0)
    return jnp.where(diagonal, 1.0, jnp.where(strict, 2.0, 0.0)).astype(jnp.float32)


def any_mesh(density, pattern):
    n_row = lax.axis_size("row")
    n_col = lax.axis_size("col")
    sub = n_col // n_row
    row = lax.axis_index("row")
    col = lax.axis_index("col")
    height, width = density.shape
    order_size = width * n_col
    place = jnp.stack([row, col]).astype(jnp.int32)

    pieces = []
    for t in range(sub):
        pairs = []
        for q in range(n_row):
            for c in range(n_col):
                p = (c + t) % sub
                if c > q * sub + p:
                    pairs.append((q * n_col + c, (c // sub) * n_col + q * sub + p))
        start = lax.rem(col + t, sub) * width
        piece = lax.dynamic_slice_in_dim(density, start, width, 0)
        pieces.append(lax.ppermute(piece, ("row", "col"), pairs))
    full = pl.pallas_call(
        functools.partial(symmetric_kernel, sub),
        out_shape=jax.ShapeDtypeStruct(density.shape, density.dtype),
        in_specs=[SMEM, SMEM] + [VMEM] * (sub + 1),
        out_specs=VMEM,
        compiler_params=PARAMS,
    )(place, pattern, density, *pieces)

    weights = block_weights(pattern, row, col, height // BLK, width // BLK)
    values = density.astype(jnp.float32).reshape(height // BLK, BLK, width // BLK, BLK)
    squares = jnp.sum(values * values, axis=(1, 3))
    rows_at = row * height + jnp.arange(height)[:, None]
    cols_at = col * width + jnp.arange(width)[None, :]
    diagonal = jnp.where(rows_at == cols_at, density.astype(jnp.float32), 0.0)
    sums = jnp.stack([jnp.sum(diagonal), jnp.sum(jnp.where(weights > 0, weights * squares, 0.0))])
    step = 1
    while step < n_row:
        sums = sums + lax.ppermute(sums, "row", [(i, i ^ step) for i in range(n_row)])
        step *= 2
    step = 1
    while step < n_col:
        sums = sums + lax.ppermute(sums, "col", [(i, i ^ step) for i in range(n_col)])
        step *= 2
    traces = sums / order_size

    right = [full]
    for d in range(1, n_row):
        right.append(lax.ppermute(full, "row", [(i, i ^ d) for i in range(n_row)]))
    left = []
    for e in range(n_col // 2):
        shard = full
        if e > 0:
            shard = lax.ppermute(full, "col", [(i, i ^ (2 * e)) for i in range(n_col)])
        other = lax.ppermute(shard, "col", [(i, i ^ 1) for i in range(n_col)])
        left += [shard, other]
    square = pl.pallas_call(
        functools.partial(product_kernel, n_col // 2, n_row),
        out_shape=jax.ShapeDtypeStruct(density.shape, density.dtype),
        in_specs=[SMEM, SMEM] + [VMEM] * (len(left) + len(right)),
        out_specs=VMEM,
        scratch_shapes=[pltpu.VMEM((order_size, width), density.dtype)],
        compiler_params=PARAMS,
    )(place, pattern, *left, *right)
    return (square, traces)

GRID_PARAMS = pltpu.CompilerParams(vmem_limit_bytes=14 * 2**20)
USES = 8
FIRST = 5
SECOND = 3
SEEN = ((), (0,), (1, 3), (2,))

MESSAGES = (
    (0, (0, 0), 1, (0, 0, 1), (0, 3, 1)),
    (0, (0, 2), 0, (0, 1, 0), (0, 0, 1)),
    (0, (2, 2), 0, (0, 2, 0), (1, 2, 1)),
    (0, (0, 3), 1, (0, 2, 1), (0, 0, 0)),
    (0, (2, 3), 0, (0, 3, 0), (0, 2, 1)),
    (0, (2, 3), 1, (0, 3, 1), (0, 2, 0)),
    (0, (0, 1), 0, (1, 1, 0), (1, 3, 0)),
    (0, (1, 2), 1, (1, 1, 1), (0, 1, 0)),
    (0, (1, 3), 0, (1, 2, 0), (0, 1, 1)),
    (0, (1, 1), 1, (1, 2, 1), (1, 3, 1)),
    (0, (0, 3), 0, (1, 3, 0), (3, 3, 1)),
    (0, (1, 2), 1, (1, 3, 1), (2, 3, 0)),
    (0, (0, 1), 1, (2, 1, 1), (0, 3, 0)),
    (0, (0, 3), 1, (2, 3, 1), (3, 3, 0)),
    (0, (1, 2), 0, (3, 2, 0), (2, 3, 1)),
    (0, (2, 3), 0, (3, 3, 0), (1, 2, 0)),
    (0, (1, 3), 1, (3, 3, 1), (1, 1, 0)),
    (1, (0, 1), 1, (0, 2, 1), (1, 2, 0)),
    (1, (0, 3), 0, (0, 3, 0), (0, 0, 0)),
    (1, (1, 3), 1, (0, 3, 1), (2, 3, 0)),
    (1, (0, 1), 0, (1, 1, 0), (1, 2, 1)),
    (1, (0, 1), 1, (1, 1, 1), (1, 3, 1)),
    (1, (1, 2), 0, (1, 2, 0), (2, 2, 1)),
    (1, (0, 2), 1, (1, 2, 1), (0, 0, 1)),
    (1, (3, 3), 0, (1, 3, 0), (0, 3, 0)),
    (1, (1, 3), 1, (1, 3, 1), (0, 1, 1)),
    (1, (0, 0), 0, (2, 0, 0), (0, 2, 0)),
    (1, (0, 1), 0, (2, 1, 0), (0, 3, 1)),
    (1, (0, 2), 0, (2, 2, 0), (2, 3, 1)),
    (1, (0, 3), 0, (2, 3, 0), (0, 1, 0)),
    (1, (2, 3), 1, (2, 3, 1), (1, 3, 0)),
    (2, (0, 0), 0, (0, 1, 0), (0, 3, 1)),
    (2, (0, 0), 1, (0, 1, 1), (0, 2, 1)),
    (2, (1, 2), 0, (0, 2, 0), (0, 1, 0)),
    (2, (1, 2), 1, (0, 2, 1), (2, 2, 0)),
    (2, (2, 3), 0, (0, 3, 0), (1, 3, 1)),
    (2, (0, 2), 1, (0, 3, 1), (2, 3, 0)),
    (2, (1, 3), 0, (1, 3, 0), (2, 3, 1)),
    (2, (3, 3), 1, (1, 3, 1), (0, 3, 0)),
    (2, (2, 3), 1, (2, 2, 1), (1, 2, 0)),
    (2, (0, 3), 1, (2, 3, 1), (0, 1, 1)),
    (2, (1, 1), 0, (3, 1, 0), (1, 3, 0)),
    (2, (2, 2), 1, (3, 2, 1), (1, 2, 1)),
    (2, (1, 3), 0, (3, 3, 0), (1, 1, 1)),
)


def number(device):
    return 8 * device[0] + 2 * device[1] + device[2]


def wanted(r, z):
    if r > z:
        return [None] * USES
    return [(min(r, j), max(r, j)) for j in range(4)] + [(min(z, j), max(z, j)) for j in range(4)]


def first_round(devices):
    def ring(r, z, k, up):
        step = 1 if (k == 0) == up else -1
        return (r, z + step, k) if 0 <= z + step < 4 else (r, z, 1 - k)

    return [[(d, ring(*d, up)) for d in devices] for up in (True, False)] + [
        [((r, z, k), (r ^ (1 + (k + turn) % 2), z, k)) for r, z, k in devices] for turn in (0, 1)
    ]


def closed(pairs, devices):
    def hops(a, b):
        return abs(a[1] - b[1]) + bin(a[0] ^ b[0]).count("1")

    sends, receives = {a for a, _ in pairs}, {b for _, b in pairs}
    free = sorted((hops(a, b), a, b) for a in devices for b in devices if a not in sends and b not in receives and a != b)
    extra = []
    for _, a, b in free:
        if a not in sends and b not in receives:
            sends.add(a)
            receives.add(b)
            extra.append((a, b))
    return pairs + extra


def schedule():
    devices = [(r, z, k) for r in range(4) for z in range(4) for k in range(2)]
    first = first_round(devices)
    held = {d: [((d[0], d[1]), d[2])] for d in devices}
    for pairs in first:
        for a, b in pairs:
            held[b].append(((a[0], a[1]), a[2]))
    second = [[] for _ in range(SECOND)]
    later = {d: [None] * SECOND for d in devices}
    sends = [{} for _ in range(SECOND)]
    for i, tile, half, a, b in MESSAGES:
        second[i].append((a, b))
        sends[i][number(a)] = held[a].index((tile, half))
        later[b][i] = (tile, half)
    second = [closed(pairs, devices) for pairs in second]
    adds = [set() for _ in range(FIRST)]
    uses = [[{} for _ in range(USES)] for _ in range(2)]
    for d in devices:
        r, z, k = d
        added = {(r, z), (r ^ 1, z), (r ^ 2, z)} | {(r, j) for j in SEEN[z]}
        for s, (tile, half) in enumerate(held[d]):
            if tile in added and half == k and (s == 0 or tile != (r, z)):
                adds[s].add(number(d))
        for u, tile in enumerate(wanted(r, z)):
            for n, shards in enumerate((held, later)):
                here = shards[d] + shards[r, z, 1 - k]
                if tile and (tile, 0) in here and (tile, 1) in here and not any(number(d) in uses[m][u] for m in range(n)):
                    uses[n][u][number(d)] = (here.index((tile, 0)), here.index((tile, 1)))
            assert tile is None or any(number(d) in uses[n][u] for n in range(2))

    def flat(pairs):
        assert len({a for a, _ in pairs}) == len({b for _, b in pairs}) == len(devices)
        return [(number(a), number(b)) for a, b in pairs]

    return [flat(p) for p in first], [flat(p) for p in second], sends, adds, uses


class Place:
    def __init__(self):
        self.row, self.col = lax.axis_index("row"), lax.axis_index("col")
        self.line, self.core = self.col // 2, lax.rem(self.col, 2)
        self.number = self.row * 8 + self.col

    def among(self, devices):
        bits = sum(1 << d for d in devices)
        bits -= (bits >> 31) << 32
        return (lax.shift_right_logical(jnp.int32(bits), self.number) & 1) == 1


def kept(pattern, i, j):
    low, high = jnp.minimum(i, j), jnp.maximum(i, j)
    return (low == high) | (pattern[low, high] != 0)


def partial_kernel(adds, order_size, pattern, *refs):
    me = Place()
    packed, out, squares, diagonals = refs[FIRST:]
    out[...] = jnp.zeros_like(out)
    at_row = lax.broadcasted_iota(jnp.int32, out.shape, 0)
    at_col = lax.broadcasted_iota(jnp.int32, out.shape, 1)
    both = [(refs[s], s, 0) for s in range(FIRST)] + [(packed.at[s], s, 1) for s in range(FIRST)]
    for ref, s, other in both:
        devices = {d ^ other for d in adds[s]}
        core = me.core ^ other
        before, after = me.line - 1 + 2 * core, me.line + 1 - 2 * core
        row = (me.row, me.row, me.row, me.row ^ (1 + core), me.row ^ (2 - core))[s]
        line = (me.line, before, after, me.line, me.line)[s]
        row_blocks, col_blocks = ref.shape[0] // BLK, ref.shape[1] // BLK

        @pl.when(me.among(devices) & (row <= line))
        def _():
            zero = jnp.zeros((BLK, BLK), jnp.float32)
            total = zero
            for a in range(row_blocks):
                for b in range(col_blocks):
                    i, j = row * row_blocks + a, (2 * line + core) * col_blocks + b
                    block = ref[a * BLK : (a + 1) * BLK, b * BLK : (b + 1) * BLK].astype(jnp.float32)
                    block = jnp.where((i <= j) & kept(pattern, i, j), block, zero)
                    total += jnp.where(i == j, 1.0, 2.0) * (block * block)
            squares[...] = total
            diagonals[...] = zero

            @pl.when(row == line)
            def _():
                rows_at = lax.broadcasted_iota(jnp.int32, (BLK, BLK), 0)
                cols_at = lax.broadcasted_iota(jnp.int32, (BLK, BLK), 1)
                for b in range(col_blocks):
                    start = pl.multiple_of((core * col_blocks + b) * BLK, BLK)
                    block = ref[pl.ds(start, BLK), b * BLK : (b + 1) * BLK].astype(jnp.float32)
                    diagonals[...] += jnp.where(rows_at == cols_at, block, zero)

            owner = 8 * row + 2 * line + core
            for i, values in enumerate((diagonals, squares)):
                out[...] += jnp.where((at_row == i) & (at_col == owner), jnp.sum(values[...]) / order_size, 0.0)


def copy_kernel(source, out):
    out[...] = source[...]


def pack_kernel(*refs):
    out = refs[-1]
    for i, ref in enumerate(refs[:-1]):
        out[i] = ref[...]


def copy_kernel(source, out):
    out[...] = source[...]


def pack_kernel(*refs):
    out = refs[-1]
    for i, ref in enumerate(refs[:-1]):
        out[i] = ref[...]


def choose_kernel(sends, *refs):
    me = Place()
    held, outs = refs[:FIRST], refs[FIRST:]
    for out, send in zip(outs, sends):
        for s, ref in enumerate(held):
            devices = [d for d in send if send[d] == s]
            if devices:
                @pl.when(me.among(devices))
                def _():
                    out[...] = ref[...]


def pack_kernel(*refs):
    out = refs[-1]
    for i, ref in enumerate(refs[:-1]):
        out[i] = ref[...]


def place_tiles(uses, me, shards, keep, left, right, raw):
    tile, width = left.shape[0], right.shape[1]
    blocks, half_blocks = tile // BLK, width // BLK
    zero = jnp.zeros((BLK, BLK), left.dtype)

    def stored(a, b):
        return raw[(b // 2) * tile + a * BLK : (b // 2) * tile + (a + 1) * BLK, (b % 2) * BLK : (b % 2 + 1) * BLK]

    def direct(a, b):
        start = pl.multiple_of(me.core * tile + a * BLK, BLK)
        return raw[pl.ds(start, BLK), b * BLK : (b + 1) * BLK]

    def mirrored(a, b):
        start = pl.multiple_of((a // 2) * tile + (me.core * half_blocks + b) * BLK, BLK)
        return raw[pl.ds(start, BLK), (a % 2) * BLK : (a % 2 + 1) * BLK].T

    left_ways = (
        stored,
        lambda a, b: stored(b, a).T,
        lambda a, b: stored(a, b) if a <= b else stored(b, a).T,
    )
    right_ways = (
        direct,
        mirrored,
        lambda a, b: jnp.where(a <= me.core * half_blocks + b, direct(a, b), mirrored(a, b)),
    )

    def fill(panel, at, cols, u, block_of):
        j = u % 4
        for a in range(blocks):
            for b in range(cols):
                rows = slice(at[0] + a * BLK, at[0] + (a + 1) * BLK)
                lanes = slice(at[1] + b * BLK, at[1] + (b + 1) * BLK)
                if u < 4:
                    flag = keep(panel, rows, lanes, me.row * blocks + a, j * blocks + b)
                else:
                    flag = keep(panel, rows, lanes, j * blocks + a, me.col * half_blocks + b)
                panel[rows, lanes] = jnp.where(flag, block_of(a, b), zero)

    for u, here in enumerate(uses):
        j = u % 4
        panel, at, cols, ways = (left, (0, j * tile), blocks, left_ways) if u < 4 else (
            right, (j * tile, 0), half_blocks, right_ways)

        def index(d):
            return d // 8 if u < 4 else (d % 8) // 2

        def above(d):
            return 2 if index(d) == j else int((index(d) > j) == (u < 4))

        if here:
            @pl.when(me.among(here))
            def _():
                for half in range(2):
                    for s in sorted({here[d][half] for d in here}):
                        @pl.when(me.among([d for d in here if here[d][half] == s]))
                        def _():
                            raw[half * tile : (half + 1) * tile, :] = shards[s][...]

                for way in sorted({above(d) for d in here}):
                    @pl.when(me.among([d for d in here if above(d) == way]))
                    def _():
                        fill(panel, at, cols, u, ways[way])


def place_last_tiles(uses, me, shards, left, right, raw):
    tile, width = left.shape[0], right.shape[1]
    blocks, half_blocks = tile // BLK, width // BLK
    part = 16

    def put(panel, row_at, col_at, block):
        lanes = slice(col_at, col_at + BLK)
        flag = panel[row_at : row_at + part, lanes] != 0
        for q in range(0, BLK, part):
            value = block[q : q + part, :]
            panel[row_at + q : row_at + q + part, lanes] = jnp.where(flag, value, jnp.zeros_like(value))

    def square(ref, a, b):
        return ref[a * BLK : (a + 1) * BLK, b * BLK : (b + 1) * BLK]

    diagonal = [{} for _ in range(USES)]
    for u, here in enumerate(uses):
        j = u % 4
        of_left = u < 4

        def index(d):
            return d // 8 if of_left else (d % 8) // 2

        diagonal[u] = {d: here[d] for d in here if index(d) == j}
        for half in range(2):
            for s in sorted({here[d][half] for d in here}):
                ref = shards[s]
                found = [d for d in here if here[d][half] == s]
                stands = [d for d in found if (index(d) < j if of_left else index(d) > j)]
                lies = [d for d in found if (index(d) > j if of_left else index(d) < j)]
                if of_left and stands:
                    @pl.when(me.among(stands))
                    def _():
                        for a in range(blocks):
                            for b in range(half_blocks):
                                put(left, a * BLK, j * tile + (half * half_blocks + b) * BLK, square(ref, a, b))
                if of_left and lies:
                    @pl.when(me.among(lies))
                    def _():
                        for a in range(half_blocks):
                            for b in range(blocks):
                                put(left, (half * half_blocks + a) * BLK, j * tile + b * BLK, square(ref, b, a).T)
                mine = [d for d in stands if d % 2 == half]
                if not of_left and mine:
                    @pl.when(me.among(mine))
                    def _():
                        for a in range(blocks):
                            for b in range(half_blocks):
                                put(right, j * tile + a * BLK, b * BLK, square(ref, a, b))
                if not of_left and lies:
                    @pl.when(me.among(lies))
                    def _():
                        for a in range(half_blocks):
                            for b in range(half_blocks):
                                start = pl.multiple_of((me.core * half_blocks + b) * BLK, BLK)
                                block = ref[pl.ds(start, BLK), a * BLK : (a + 1) * BLK]
                                put(right, j * tile + (half * half_blocks + a) * BLK, b * BLK, block.T)

    def keep(panel, rows, lanes, i, j):
        return panel[rows, lanes] != 0

    place_tiles(diagonal, me, shards, keep, left, right, raw)


def panels_kernel(uses, pattern, *refs):
    packed, left, right, keeps, raw = refs[FIRST:]
    me = Place()
    shards = list(refs[:FIRST]) + [packed.at[i] for i in range(FIRST)]

    def keep(panel, rows, lanes, i, j):
        return kept(pattern, i, j)

    place_tiles(uses[0], me, shards, keep, left, right, raw)
    tile, width = left.shape[0], right.shape[1]
    blocks, half_blocks = tile // BLK, width // BLK

    def flags(ref, row_at, col_at, cols, flag):
        for a in range(blocks):
            for b in range(cols):
                value = jnp.where(flag(a, b), 1.0, 0.0).astype(ref.dtype)
                ref[row_at + a * BLK : row_at + (a + 1) * BLK, col_at + b * BLK : col_at + (b + 1) * BLK] = (
                    jnp.full((BLK, BLK), value, ref.dtype)
                )

    for u, later in enumerate(uses[1]):
        j = u % 4
        if later:
            @pl.when(me.among(later))
            def _():
                if u < 4:
                    flags(left, 0, j * tile, blocks, lambda a, b: kept(pattern, me.row * blocks + a, j * blocks + b))
                else:
                    flags(
                        right, j * tile, 0, half_blocks,
                        lambda a, b: kept(pattern, j * blocks + a, me.col * half_blocks + b),
                    )

    def square_kept(a, b):
        i, j = me.row * blocks + a, me.col * half_blocks + b
        return (i <= j) & kept(pattern, i, j)

    flags(keeps, 0, 0, half_blocks, square_kept)


def grid_product_kernel(uses, *refs):
    shards = refs[: 2 * SECOND]
    keeps, _, _, left, right, out, raw, result, sems = refs[2 * SECOND :]
    me = Place()
    place_last_tiles(uses[1], me, shards, left, right, raw)
    height = out.shape[0]
    part = height // 2
    copies = []
    for c in range(2):
        rows = pl.ds(c * part, part)

        @pl.when(me.row <= me.line)
        def _():
            product = jnp.dot(left[rows, :], right[...], preferred_element_type=jnp.float32)
            result[rows, :] = jnp.where(
                keeps[rows, :].astype(jnp.float32) != 0, product, jnp.zeros_like(product)
            ).astype(result.dtype)

        @pl.when(me.row > me.line)
        def _():
            result[rows, :] = jnp.zeros((part, result.shape[1]), result.dtype)

        copies.append(pltpu.make_async_copy(result.at[rows], out.at[rows], sems.at[c]))
        copies[-1].start()
    for copy in copies:
        copy.wait()


def chip_grid(density, pattern):
    height, width = density.shape
    n_col = lax.axis_size("col")
    n_devices = lax.axis_size("row") * n_col
    order_size = width * lax.axis_size("col")
    dtype = density.dtype
    axes = ("row", "col")
    first, second, sends, adds, uses = schedule()
    shard = jax.ShapeDtypeStruct(density.shape, dtype)
    raw = pltpu.VMEM((2 * height, width), dtype)
    panels = [
        jax.ShapeDtypeStruct((height, order_size), dtype),
        jax.ShapeDtypeStruct((order_size, width), dtype),
    ]

    def call(kernel, out_shape, smem, args, scratch=(), out_specs=VMEM, aliases=None, cost=None):
        return pl.pallas_call(
            kernel,
            out_shape=out_shape,
            in_specs=[SMEM] * smem + [VMEM] * (len(args) - smem),
            out_specs=out_specs,
            scratch_shapes=list(scratch),
            input_output_aliases=aliases or {},
            compiler_params=GRID_PARAMS,
            cost_estimate=cost,
        )(*args)

    def share(value):
        return lax.ppermute(value, axes, [(d, d ^ 1) for d in range(n_devices)])

    def part_from(parts, row_bits, col_bits):
        return lax.ppermute(parts, axes, [(d, d ^ (row_bits * n_col + col_bits)) for d in range(n_devices)])

    came = [lax.ppermute(density, axes, pairs) for pairs in first]
    came[0], own = lax.optimization_barrier((came[0], call(copy_kernel, shard, 0, [density])))
    held = [own] + came
    chosen = call(functools.partial(choose_kernel, sends), [shard] * SECOND, 0, held, (), [VMEM] * SECOND)
    tied = lax.optimization_barrier((*chosen, *held))
    chosen, held = tied[:SECOND], list(tied[SECOND:])
    later = [lax.ppermute(value, axes, pairs) for value, pairs in zip(chosen, second)]
    packed = share(call(pack_kernel, jax.ShapeDtypeStruct((FIRST, height, width), dtype), 0, held))
    parts = call(
        functools.partial(partial_kernel, adds, order_size),
        jax.ShapeDtypeStruct((8, 128), jnp.float32),
        1,
        [pattern] + held + [packed],
        [pltpu.VMEM((BLK, BLK), jnp.float32)] * 2,
    )
    packed, parts = lax.optimization_barrier((packed, parts))
    received = part_from(parts, 3, 2)
    left, right, keeps = call(
        functools.partial(panels_kernel, uses), panels + [shard], 1, [pattern] + held + [packed], [raw], [VMEM] * 3
    )
    left, parts = lax.optimization_barrier((left, parts + received))
    received = part_from(parts, 0, 4)
    left, parts = lax.optimization_barrier((left, parts))
    shared = []
    for i in range(SECOND):
        later[i], left = lax.optimization_barrier((later[i], left))
        shared.append(share(later[i]))
    inputs = later + shared + [keeps, left, right]
    square = call(
        functools.partial(grid_product_kernel, uses),
        panels + [shard],
        0,
        inputs,
        [raw, pltpu.VMEM(density.shape, dtype), pltpu.SemaphoreType.DMA((2,))],
        [VMEM, VMEM, pl.BlockSpec(memory_space=pltpu.HBM)],
        {len(inputs) - 2: 0, len(inputs) - 1: 1},
    )[2]
    square, received = lax.optimization_barrier((square, received))
    traces = jnp.sum(parts[:2] + received[:2], axis=1)
    return (square, traces)


def per_device(density, pattern):
    if lax.axis_size("row") == 4 and lax.axis_size("col") == 8 and density.shape[0] == 2 * density.shape[1]:
        return chip_grid(density, pattern)
    return any_mesh(density, pattern)


def solution(mesh):
    placed = (P("row", "col"), P())
    return jax.shard_map(
        per_device, mesh=mesh, in_specs=placed, out_specs=(P("row", "col"), P()), check_vma=False
    )
```

time: 34.1 us -> 33.4 us (0.979); the launches traced: 33.5 us -> 33.2 us
  starting transfers between devices: 13.9 us -> 16.3 us
  Pallas kernels: 7.64 us -> 6.36 us
  local copies, waits for them, and re-layouts: 1.67 us -> 0.99 us
  other arithmetic: 1.23 us -> 0.63 us
    ppermute x3 -> x2, starting transfers between devices: 1.78 us -> 5.08 us  [part_from(): lax.ppermute(parts, axes, [(d, d ^ row_bits * n_col + col_bits) for d in...]
    ppermute x3 -> x2, waiting for transfers between devices: 1.58 us -> 0.23 us  [part_from(): lax.ppermute(parts, axes, [(d, d ^ row_bits * n_col + col_bits) for d in...]
    pallas_call x6, Pallas kernels: 7.64 us -> 6.36 us  [call(): pl.pallas_call(kernel, out_shape=out_shape, in_specs=[SMEM] * smem + [VME...]
    ppermute x4, waiting for transfers between devices: 4.18 us -> 5.36 us  [chip_grid(): came = [lax.ppermute(density, axes, pairs) for pairs in first]]
    ppermute x3, starting transfers between devices: 5.15 us -> 4.11 us  [chip_grid(): lax.ppermute(value, axes, pairs)]
    concatenate x1 -> x0, other arithmetic: 0.7 us -> none  [chip_grid(): plan = jnp.concatenate([plan, pattern], axis=0)]
    squeeze x1 -> x0, local copies, waits for them, and re-layouts: 0.69 us -> none  [chip_grid(): lax.dynamic_index_in_dim(table.reshape(n_devices, plan_rows, lanes), me,...]
    reduce_sum x0 -> x1, other arithmetic: none -> 0.63 us  [chip_grid(): traces = jnp.sum(parts[:2] + received[:2], axis=1)]
  transfers between devices with their start and end apart: 14 -> 13, of which waited for: 7 -> 5; matrix products, arithmetic and copies ran while one was open for 4% -> 0% of each run, Pallas kernels for 20% -> 19%
where the time goes in v2:
time: 33.4 us; the launch traced here: 33.2 us
  starting transfers between devices  16.3 us (49%)
  waiting for transfers between devices  8.23 us (25%)
  Pallas kernels  6.36 us (19%)
  local copies, waits for them, and re-layouts  0.99 us (3%)
  between operations  0.7 us (2%)
  other arithmetic  0.63 us (2%)
    pallas_call x6, Pallas kernels, call(): pl.pallas_call(kernel, out_shape=out_shape, in_specs=[SMEM] * smem + [VME...  6.36 us
    ppermute x4, starting transfers between devices, chip_grid(): came = [lax.ppermute(density, axes, pairs) for pairs in first]  6.05 us
    ppermute x4, waiting for transfers between devices, chip_grid(): came = [lax.ppermute(density, axes, pairs) for pairs in first]  5.36 us
    ppermute x2, starting transfers between devices, part_from(): lax.ppermute(parts, axes, [(d, d ^ row_bits * n_col + col_bits) for d in...  5.08 us
    ppermute x3, starting transfers between devices, chip_grid(): lax.ppermute(value, axes, pairs)  4.11 us
    ppermute x3, waiting for transfers between devices, chip_grid(): lax.ppermute(value, axes, pairs)  2.64 us
    ppermute x4, starting transfers between devices, share(): return lax.ppermute(value, axes, [(d, d ^ 1) for d in range(n_devices)])  1.08 us
    unnamed x4, local copies, waits for them, and re-layouts  0.99 us
  transfers between devices with their start and end apart: 13, of which 5 were waited for; matrix products, arithmetic and copies ran while one was open for 0% of the time, Pallas kernels for 19%

profile of v2, /device:TPU:0, one launch (start us, length us, event | category | flops | bytes accessed | tf_op | source)
XLA Modules:
  0.0 33.2 jit_solution(7393422060155179700)
XLA Ops:
  0.6 3.0 %collective-permute-start = (bf16[512,256]{1,0:T(8,128)(2,1)}, bf16[512,256]{1,0:T(8,128)(2,1)S(1)}, u32[]{:S(2)}, u32[]{:S(2)}) collective-permute-start(bf16[512,256]{1,0:T(8,128)(2,1)} %source.1), channel_id=1, source_target_pairs={{0,2},{1,0},{2,4},{3,1},{4,6},{5,3},{6,7},{7,5},{8,10},{9,8},{10,1... | collective-permute-start | bytes 786440 | tf_op jit(solution)/shard_map/ppermute | solution.py:603
  3.7 0.0 collective-permute-start.1
  3.7 1.5 %collective-permute-start.2 = (bf16[512,256]{1,0:T(8,128)(2,1)}, bf16[512,256]{1,0:T(8,128)(2,1)S(1)}, u32[]{:S(2)}, u32[]{:S(2)}) collective-permute-start(bf16[512,256]{1,0:T(8,128)(2,1)} %source.1), channel_id=1, source_target_pairs={{0,8},{1,17},{2,10},{3,19},{4,12},{5,21},{6,14},{7,23},{8,0},{9,25... | collective-permute-start | bytes 786440 | tf_op jit(solution)/shard_map/ppermute | solution.py:603
  5.2 1.5 %collective-permute-start.3 = (bf16[512,256]{1,0:T(8,128)(2,1)}, bf16[512,256]{1,0:T(8,128)(2,1)S(1)}, u32[]{:S(2)}, u32[]{:S(2)}) collective-permute-start(bf16[512,256]{1,0:T(8,128)(2,1)} %source.1), channel_id=1, source_target_pairs={{0,16},{1,9},{2,18},{3,11},{4,20},{5,13},{6,22},{7,15},{8,24},{9,1... | collective-permute-start | bytes 786440 | tf_op jit(solution)/shard_map/ppermute | solution.py:603
  6.7 0.0 copy-start
  6.7 1.0 %copy-done = bf16[512,256]{1,0:T(8,128)(2,1)S(1)} copy-done((bf16[512,256]{1,0:T(8,128)(2,1)S(1)}, bf16[512,256]{1,0:T(8,128)(2,1)}, u32[]{:S(2)}) %copy-start) | copy-done | bytes 262168
  7.7 0.0 copy-start.1
  7.7 1.9 %collective-permute-done.refs_1_ = bf16[512,256]{1,0:T(8,128)(2,1)S(1)} collective-permute-done((bf16[512,256]{1,0:T(8,128)(2,1)}, bf16[512,256]{1,0:T(8,128)(2,1)S(1)}, u32[]{:S(2)}, u32[]{:S(2)}) %collective-permute-start) | collective-permute-done | bytes 262176 | tf_op jit(solution)/shard_map/ppermute | solution.py:603
  9.6 0.7 %collective-permute-done.1.refs_2_ = bf16[512,256]{1,0:T(8,128)(2,1)S(1)} collective-permute-done((bf16[512,256]{1,0:T(8,128)(2,1)}, bf16[512,256]{1,0:T(8,128)(2,1)S(1)}, u32[]{:S(2)}, u32[]{:S(2)}) %collective-permute-start.1) | collective-permute-done | bytes 262176 | tf_op jit(solution)/shard_map/ppermute | solution.py:603
  10.3 2.8 %collective-permute-done.2.refs_3_ = bf16[512,256]{1,0:T(8,128)(2,1)S(1)} collective-permute-done((bf16[512,256]{1,0:T(8,128)(2,1)}, bf16[512,256]{1,0:T(8,128)(2,1)S(1)}, u32[]{:S(2)}, u32[]{:S(2)}) %collective-permute-start.2) | collective-permute-done | bytes 262176 | tf_op jit(solution)/shard_map/ppermute | solution.py:603
  13.1 0.0 collective-permute-done.3.refs_4_
  13.1 0.1 shard_map.43
  13.2 0.3 collective-permute-start.5
  13.4 1.6 %collective-permute-start.4 = (bf16[512,256]{1,0:T(8,128)(2,1)S(1)}, bf16[512,256]{1,0:T(8,128)(2,1)S(1)}, u32[]{:S(2)}, u32[]{:S(2)}) collective-permute-start(bf16[512,256]{1,0:T(8,128)(2,1)S(1)} %get-tuple-element.37), channel_id=1, source_target_pairs={{1,7},{2,1},{4,13},{5,0},{6,5},{7,4},{10,14},{11,2},{12,3},{13,15}... | collective-permute-start | bytes 786440 | tf_op jit(solution)/shard_map/ppermute | solution.py:609
  15.0 0.0 collective-permute-start.7
  15.0 2.5 %collective-permute-start.8 = (bf16[512,256]{1,0:T(8,128)(2,1)S(1)}, bf16[512,256]{1,0:T(8,128)(2,1)S(1)}, u32[]{:S(2)}, u32[]{:S(2)}) collective-permute-start(bf16[512,256]{1,0:T(8,128)(2,1)S(1)} %get-tuple-element.51), channel_id=1, source_target_pairs={{2,7},{3,5},{4,2},{5,20},{6,15},{7,22},{14,23},{15,6},{21,12},{23,... | collective-permute-start | bytes 786440 | tf_op jit(solution)/shard_map/ppermute | solution.py:609
  17.5 0.0 collective-permute-done.5.refs_5_
  17.5 0.0 copy-done.1
  17.5 1.3 %shard_map.44 = f32[8,128]{1,0:T(8,128)S(1)} custom-call(s32[16,16]{1,0:T(8,128)S(1)} %copy-done.1, bf16[512,256]{1,0:T(8,128)(2,1)S(1)} %shard_map.41.refs_0_, bf16[512,256]{1,0:T(8,128)(2,1)S(1)} %collective-permute-done.refs_1_, bf16[512,256]{1,0:T(8,128)(2,1)S(1)} %collective-permute-done.1.refs_2_, bf16[512,256]{1,0:T(8,128)(2,1)S(1)} %collective-permute-done.2.refs_3_, ...), custom_call_target="tpu_custom_call" | custom-call | tf_op jit(solution)/shard_map/pallas_call | solution.py:586
  18.8 2.9 %collective-permute-start.6 = (f32[8,128]{1,0:T(8,128)S(1)}, f32[8,128]{1,0:T(8,128)S(1)}, u32[]{:S(2)}, u32[]{:S(2)}) collective-permute-start(f32[8,128]{1,0:T(8,128)S(1)} %shard_map.44), channel_id=1, source_target_pairs={{0,26},{1,27},{2,24},{3,25},{4,30},{5,31},{6,28},{7,29},{8,18},{9,... | collective-permute-start | bytes 12296 | tf_op jit(solution)/shard_map/ppermute | solution.py:601
  21.7 2.3 %shard_map.45 = (bf16[512,2048]{1,0:T(8,128)(2,1)S(1)}, bf16[2048,256]{1,0:T(8,128)(2,1)S(1)}, bf16[512,256]{1,0:T(8,128)(2,1)S(1)}) custom-call(s32[16,16]{1,0:T(8,128)S(1)} %copy-done.1, bf16[512,256]{1,0:T(8,128)(2,1)S(1)} %shard_map.41.refs_0_, bf16[512,256]{1,0:T(8,128)(2,1)S(1)} %collective-permute-done.refs_1_, ...), custom_call_target="tpu_custom_call" | custom-call | tf_op jit(solution)/shard_map/pallas_call | solution.py:586
  24.0 0.2 collective-permute-done.6
  24.3 0.0 collective-permute-done.4.refs_0_
  24.3 2.6 %collective-permute-done.7.refs_1_ = bf16[512,256]{1,0:T(8,128)(2,1)S(1)} collective-permute-done((bf16[512,256]{1,0:T(8,128)(2,1)S(1)}, bf16[512,256]{1,0:T(8,128)(2,1)S(1)}, u32[]{:S(2)}, u32[]{:S(2)}) %collective-permute-start.7) | collective-permute-done | bytes 262176 | tf_op jit(solution)/shard_map/ppermute | solution.py:609
  26.9 0.0 collective-permute-done.8.refs_2_
  26.9 0.3 collective-permute-start.11
  27.2 0.2 collective-permute-start.10
  27.4 0.3 collective-permute-start.9
  27.7 2.1 %collective-permute-start.12 = (f32[8,128]{1,0:T(8,128)S(1)}, f32[8,128]{1,0:T(8,128)S(1)}, u32[]{:S(2)}, u32[]{:S(2)}) collective-permute-start(f32[8,128]{1,0:T(8,128)S(1)} %add.6), channel_id=1, source_target_pairs={{0,4},{1,5},{2,6},{3,7},{4,0},{5,1},{6,2},{7,3},{8,12},{9,13},{10,... | collective-permute-start | bytes 12296 | tf_op jit(solution)/shard_map/ppermute | solution.py:601
  29.9 0.0 collective-permute-done.11.refs_5_
  29.9 0.0 collective-permute-done.10.refs_4_
  29.9 0.0 collective-permute-done.9.refs_3_
  29.9 2.7 %shard_map.46 = (bf16[512,2048]{1,0:T(8,128)(2,1)S(1)}, bf16[2048,256]{1,0:T(8,128)(2,1)S(1)}, bf16[512,256]{1,0:T(8,128)(2,1)}) custom-call(bf16[512,256]{1,0:T(8,128)(2,1)S(1)} %collective-permute-done.4.refs_0_, bf16[512,256]{1,0:T(8,128)(2,1)S(1)} %collective-permute-done.7.refs_1_, ...), custom_call_target="tpu_custom_call", output_to_operand_aliasing={{0}: (7, {}), {1}: (8, {})} | custom-call | tf_op jit(solution)/shard_map/pallas_call | solution.py:586
  32.6 0.0 collective-permute-done.12
  32.6 0.6 %add_reduce_fusion = f32[2]{0:T(128)} fusion(f32[8,128]{1,0:T(8,128)S(1)} %collective-permute-done.12, f32[8,128]{1,0:T(8,128)S(1)} %add.6), kind=kLoop, calls=%fused_computation | loop fusion | flops 510 | bytes 2056 | tf_op jit(solution)/shard_map/reduce_sum | solution.py:641
  (3 shorter events, 0.0 us)
Async XLA Ops:
  0.6 8.9 %collective-permute-start = (bf16[512,256]{1,0:T(8,128)(2,1)}, bf16[512,256]{1,0:T(8,128)(2,1)S(1)}, u32[]{:S(2)}, u32[]{:S(2)}) collective-permute-start(bf16[512,256]{1,0:T(8,128)(2,1)} %source.1), channel_id=1, source_target_pairs={{0,2},{1,0},{2,4},{3,1},{4,6},{5,3},{6,7},{7,5},{8,10},{9,8},{10,1... | collective-permute-start | bytes 786440 | tf_op jit(solution)/shard_map/ppermute | solution.py:603
  3.7 6.6 %collective-permute-start.1 = (bf16[512,256]{1,0:T(8,128)(2,1)}, bf16[512,256]{1,0:T(8,128)(2,1)S(1)}, u32[]{:S(2)}, u32[]{:S(2)}) collective-permute-start(bf16[512,256]{1,0:T(8,128)(2,1)} %source.1), channel_id=1, source_target_pairs={{0,1},{1,3},{2,0},{3,5},{4,2},{5,7},{6,4},{7,6},{8,9},{9,11},{10,8... | collective-permute-start | bytes 786440 | tf_op jit(solution)/shard_map/ppermute | solution.py:603
  3.7 9.4 %collective-permute-start.2 = (bf16[512,256]{1,0:T(8,128)(2,1)}, bf16[512,256]{1,0:T(8,128)(2,1)S(1)}, u32[]{:S(2)}, u32[]{:S(2)}) collective-permute-start(bf16[512,256]{1,0:T(8,128)(2,1)} %source.1), channel_id=1, source_target_pairs={{0,8},{1,17},{2,10},{3,19},{4,12},{5,21},{6,14},{7,23},{8,0},{9,25... | collective-permute-start | bytes 786440 | tf_op jit(solution)/shard_map/ppermute | solution.py:603
  5.2 7.9 %collective-permute-start.3 = (bf16[512,256]{1,0:T(8,128)(2,1)}, bf16[512,256]{1,0:T(8,128)(2,1)S(1)}, u32[]{:S(2)}, u32[]{:S(2)}) collective-permute-start(bf16[512,256]{1,0:T(8,128)(2,1)} %source.1), channel_id=1, source_target_pairs={{0,16},{1,9},{2,18},{3,11},{4,20},{5,13},{6,22},{7,15},{8,24},{9,1... | collective-permute-start | bytes 786440 | tf_op jit(solution)/shard_map/ppermute | solution.py:603
  6.7 1.0 %copy-start = (bf16[512,256]{1,0:T(8,128)(2,1)S(1)}, bf16[512,256]{1,0:T(8,128)(2,1)}, u32[]{:S(2)}) copy-start(bf16[512,256]{1,0:T(8,128)(2,1)} %source.1) | copy-start | bytes 786436
  7.7 9.9 %copy-start.1 = (s32[16,16]{1,0:T(8,128)S(1)}, s32[16,16]{1,0:T(8,128)}, u32[]{:S(2)}) copy-start(s32[16,16]{1,0:T(8,128)} %pattern.3) | copy-start | bytes 3076
  13.2 4.4 %collective-permute-start.5 = (bf16[5,512,256]{2,1,0:T(8,128)(2,1)S(1)}, bf16[5,512,256]{2,1,0:T(8,128)(2,1)S(1)}, u32[]{:S(2)}, u32[]{:S(2)}) collective-permute-start(bf16[5,512,256]{2,1,0:T(8,128)(2,1)S(1)} %shard_map.43), channel_id=1, source_target_pairs={{0,1},{1,0},{2,3},{3,2},{4,5},{5,4},{6,7},{7,6},{8,9},{9,8},{10,11... | collective-permute-start | bytes 3932168 | tf_op jit(solution)/shard_map/ppermute | solution.py:598
  13.4 10.9 %collective-permute-start.4 = (bf16[512,256]{1,0:T(8,128)(2,1)S(1)}, bf16[512,256]{1,0:T(8,128)(2,1)S(1)}, u32[]{:S(2)}, u32[]{:S(2)}) collective-permute-start(bf16[512,256]{1,0:T(8,128)(2,1)S(1)} %get-tuple-element.37), channel_id=1, source_target_pairs={{1,7},{2,1},{4,13},{5,0},{6,5},{7,4},{10,14},{11,2},{12,3},{13,15}... | collective-permute-start | bytes 786440 | tf_op jit(solution)/shard_map/ppermute | solution.py:609
  15.0 11.9 %collective-permute-start.7 = (bf16[512,256]{1,0:T(8,128)(2,1)S(1)}, bf16[512,256]{1,0:T(8,128)(2,1)S(1)}, u32[]{:S(2)}, u32[]{:S(2)}) collective-permute-start(bf16[512,256]{1,0:T(8,128)(2,1)S(1)} %get-tuple-element.48), channel_id=1, source_target_pairs={{5,12},{6,0},{7,22},{10,13},{11,15},{12,21},{13,1},{14,6},{15,3},{... | collective-permute-start | bytes 786440 | tf_op jit(solution)/shard_map/ppermute | solution.py:609
  15.0 11.9 %collective-permute-start.8 = (bf16[512,256]{1,0:T(8,128)(2,1)S(1)}, bf16[512,256]{1,0:T(8,128)(2,1)S(1)}, u32[]{:S(2)}, u32[]{:S(2)}) collective-permute-start(bf16[512,256]{1,0:T(8,128)(2,1)S(1)} %get-tuple-element.51), channel_id=1, source_target_pairs={{2,7},{3,5},{4,2},{5,20},{6,15},{7,22},{14,23},{15,6},{21,12},{23,... | collective-permute-start | bytes 786440 | tf_op jit(solution)/shard_map/ppermute | solution.py:609
  18.8 5.5 %collective-permute-start.6 = (f32[8,128]{1,0:T(8,128)S(1)}, f32[8,128]{1,0:T(8,128)S(1)}, u32[]{:S(2)}, u32[]{:S(2)}) collective-permute-start(f32[8,128]{1,0:T(8,128)S(1)} %shard_map.44), channel_id=1, source_target_pairs={{0,26},{1,27},{2,24},{3,25},{4,30},{5,31},{6,28},{7,29},{8,18},{9,... | collective-permute-start | bytes 12296 | tf_op jit(solution)/shard_map/ppermute | solution.py:601
  26.9 3.0 %collective-permute-start.11 = (bf16[512,256]{1,0:T(8,128)(2,1)S(1)}, bf16[512,256]{1,0:T(8,128)(2,1)S(1)}, u32[]{:S(2)}, u32[]{:S(2)}) collective-permute-start(bf16[512,256]{1,0:T(8,128)(2,1)S(1)} %collective-permute-done.8.refs_2_), channel_id=1, source_target_pairs={{0,1},{1,0},{2,3},{3,2},{4,5},{5,4},{6,7},{7,6},{8,9},{9,8},{10,11... | collective-permute-start | bytes 786440 | tf_op jit(solution)/shard_map/ppermute | solution.py:598
  27.2 2.7 %collective-permute-start.10 = (bf16[512,256]{1,0:T(8,128)(2,1)S(1)}, bf16[512,256]{1,0:T(8,128)(2,1)S(1)}, u32[]{:S(2)}, u32[]{:S(2)}) collective-permute-start(bf16[512,256]{1,0:T(8,128)(2,1)S(1)} %collective-permute-done.7.refs_1_), channel_id=1, source_target_pairs={{0,1},{1,0},{2,3},{3,2},{4,5},{5,4},{6,7},{7,6},{8,9},{9,8},{10,11... | collective-permute-start | bytes 786440 | tf_op jit(solution)/shard_map/ppermute | solution.py:598
  27.4 2.5 %collective-permute-start.9 = (bf16[512,256]{1,0:T(8,128)(2,1)S(1)}, bf16[512,256]{1,0:T(8,128)(2,1)S(1)}, u32[]{:S(2)}, u32[]{:S(2)}) collective-permute-start(bf16[512,256]{1,0:T(8,128)(2,1)S(1)} %collective-permute-done.4.refs_0_), channel_id=1, source_target_pairs={{0,1},{1,0},{2,3},{3,2},{4,5},{5,4},{6,7},{7,6},{8,9},{9,8},{10,11... | collective-permute-start | bytes 786440 | tf_op jit(solution)/shard_map/ppermute | solution.py:598
  27.7 4.9 %collective-permute-start.12 = (f32[8,128]{1,0:T(8,128)S(1)}, f32[8,128]{1,0:T(8,128)S(1)}, u32[]{:S(2)}, u32[]{:S(2)}) collective-permute-start(f32[8,128]{1,0:T(8,128)S(1)} %add.6), channel_id=1, source_target_pairs={{0,4},{1,5},{2,6},{3,7},{4,0},{5,1},{6,2},{7,3},{8,12},{9,13},{10,... | collective-permute-start | bytes 12296 | tf_op jit(solution)/shard_map/ppermute | solution.py:601

commit v3 on v2

--- a/solution.py
+++ b/solution.py
@@ -217,7 +217,7 @@
         return (r, z + step, k) if 0 <= z + step < 4 else (r, z, 1 - k)
 
     return [[(d, ring(*d, up)) for d in devices] for up in (True, False)] + [
-        [((r, z, k), (r ^ (1 + (k + turn) % 2), z, k)) for r, z, k in devices] for turn in (0, 1)
+        [((r, z, k), (r ^ bit, z, k)) for r, z, k in devices] for bit in (1, 2)
     ]
 
 
@@ -301,7 +301,7 @@
         devices = {d ^ other for d in adds[s]}
         core = me.core ^ other
         before, after = me.line - 1 + 2 * core, me.line + 1 - 2 * core
-        row = (me.row, me.row, me.row, me.row ^ (1 + core), me.row ^ (2 - core))[s]
+        row = (me.row, me.row, me.row, me.row ^ 1, me.row ^ 2)[s]
         line = (me.line, before, after, me.line, me.line)[s]
         row_blocks, col_blocks = ref.shape[0] // BLK, ref.shape[1] // BLK
 
@@ -375,21 +375,22 @@
     blocks, half_blocks = tile // BLK, width // BLK
     zero = jnp.zeros((BLK, BLK), left.dtype)
 
+    def at_block(start):
+        return pl.ds(start if isinstance(start, int) else pl.multiple_of(start, BLK), BLK)
+
     def stored(a, b):
-        return raw[(b // 2) * tile + a * BLK : (b // 2) * tile + (a + 1) * BLK, (b % 2) * BLK : (b % 2 + 1) * BLK]
+        return raw[at_block((b // 2) * tile + a * BLK), at_block((b % 2) * BLK)]
 
     def direct(a, b):
-        start = pl.multiple_of(me.core * tile + a * BLK, BLK)
-        return raw[pl.ds(start, BLK), b * BLK : (b + 1) * BLK]
+        return raw[at_block(me.core * tile + a * BLK), at_block(b * BLK)]
 
     def mirrored(a, b):
-        start = pl.multiple_of((a // 2) * tile + (me.core * half_blocks + b) * BLK, BLK)
-        return raw[pl.ds(start, BLK), (a % 2) * BLK : (a % 2 + 1) * BLK].T
+        return raw[at_block((a // 2) * tile + (me.core * half_blocks + b) * BLK), at_block((a % 2) * BLK)].T
 
     left_ways = (
         stored,
         lambda a, b: stored(b, a).T,
-        lambda a, b: stored(a, b) if a <= b else stored(b, a).T,
+        lambda a, b: jnp.where(a <= b, stored(a, b), stored(b, a).T),
     )
     right_ways = (
         direct,
@@ -399,15 +400,25 @@
 
     def fill(panel, at, cols, u, block_of):
         j = u % 4
-        for a in range(blocks):
+
+        def block_row(a, carry):
             for b in range(cols):
-                rows = slice(at[0] + a * BLK, at[0] + (a + 1) * BLK)
-                lanes = slice(at[1] + b * BLK, at[1] + (b + 1) * BLK)
+                rows, lanes = at_block(at[0] + a * BLK), at_block(at[1] + b * BLK)
                 if u < 4:
                     flag = keep(panel, rows, lanes, me.row * blocks + a, j * blocks + b)
                 else:
                     flag = keep(panel, rows, lanes, j * blocks + a, me.col * half_blocks + b)
                 panel[rows, lanes] = jnp.where(flag, block_of(a, b), zero)
+            return carry
+
+        lax.fori_loop(0, blocks, block_row, 0)
+
+    def fetch(half, ref):
+        def block_row(a, carry):
+            raw[at_block(half * tile + a * BLK), :] = ref[at_block(a * BLK), :]
+            return carry
+
+        lax.fori_loop(0, blocks, block_row, 0)
 
     for u, here in enumerate(uses):
         j = u % 4
@@ -427,7 +438,7 @@
                     for s in sorted({here[d][half] for d in here}):
                         @pl.when(me.among([d for d in here if here[d][half] == s]))
                         def _():
-                            raw[half * tile : (half + 1) * tile, :] = shards[s][...]
+                            fetch(half, shards[s])
 
                 for way in sorted({above(d) for d in here}):
                     @pl.when(me.among([d for d in here if above(d) == way]))
@@ -435,70 +446,6 @@
                         fill(panel, at, cols, u, ways[way])
 
 
-def place_last_tiles(uses, me, shards, left, right, raw):
-    tile, width = left.shape[0], right.shape[1]
-    blocks, half_blocks = tile // BLK, width // BLK
-    part = 16
-
-    def put(panel, row_at, col_at, block):
-        lanes = slice(col_at, col_at + BLK)
-        flag = panel[row_at : row_at + part, lanes] != 0
-        for q in range(0, BLK, part):
-            value = block[q : q + part, :]
-            panel[row_at + q : row_at + q + part, lanes] = jnp.where(flag, value, jnp.zeros_like(value))
-
-    def square(ref, a, b):
-        return ref[a * BLK : (a + 1) * BLK, b * BLK : (b + 1) * BLK]
-
-    diagonal = [{} for _ in range(USES)]
-    for u, here in enumerate(uses):
-        j = u % 4
-        of_left = u < 4
-
-        def index(d):
-            return d // 8 if of_left else (d % 8) // 2
-
-        diagonal[u] = {d: here[d] for d in here if index(d) == j}
-        for half in range(2):
-            for s in sorted({here[d][half] for d in here}):
-                ref = shards[s]
-                found = [d for d in here if here[d][half] == s]
-                stands = [d for d in found if (index(d) < j if of_left else index(d) > j)]
-                lies = [d for d in found if (index(d) > j if of_left else index(d) < j)]
-                if of_left and stands:
-                    @pl.when(me.among(stands))
-                    def _():
-                        for a in range(blocks):
-                            for b in range(half_blocks):
-                                put(left, a * BLK, j * tile + (half * half_blocks + b) * BLK, square(ref, a, b))
-                if of_left and lies:
-                    @pl.when(me.among(lies))
-                    def _():
-                        for a in range(half_blocks):
-                            for b in range(blocks):
-                                put(left, (half * half_blocks + a) * BLK, j * tile + b * BLK, square(ref, b, a).T)
-                mine = [d for d in stands if d % 2 == half]
-                if not of_left and mine:
-                    @pl.when(me.among(mine))
-                    def _():
-                        for a in range(blocks):
-                            for b in range(half_blocks):
-                                put(right, j * tile + a * BLK, b * BLK, square(ref, a, b))
-                if not of_left and lies:
-                    @pl.when(me.among(lies))
-                    def _():
-                        for a in range(half_blocks):
-                            for b in range(half_blocks):
-                                start = pl.multiple_of((me.core * half_blocks + b) * BLK, BLK)
-                                block = ref[pl.ds(start, BLK), a * BLK : (a + 1) * BLK]
-                                put(right, j * tile + (half * half_blocks + a) * BLK, b * BLK, block.T)
-
-    def keep(panel, rows, lanes, i, j):
-        return panel[rows, lanes] != 0
-
-    place_tiles(diagonal, me, shards, keep, left, right, raw)
-
-
 def panels_kernel(uses, pattern, *refs):
     packed, left, right, keeps, raw = refs[FIRST:]
     me = Place()
@@ -512,12 +459,14 @@
     blocks, half_blocks = tile // BLK, width // BLK
 
     def flags(ref, row_at, col_at, cols, flag):
-        for a in range(blocks):
+        def block_row(a, carry):
             for b in range(cols):
                 value = jnp.where(flag(a, b), 1.0, 0.0).astype(ref.dtype)
-                ref[row_at + a * BLK : row_at + (a + 1) * BLK, col_at + b * BLK : col_at + (b + 1) * BLK] = (
-                    jnp.full((BLK, BLK), value, ref.dtype)
-                )
+                rows = pl.ds(pl.multiple_of(row_at + a * BLK, BLK), BLK)
+                ref[rows, col_at + b * BLK : col_at + (b + 1) * BLK] = jnp.full((BLK, BLK), value, ref.dtype)
+            return carry
+
+        lax.fori_loop(0, blocks, block_row, 0)
 
     for u, later in enumerate(uses[1]):
         j = u % 4
@@ -543,7 +492,11 @@
     shards = refs[: 2 * SECOND]
     keeps, _, _, left, right, out, raw, result, sems = refs[2 * SECOND :]
     me = Place()
-    place_last_tiles(uses[1], me, shards, left, right, raw)
+
+    def keep(panel, rows, lanes, i, j):
+        return panel[rows, lanes] != 0
+
+    place_tiles(uses[1], me, shards, keep, left, right, raw)
     height = out.shape[0]
     part = height // 2
     copies = []

time: 33.4 us -> 33 us (0.988)
  Pallas kernels: 6.36 us -> 7.68 us
  starting transfers between devices: 16.3 us -> 15.4 us
  waiting for transfers between devices: 8.23 us -> 7.43 us
    pallas_call x6, Pallas kernels: 6.36 us -> 7.68 us  [call(): pl.pallas_call(kernel, out_shape=out_shape, in_specs=[SMEM] * smem + [VME...]
    ppermute x2, starting transfers between devices: 5.08 us -> 4.13 us  [part_from(): lax.ppermute(parts, axes, [(d, d ^ row_bits * n_col + col_bits) for d in...]
    ppermute x3, waiting for transfers between devices: 2.64 us -> 1.85 us  [chip_grid(): lax.ppermute(value, axes, pairs)]
  transfers between devices with their start and end apart: 13 -> 13, of which waited for: 5 -> 6; matrix products, arithmetic and copies ran while one was open for 0% -> 0% of each run, Pallas kernels for 19% -> 23%
where the time goes in v3:
time: 33 us; the launch traced here: 32.9 us
  starting transfers between devices  15.4 us (47%)
  Pallas kernels  7.68 us (23%)
  waiting for transfers between devices  7.43 us (23%)
  local copies, waits for them, and re-layouts  0.99 us (3%)
  between operations  0.72 us (2%)
  other arithmetic  0.63 us (2%)
    pallas_call x6, Pallas kernels, call(): pl.pallas_call(kernel, out_shape=out_shape, in_specs=[SMEM] * smem + [VME...  7.68 us
    ppermute x4, starting transfers between devices, chip_grid(): came = [lax.ppermute(density, axes, pairs) for pairs in first]  6.05 us
    ppermute x4, waiting for transfers between devices, chip_grid(): came = [lax.ppermute(density, axes, pairs) for pairs in first]  5.32 us
    ppermute x3, starting transfers between devices, chip_grid(): lax.ppermute(value, axes, pairs)  4.31 us
    ppermute x2, starting transfers between devices, part_from(): lax.ppermute(parts, axes, [(d, d ^ row_bits * n_col + col_bits) for d in...  4.13 us
    ppermute x3, waiting for transfers between devices, chip_grid(): lax.ppermute(value, axes, pairs)  1.85 us
    unnamed x4, local copies, waits for them, and re-layouts  0.99 us
    ppermute x4, starting transfers between devices, share(): return lax.ppermute(value, axes, [(d, d ^ 1) for d in range(n_devices)])  0.92 us
  transfers between devices with their start and end apart: 13, of which 6 were waited for; matrix products, arithmetic and copies ran while one was open for 0% of the time, Pallas kernels for 23%

profile of v3, /device:TPU:0, one launch (start us, length us, event | category | flops | bytes accessed | tf_op | source)
XLA Modules:
  0.0 32.9 jit_solution(3741354234902020154)
XLA Ops:
  0.6 3.0 %collective-permute-start = (bf16[512,256]{1,0:T(8,128)(2,1)}, bf16[512,256]{1,0:T(8,128)(2,1)S(1)}, u32[]{:S(2)}, u32[]{:S(2)}) collective-permute-start(bf16[512,256]{1,0:T(8,128)(2,1)} %source.1), channel_id=1, source_target_pairs={{0,2},{1,0},{2,4},{3,1},{4,6},{5,3},{6,7},{7,5},{8,10},{9,8},{10,1... | collective-permute-start | bytes 786440 | tf_op jit(solution)/shard_map/ppermute | solution.py:556
  3.7 0.0 collective-permute-start.1
  3.7 1.5 %collective-permute-start.2 = (bf16[512,256]{1,0:T(8,128)(2,1)}, bf16[512,256]{1,0:T(8,128)(2,1)S(1)}, u32[]{:S(2)}, u32[]{:S(2)}) collective-permute-start(bf16[512,256]{1,0:T(8,128)(2,1)} %source.1), channel_id=1, source_target_pairs={{0,8},{1,9},{2,10},{3,11},{4,12},{5,13},{6,14},{7,15},{8,0},{9,1},... | collective-permute-start | bytes 786440 | tf_op jit(solution)/shard_map/ppermute | solution.py:556
  5.2 1.5 %collective-permute-start.3 = (bf16[512,256]{1,0:T(8,128)(2,1)}, bf16[512,256]{1,0:T(8,128)(2,1)S(1)}, u32[]{:S(2)}, u32[]{:S(2)}) collective-permute-start(bf16[512,256]{1,0:T(8,128)(2,1)} %source.1), channel_id=1, source_target_pairs={{0,16},{1,17},{2,18},{3,19},{4,20},{5,21},{6,22},{7,23},{8,24},{9,... | collective-permute-start | bytes 786440 | tf_op jit(solution)/shard_map/ppermute | solution.py:556
  6.7 0.0 copy-start
  6.7 1.0 %copy-done = bf16[512,256]{1,0:T(8,128)(2,1)S(1)} copy-done((bf16[512,256]{1,0:T(8,128)(2,1)S(1)}, bf16[512,256]{1,0:T(8,128)(2,1)}, u32[]{:S(2)}) %copy-start) | copy-done | bytes 262168
  7.7 0.0 copy-start.1
  7.7 1.9 %collective-permute-done.refs_1_ = bf16[512,256]{1,0:T(8,128)(2,1)S(1)} collective-permute-done((bf16[512,256]{1,0:T(8,128)(2,1)}, bf16[512,256]{1,0:T(8,128)(2,1)S(1)}, u32[]{:S(2)}, u32[]{:S(2)}) %collective-permute-start) | collective-permute-done | bytes 262176 | tf_op jit(solution)/shard_map/ppermute | solution.py:556
  9.6 0.7 %collective-permute-done.1.refs_2_ = bf16[512,256]{1,0:T(8,128)(2,1)S(1)} collective-permute-done((bf16[512,256]{1,0:T(8,128)(2,1)}, bf16[512,256]{1,0:T(8,128)(2,1)S(1)}, u32[]{:S(2)}, u32[]{:S(2)}) %collective-permute-start.1) | collective-permute-done | bytes 262176 | tf_op jit(solution)/shard_map/ppermute | solution.py:556
  10.3 1.4 %collective-permute-done.2.refs_3_ = bf16[512,256]{1,0:T(8,128)(2,1)S(1)} collective-permute-done((bf16[512,256]{1,0:T(8,128)(2,1)}, bf16[512,256]{1,0:T(8,128)(2,1)S(1)}, u32[]{:S(2)}, u32[]{:S(2)}) %collective-permute-start.2) | collective-permute-done | bytes 262176 | tf_op jit(solution)/shard_map/ppermute | solution.py:556
  11.7 1.4 %collective-permute-done.3.refs_4_ = bf16[512,256]{1,0:T(8,128)(2,1)S(1)} collective-permute-done((bf16[512,256]{1,0:T(8,128)(2,1)}, bf16[512,256]{1,0:T(8,128)(2,1)S(1)}, u32[]{:S(2)}, u32[]{:S(2)}) %collective-permute-start.3) | collective-permute-done | bytes 262176 | tf_op jit(solution)/shard_map/ppermute | solution.py:556
  13.0 0.1 shard_map.43
  13.1 0.1 collective-permute-start.5
  13.2 2.6 %collective-permute-start.4 = (bf16[512,256]{1,0:T(8,128)(2,1)S(1)}, bf16[512,256]{1,0:T(8,128)(2,1)S(1)}, u32[]{:S(2)}, u32[]{:S(2)}) collective-permute-start(bf16[512,256]{1,0:T(8,128)(2,1)S(1)} %get-tuple-element.37), channel_id=1, source_target_pairs={{1,7},{2,1},{4,13},{5,0},{6,5},{7,4},{10,14},{11,2},{12,3},{13,15}... | collective-permute-start | bytes 786440 | tf_op jit(solution)/shard_map/ppermute | solution.py:562
  15.8 0.0 collective-permute-start.7
  15.8 1.7 %collective-permute-start.8 = (bf16[512,256]{1,0:T(8,128)(2,1)S(1)}, bf16[512,256]{1,0:T(8,128)(2,1)S(1)}, u32[]{:S(2)}, u32[]{:S(2)}) collective-permute-start(bf16[512,256]{1,0:T(8,128)(2,1)S(1)} %get-tuple-element.51), channel_id=1, source_target_pairs={{2,7},{3,5},{4,2},{5,20},{6,15},{7,22},{14,23},{15,6},{21,12},{23,... | collective-permute-start | bytes 786440 | tf_op jit(solution)/shard_map/ppermute | solution.py:562
  17.5 0.0 collective-permute-done.5.refs_5_
  17.5 0.0 copy-done.1
  17.5 1.3 %shard_map.44 = f32[8,128]{1,0:T(8,128)S(1)} custom-call(s32[16,16]{1,0:T(8,128)S(1)} %copy-done.1, bf16[512,256]{1,0:T(8,128)(2,1)S(1)} %shard_map.41.refs_0_, bf16[512,256]{1,0:T(8,128)(2,1)S(1)} %collective-permute-done.refs_1_, bf16[512,256]{1,0:T(8,128)(2,1)S(1)} %collective-permute-done.1.refs_2_, bf16[512,256]{1,0:T(8,128)(2,1)S(1)} %collective-permute-done.2.refs_3_, ...), custom_call_target="tpu_custom_call" | custom-call | tf_op jit(solution)/shard_map/pallas_call | solution.py:539
  18.8 2.9 %collective-permute-start.6 = (f32[8,128]{1,0:T(8,128)S(1)}, f32[8,128]{1,0:T(8,128)S(1)}, u32[]{:S(2)}, u32[]{:S(2)}) collective-permute-start(f32[8,128]{1,0:T(8,128)S(1)} %shard_map.44), channel_id=1, source_target_pairs={{0,26},{1,27},{2,24},{3,25},{4,30},{5,31},{6,28},{7,29},{8,18},{9,... | collective-permute-start | bytes 12296 | tf_op jit(solution)/shard_map/ppermute | solution.py:554
  21.7 3.2 %shard_map.45 = (bf16[512,2048]{1,0:T(8,128)(2,1)S(1)}, bf16[2048,256]{1,0:T(8,128)(2,1)S(1)}, bf16[512,256]{1,0:T(8,128)(2,1)S(1)}) custom-call(s32[16,16]{1,0:T(8,128)S(1)} %copy-done.1, bf16[512,256]{1,0:T(8,128)(2,1)S(1)} %shard_map.41.refs_0_, bf16[512,256]{1,0:T(8,128)(2,1)S(1)} %collective-permute-done.refs_1_, ...), custom_call_target="tpu_custom_call" | custom-call | tf_op jit(solution)/shard_map/pallas_call | solution.py:539
  25.0 0.0 collective-permute-done.6
  25.0 0.0 collective-permute-done.4.refs_0_
  25.0 1.8 %collective-permute-done.7.refs_1_ = bf16[512,256]{1,0:T(8,128)(2,1)S(1)} collective-permute-done((bf16[512,256]{1,0:T(8,128)(2,1)S(1)}, bf16[512,256]{1,0:T(8,128)(2,1)S(1)}, u32[]{:S(2)}, u32[]{:S(2)}) %collective-permute-start.7) | collective-permute-done | bytes 262176 | tf_op jit(solution)/shard_map/ppermute | solution.py:562
  26.8 0.0 collective-permute-done.8.refs_2_
  26.8 0.3 %collective-permute-start.11 = (bf16[512,256]{1,0:T(8,128)(2,1)S(1)}, bf16[512,256]{1,0:T(8,128)(2,1)S(1)}, u32[]{:S(2)}, u32[]{:S(2)}) collective-permute-start(bf16[512,256]{1,0:T(8,128)(2,1)S(1)} %collective-permute-done.8.refs_2_), channel_id=1, source_target_pairs={{0,1},{1,0},{2,3},{3,2},{4,5},{5,4},{6,7},{7,6},{8,9},{9,8},{10,11... | collective-permute-start | bytes 786440 | tf_op jit(solution)/shard_map/ppermute | solution.py:551
  27.2 0.2 collective-permute-start.10
  27.4 0.3 %collective-permute-start.9 = (bf16[512,256]{1,0:T(8,128)(2,1)S(1)}, bf16[512,256]{1,0:T(8,128)(2,1)S(1)}, u32[]{:S(2)}, u32[]{:S(2)}) collective-permute-start(bf16[512,256]{1,0:T(8,128)(2,1)S(1)} %collective-permute-done.4.refs_0_), channel_id=1, source_target_pairs={{0,1},{1,0},{2,3},{3,2},{4,5},{5,4},{6,7},{7,6},{8,9},{9,8},{10,11... | collective-permute-start | bytes 786440 | tf_op jit(solution)/shard_map/ppermute | solution.py:551
  27.7 1.2 %collective-permute-start.12 = (f32[8,128]{1,0:T(8,128)S(1)}, f32[8,128]{1,0:T(8,128)S(1)}, u32[]{:S(2)}, u32[]{:S(2)}) collective-permute-start(f32[8,128]{1,0:T(8,128)S(1)} %add.6), channel_id=1, source_target_pairs={{0,4},{1,5},{2,6},{3,7},{4,0},{5,1},{6,2},{7,3},{8,12},{9,13},{10,... | collective-permute-start | bytes 12296 | tf_op jit(solution)/shard_map/ppermute | solution.py:554
  28.9 0.0 collective-permute-done.11.refs_5_
  28.9 0.0 collective-permute-done.10.refs_4_
  28.9 0.2 collective-permute-done.9.refs_3_
  29.1 3.1 %shard_map.46 = (bf16[512,2048]{1,0:T(8,128)(2,1)S(1)}, bf16[2048,256]{1,0:T(8,128)(2,1)S(1)}, bf16[512,256]{1,0:T(8,128)(2,1)}) custom-call(bf16[512,256]{1,0:T(8,128)(2,1)S(1)} %collective-permute-done.4.refs_0_, bf16[512,256]{1,0:T(8,128)(2,1)S(1)} %collective-permute-done.7.refs_1_, ...), custom_call_target="tpu_custom_call", output_to_operand_aliasing={{0}: (7, {}), {1}: (8, {})} | custom-call | tf_op jit(solution)/shard_map/pallas_call | solution.py:539
  32.2 0.0 collective-permute-done.12
  32.2 0.6 %add_reduce_fusion = f32[2]{0:T(128)} fusion(f32[8,128]{1,0:T(8,128)S(1)} %collective-permute-done.12, f32[8,128]{1,0:T(8,128)S(1)} %add.6), kind=kLoop, calls=%fused_computation | loop fusion | flops 510 | bytes 2056 | tf_op jit(solution)/shard_map/reduce_sum | solution.py:594
  (3 shorter events, 0.0 us)
Async XLA Ops:
  0.6 8.9 %collective-permute-start = (bf16[512,256]{1,0:T(8,128)(2,1)}, bf16[512,256]{1,0:T(8,128)(2,1)S(1)}, u32[]{:S(2)}, u32[]{:S(2)}) collective-permute-start(bf16[512,256]{1,0:T(8,128)(2,1)} %source.1), channel_id=1, source_target_pairs={{0,2},{1,0},{2,4},{3,1},{4,6},{5,3},{6,7},{7,5},{8,10},{9,8},{10,1... | collective-permute-start | bytes 786440 | tf_op jit(solution)/shard_map/ppermute | solution.py:556
  3.7 6.6 %collective-permute-start.1 = (bf16[512,256]{1,0:T(8,128)(2,1)}, bf16[512,256]{1,0:T(8,128)(2,1)S(1)}, u32[]{:S(2)}, u32[]{:S(2)}) collective-permute-start(bf16[512,256]{1,0:T(8,128)(2,1)} %source.1), channel_id=1, source_target_pairs={{0,1},{1,3},{2,0},{3,5},{4,2},{5,7},{6,4},{7,6},{8,9},{9,11},{10,8... | collective-permute-start | bytes 786440 | tf_op jit(solution)/shard_map/ppermute | solution.py:556
  3.7 8.0 %collective-permute-start.2 = (bf16[512,256]{1,0:T(8,128)(2,1)}, bf16[512,256]{1,0:T(8,128)(2,1)S(1)}, u32[]{:S(2)}, u32[]{:S(2)}) collective-permute-start(bf16[512,256]{1,0:T(8,128)(2,1)} %source.1), channel_id=1, source_target_pairs={{0,8},{1,9},{2,10},{3,11},{4,12},{5,13},{6,14},{7,15},{8,0},{9,1},... | collective-permute-start | bytes 786440 | tf_op jit(solution)/shard_map/ppermute | solution.py:556
  5.2 7.9 %collective-permute-start.3 = (bf16[512,256]{1,0:T(8,128)(2,1)}, bf16[512,256]{1,0:T(8,128)(2,1)S(1)}, u32[]{:S(2)}, u32[]{:S(2)}) collective-permute-start(bf16[512,256]{1,0:T(8,128)(2,1)} %source.1), channel_id=1, source_target_pairs={{0,16},{1,17},{2,18},{3,19},{4,20},{5,21},{6,22},{7,23},{8,24},{9,... | collective-permute-start | bytes 786440 | tf_op jit(solution)/shard_map/ppermute | solution.py:556
  6.7 1.0 %copy-start = (bf16[512,256]{1,0:T(8,128)(2,1)S(1)}, bf16[512,256]{1,0:T(8,128)(2,1)}, u32[]{:S(2)}) copy-start(bf16[512,256]{1,0:T(8,128)(2,1)} %source.1) | copy-start | bytes 786436
  7.7 9.8 %copy-start.1 = (s32[16,16]{1,0:T(8,128)S(1)}, s32[16,16]{1,0:T(8,128)}, u32[]{:S(2)}) copy-start(s32[16,16]{1,0:T(8,128)} %pattern.3) | copy-start | bytes 3076
  13.1 4.4 %collective-permute-start.5 = (bf16[5,512,256]{2,1,0:T(8,128)(2,1)S(1)}, bf16[5,512,256]{2,1,0:T(8,128)(2,1)S(1)}, u32[]{:S(2)}, u32[]{:S(2)}) collective-permute-start(bf16[5,512,256]{2,1,0:T(8,128)(2,1)S(1)} %shard_map.43), channel_id=1, source_target_pairs={{0,1},{1,0},{2,3},{3,2},{4,5},{5,4},{6,7},{7,6},{8,9},{9,8},{10,11... | collective-permute-start | bytes 3932168 | tf_op jit(solution)/shard_map/ppermute | solution.py:551
  13.2 11.8 %collective-permute-start.4 = (bf16[512,256]{1,0:T(8,128)(2,1)S(1)}, bf16[512,256]{1,0:T(8,128)(2,1)S(1)}, u32[]{:S(2)}, u32[]{:S(2)}) collective-permute-start(bf16[512,256]{1,0:T(8,128)(2,1)S(1)} %get-tuple-element.37), channel_id=1, source_target_pairs={{1,7},{2,1},{4,13},{5,0},{6,5},{7,4},{10,14},{11,2},{12,3},{13,15}... | collective-permute-start | bytes 786440 | tf_op jit(solution)/shard_map/ppermute | solution.py:562
  15.8 11.0 %collective-permute-start.7 = (bf16[512,256]{1,0:T(8,128)(2,1)S(1)}, bf16[512,256]{1,0:T(8,128)(2,1)S(1)}, u32[]{:S(2)}, u32[]{:S(2)}) collective-permute-start(bf16[512,256]{1,0:T(8,128)(2,1)S(1)} %get-tuple-element.48), channel_id=1, source_target_pairs={{5,12},{6,0},{7,22},{10,13},{11,15},{12,21},{13,1},{14,6},{15,3},{... | collective-permute-start | bytes 786440 | tf_op jit(solution)/shard_map/ppermute | solution.py:562
  15.8 11.0 %collective-permute-start.8 = (bf16[512,256]{1,0:T(8,128)(2,1)S(1)}, bf16[512,256]{1,0:T(8,128)(2,1)S(1)}, u32[]{:S(2)}, u32[]{:S(2)}) collective-permute-start(bf16[512,256]{1,0:T(8,128)(2,1)S(1)} %get-tuple-element.51), channel_id=1, source_target_pairs={{2,7},{3,5},{4,2},{5,20},{6,15},{7,22},{14,23},{15,6},{21,12},{23,... | collective-permute-start | bytes 786440 | tf_op jit(solution)/shard_map/ppermute | solution.py:562
  18.8 6.2 %collective-permute-start.6 = (f32[8,128]{1,0:T(8,128)S(1)}, f32[8,128]{1,0:T(8,128)S(1)}, u32[]{:S(2)}, u32[]{:S(2)}) collective-permute-start(f32[8,128]{1,0:T(8,128)S(1)} %shard_map.44), channel_id=1, source_target_pairs={{0,26},{1,27},{2,24},{3,25},{4,30},{5,31},{6,28},{7,29},{8,18},{9,... | collective-permute-start | bytes 12296 | tf_op jit(solution)/shard_map/ppermute | solution.py:554
  26.8 2.0 %collective-permute-start.11 = (bf16[512,256]{1,0:T(8,128)(2,1)S(1)}, bf16[512,256]{1,0:T(8,128)(2,1)S(1)}, u32[]{:S(2)}, u32[]{:S(2)}) collective-permute-start(bf16[512,256]{1,0:T(8,128)(2,1)S(1)} %collective-permute-done.8.refs_2_), channel_id=1, source_target_pairs={{0,1},{1,0},{2,3},{3,2},{4,5},{5,4},{6,7},{7,6},{8,9},{9,8},{10,11... | collective-permute-start | bytes 786440 | tf_op jit(solution)/shard_map/ppermute | solution.py:551
  27.2 1.7 %collective-permute-start.10 = (bf16[512,256]{1,0:T(8,128)(2,1)S(1)}, bf16[512,256]{1,0:T(8,128)(2,1)S(1)}, u32[]{:S(2)}, u32[]{:S(2)}) collective-permute-start(bf16[512,256]{1,0:T(8,128)(2,1)S(1)} %collective-permute-done.7.refs_1_), channel_id=1, source_target_pairs={{0,1},{1,0},{2,3},{3,2},{4,5},{5,4},{6,7},{7,6},{8,9},{9,8},{10,11... | collective-permute-start | bytes 786440 | tf_op jit(solution)/shard_map/ppermute | solution.py:551
  27.4 1.8 %collective-permute-start.9 = (bf16[512,256]{1,0:T(8,128)(2,1)S(1)}, bf16[512,256]{1,0:T(8,128)(2,1)S(1)}, u32[]{:S(2)}, u32[]{:S(2)}) collective-permute-start(bf16[512,256]{1,0:T(8,128)(2,1)S(1)} %collective-permute-done.4.refs_0_), channel_id=1, source_target_pairs={{0,1},{1,0},{2,3},{3,2},{4,5},{5,4},{6,7},{7,6},{8,9},{9,8},{10,11... | collective-permute-start | bytes 786440 | tf_op jit(solution)/shard_map/ppermute | solution.py:551
  27.7 4.5 %collective-permute-start.12 = (f32[8,128]{1,0:T(8,128)S(1)}, f32[8,128]{1,0:T(8,128)S(1)}, u32[]{:S(2)}, u32[]{:S(2)}) collective-permute-start(f32[8,128]{1,0:T(8,128)S(1)} %add.6), channel_id=1, source_target_pairs={{0,4},{1,5},{2,6},{3,7},{4,0},{5,1},{6,2},{7,3},{8,12},{9,13},{10,... | collective-permute-start | bytes 12296 | tf_op jit(solution)/shard_map/ppermute | solution.py:554

commit v4 on v3

--- a/solution.py
+++ b/solution.py
@@ -154,50 +154,50 @@
 SEEN = ((), (0,), (1, 3), (2,))
 
 MESSAGES = (
-    (0, (0, 0), 1, (0, 0, 1), (0, 3, 1)),
-    (0, (0, 2), 0, (0, 1, 0), (0, 0, 1)),
+    (0, (0, 0), 0, (0, 0, 0), (0, 3, 1)),
+    (0, (0, 2), 0, (0, 1, 0), (0, 0, 0)),
     (0, (2, 2), 0, (0, 2, 0), (1, 2, 1)),
-    (0, (0, 3), 1, (0, 2, 1), (0, 0, 0)),
-    (0, (2, 3), 0, (0, 3, 0), (0, 2, 1)),
-    (0, (2, 3), 1, (0, 3, 1), (0, 2, 0)),
-    (0, (0, 1), 0, (1, 1, 0), (1, 3, 0)),
-    (0, (1, 2), 1, (1, 1, 1), (0, 1, 0)),
-    (0, (1, 3), 0, (1, 2, 0), (0, 1, 1)),
-    (0, (1, 1), 1, (1, 2, 1), (1, 3, 1)),
-    (0, (0, 3), 0, (1, 3, 0), (3, 3, 1)),
-    (0, (1, 2), 1, (1, 3, 1), (2, 3, 0)),
+    (0, (0, 3), 1, (0, 2, 1), (0, 0, 1)),
+    (0, (2, 3), 0, (0, 3, 0), (0, 2, 0)),
+    (0, (0, 2), 1, (0, 3, 1), (2, 3, 1)),
+    (0, (0, 0), 1, (1, 0, 1), (0, 2, 1)),
+    (0, (1, 1), 0, (1, 2, 0), (1, 3, 0)),
+    (0, (1, 3), 1, (1, 2, 1), (0, 1, 0)),
+    (0, (1, 2), 0, (1, 3, 0), (2, 2, 0)),
     (0, (0, 1), 1, (2, 1, 1), (0, 3, 0)),
-    (0, (0, 3), 1, (2, 3, 1), (3, 3, 0)),
-    (0, (1, 2), 0, (3, 2, 0), (2, 3, 1)),
-    (0, (2, 3), 0, (3, 3, 0), (1, 2, 0)),
-    (0, (1, 3), 1, (3, 3, 1), (1, 1, 0)),
-    (1, (0, 1), 1, (0, 2, 1), (1, 2, 0)),
-    (1, (0, 3), 0, (0, 3, 0), (0, 0, 0)),
-    (1, (1, 3), 1, (0, 3, 1), (2, 3, 0)),
-    (1, (0, 1), 0, (1, 1, 0), (1, 2, 1)),
+    (0, (0, 2), 0, (2, 2, 0), (2, 3, 0)),
+    (0, (0, 3), 0, (2, 3, 0), (0, 1, 1)),
+    (0, (1, 1), 1, (3, 1, 1), (1, 3, 1)),
+    (0, (2, 2), 1, (3, 2, 1), (1, 2, 0)),
+    (0, (1, 3), 1, (3, 3, 1), (1, 1, 1)),
+    (1, (0, 0), 1, (0, 0, 1), (0, 3, 1)),
+    (1, (0, 3), 0, (0, 2, 0), (0, 0, 0)),
+    (1, (2, 3), 1, (0, 3, 1), (1, 3, 0)),
     (1, (0, 1), 1, (1, 1, 1), (1, 3, 1)),
-    (1, (1, 2), 0, (1, 2, 0), (2, 2, 1)),
-    (1, (0, 2), 1, (1, 2, 1), (0, 0, 1)),
-    (1, (3, 3), 0, (1, 3, 0), (0, 3, 0)),
-    (1, (1, 3), 1, (1, 3, 1), (0, 1, 1)),
+    (1, (1, 3), 0, (1, 2, 0), (0, 1, 1)),
+    (1, (1, 2), 0, (1, 3, 0), (2, 3, 0)),
     (1, (0, 0), 0, (2, 0, 0), (0, 2, 0)),
-    (1, (0, 1), 0, (2, 1, 0), (0, 3, 1)),
-    (1, (0, 2), 0, (2, 2, 0), (2, 3, 1)),
-    (1, (0, 3), 0, (2, 3, 0), (0, 1, 0)),
-    (1, (2, 3), 1, (2, 3, 1), (1, 3, 0)),
-    (2, (0, 0), 0, (0, 1, 0), (0, 3, 1)),
-    (2, (0, 0), 1, (0, 1, 1), (0, 2, 1)),
-    (2, (1, 2), 0, (0, 2, 0), (0, 1, 0)),
-    (2, (1, 2), 1, (0, 2, 1), (2, 2, 0)),
-    (2, (2, 3), 0, (0, 3, 0), (1, 3, 1)),
-    (2, (0, 2), 1, (0, 3, 1), (2, 3, 0)),
-    (2, (1, 3), 0, (1, 3, 0), (2, 3, 1)),
-    (2, (3, 3), 1, (1, 3, 1), (0, 3, 0)),
-    (2, (2, 3), 1, (2, 2, 1), (1, 2, 0)),
-    (2, (0, 3), 1, (2, 3, 1), (0, 1, 1)),
-    (2, (1, 1), 0, (3, 1, 0), (1, 3, 0)),
-    (2, (2, 2), 1, (3, 2, 1), (1, 2, 1)),
-    (2, (1, 3), 0, (3, 3, 0), (1, 1, 1)),
+    (1, (0, 1), 0, (2, 1, 0), (0, 3, 0)),
+    (1, (0, 2), 1, (2, 2, 1), (0, 0, 1)),
+    (1, (0, 3), 0, (2, 3, 0), (3, 3, 1)),
+    (1, (1, 2), 0, (3, 2, 0), (0, 1, 0)),
+    (1, (1, 2), 1, (3, 2, 1), (2, 3, 1)),
+    (1, (2, 3), 0, (3, 3, 0), (1, 2, 0)),
+    (1, (2, 3), 1, (3, 3, 1), (1, 2, 1)),
+    (2, (0, 1), 1, (0, 1, 1), (1, 2, 1)),
+    (2, (0, 1), 0, (0, 2, 0), (1, 2, 0)),
+    (2, (1, 3), 0, (0, 3, 0), (2, 3, 0)),
+    (2, (0, 3), 1, (0, 3, 1), (0, 1, 0)),
+    (2, (0, 1), 0, (1, 1, 0), (1, 3, 0)),
+    (2, (1, 2), 1, (1, 1, 1), (0, 1, 1)),
+    (2, (1, 3), 0, (1, 2, 0), (1, 1, 1)),
+    (2, (3, 3), 0, (1, 3, 0), (0, 3, 0)),
+    (2, (3, 3), 1, (1, 3, 1), (0, 3, 1)),
+    (2, (2, 3), 1, (2, 2, 1), (0, 2, 1)),
+    (2, (2, 3), 0, (2, 3, 0), (1, 3, 1)),
+    (2, (0, 3), 1, (2, 3, 1), (3, 3, 0)),
+    (2, (1, 2), 1, (3, 2, 1), (2, 2, 0)),
+    (2, (1, 3), 1, (3, 3, 1), (2, 3, 1)),
 )
 
 
@@ -222,18 +222,38 @@
 
 
 def closed(pairs, devices):
-    def hops(a, b):
-        return abs(a[1] - b[1]) + bin(a[0] ^ b[0]).count("1")
-
     sends, receives = {a for a, _ in pairs}, {b for _, b in pairs}
-    free = sorted((hops(a, b), a, b) for a in devices for b in devices if a not in sends and b not in receives and a != b)
-    extra = []
-    for _, a, b in free:
-        if a not in sends and b not in receives:
-            sends.add(a)
-            receives.add(b)
-            extra.append((a, b))
-    return pairs + extra
+    ends = [d for d in devices if d not in sends]
+    starts = [d for d in devices if d not in receives]
+
+    def cost(a, b):
+        return 1000 if a == b else (abs(a[1] - b[1]) + bin(a[0] ^ b[0]).count("1")) ** 2
+
+    size = len(ends)
+    u, v, row_of = [0] * (size + 1), [0] * (size + 1), [0] * (size + 1)
+    for i in range(1, size + 1):
+        row_of[0], col = i, 0
+        least, before, done = [10**6] * (size + 1), [0] * (size + 1), [False] * (size + 1)
+        while row_of[col]:
+            done[col], row, delta, following = True, row_of[col], 10**6, 0
+            for j in range(1, size + 1):
+                if not done[j]:
+                    slack = cost(ends[row - 1], starts[j - 1]) - u[row] - v[j]
+                    if slack < least[j]:
+                        least[j], before[j] = slack, col
+                    if least[j] < delta:
+                        delta, following = least[j], j
+            for j in range(size + 1):
+                if done[j]:
+                    u[row_of[j]] += delta
+                    v[j] -= delta
+                else:
+                    least[j] -= delta
+            col = following
+        while col:
+            row_of[col] = row_of[before[col]]
+            col = before[col]
+    return pairs + [(ends[row_of[j] - 1], starts[j - 1]) for j in range(1, size + 1)]
 
 
 def schedule():
@@ -292,7 +312,7 @@
 
 def partial_kernel(adds, order_size, pattern, *refs):
     me = Place()
-    packed, out, squares, diagonals = refs[FIRST:]
+    packed, out = refs[FIRST:]
     out[...] = jnp.zeros_like(out)
     at_row = lax.broadcasted_iota(jnp.int32, out.shape, 0)
     at_col = lax.broadcasted_iota(jnp.int32, out.shape, 1)
@@ -315,21 +335,19 @@
                     block = ref[a * BLK : (a + 1) * BLK, b * BLK : (b + 1) * BLK].astype(jnp.float32)
                     block = jnp.where((i <= j) & kept(pattern, i, j), block, zero)
                     total += jnp.where(i == j, 1.0, 2.0) * (block * block)
-            squares[...] = total
-            diagonals[...] = zero
+            lane = at_col == 8 * row + 2 * line + core
+            out[...] += jnp.where((at_row == 1) & lane, jnp.sum(total) / order_size, 0.0)
 
             @pl.when(row == line)
             def _():
                 rows_at = lax.broadcasted_iota(jnp.int32, (BLK, BLK), 0)
                 cols_at = lax.broadcasted_iota(jnp.int32, (BLK, BLK), 1)
+                diagonals = zero
                 for b in range(col_blocks):
                     start = pl.multiple_of((core * col_blocks + b) * BLK, BLK)
                     block = ref[pl.ds(start, BLK), b * BLK : (b + 1) * BLK].astype(jnp.float32)
-                    diagonals[...] += jnp.where(rows_at == cols_at, block, zero)
-
-            owner = 8 * row + 2 * line + core
-            for i, values in enumerate((diagonals, squares)):
-                out[...] += jnp.where((at_row == i) & (at_col == owner), jnp.sum(values[...]) / order_size, 0.0)
+                    diagonals += jnp.where(rows_at == cols_at, block, zero)
+                out[...] += jnp.where((at_row == 0) & lane, jnp.sum(diagonals) / order_size, 0.0)
 
 
 def copy_kernel(source, out):
@@ -375,22 +393,21 @@
     blocks, half_blocks = tile // BLK, width // BLK
     zero = jnp.zeros((BLK, BLK), left.dtype)
 
-    def at_block(start):
-        return pl.ds(start if isinstance(start, int) else pl.multiple_of(start, BLK), BLK)
-
     def stored(a, b):
-        return raw[at_block((b // 2) * tile + a * BLK), at_block((b % 2) * BLK)]
+        return raw[(b // 2) * tile + a * BLK : (b // 2) * tile + (a + 1) * BLK, (b % 2) * BLK : (b % 2 + 1) * BLK]
 
     def direct(a, b):
-        return raw[at_block(me.core * tile + a * BLK), at_block(b * BLK)]
+        start = pl.multiple_of(me.core * tile + a * BLK, BLK)
+        return raw[pl.ds(start, BLK), b * BLK : (b + 1) * BLK]
 
     def mirrored(a, b):
-        return raw[at_block((a // 2) * tile + (me.core * half_blocks + b) * BLK), at_block((a % 2) * BLK)].T
+        start = pl.multiple_of((a // 2) * tile + (me.core * half_blocks + b) * BLK, BLK)
+        return raw[pl.ds(start, BLK), (a % 2) * BLK : (a % 2 + 1) * BLK].T
 
     left_ways = (
         stored,
         lambda a, b: stored(b, a).T,
-        lambda a, b: jnp.where(a <= b, stored(a, b), stored(b, a).T),
+        lambda a, b: stored(a, b) if a <= b else stored(b, a).T,
     )
     right_ways = (
         direct,
@@ -400,25 +417,15 @@
 
     def fill(panel, at, cols, u, block_of):
         j = u % 4
-
-        def block_row(a, carry):
+        for a in range(blocks):
             for b in range(cols):
-                rows, lanes = at_block(at[0] + a * BLK), at_block(at[1] + b * BLK)
+                rows = slice(at[0] + a * BLK, at[0] + (a + 1) * BLK)
+                lanes = slice(at[1] + b * BLK, at[1] + (b + 1) * BLK)
                 if u < 4:
                     flag = keep(panel, rows, lanes, me.row * blocks + a, j * blocks + b)
                 else:
                     flag = keep(panel, rows, lanes, j * blocks + a, me.col * half_blocks + b)
                 panel[rows, lanes] = jnp.where(flag, block_of(a, b), zero)
-            return carry
-
-        lax.fori_loop(0, blocks, block_row, 0)
-
-    def fetch(half, ref):
-        def block_row(a, carry):
-            raw[at_block(half * tile + a * BLK), :] = ref[at_block(a * BLK), :]
-            return carry
-
-        lax.fori_loop(0, blocks, block_row, 0)
 
     for u, here in enumerate(uses):
         j = u % 4
@@ -438,7 +445,7 @@
                     for s in sorted({here[d][half] for d in here}):
                         @pl.when(me.among([d for d in here if here[d][half] == s]))
                         def _():
-                            fetch(half, shards[s])
+                            raw[half * tile : (half + 1) * tile, :] = shards[s][...]
 
                 for way in sorted({above(d) for d in here}):
                     @pl.when(me.among([d for d in here if above(d) == way]))
@@ -459,14 +466,12 @@
     blocks, half_blocks = tile // BLK, width // BLK
 
     def flags(ref, row_at, col_at, cols, flag):
-        def block_row(a, carry):
+        for a in range(blocks):
             for b in range(cols):
                 value = jnp.where(flag(a, b), 1.0, 0.0).astype(ref.dtype)
-                rows = pl.ds(pl.multiple_of(row_at + a * BLK, BLK), BLK)
-                ref[rows, col_at + b * BLK : col_at + (b + 1) * BLK] = jnp.full((BLK, BLK), value, ref.dtype)
-            return carry
-
-        lax.fori_loop(0, blocks, block_row, 0)
+                ref[row_at + a * BLK : row_at + (a + 1) * BLK, col_at + b * BLK : col_at + (b + 1) * BLK] = (
+                    jnp.full((BLK, BLK), value, ref.dtype)
+                )
 
     for u, later in enumerate(uses[1]):
         j = u % 4
@@ -566,7 +571,6 @@
         jax.ShapeDtypeStruct((8, 128), jnp.float32),
         1,
         [pattern] + held + [packed],
-        [pltpu.VMEM((BLK, BLK), jnp.float32)] * 2,
     )
     packed, parts = lax.optimization_barrier((packed, parts))
     received = part_from(parts, 3, 2)

time: 33 us -> 32.2 us (0.976)
  waiting for transfers between devices: 7.43 us -> 8.96 us
  starting transfers between devices: 15.4 us -> 14.2 us
  Pallas kernels: 7.68 us -> 6.61 us
    ppermute x2, waiting for transfers between devices: 0.01 us -> 1.99 us  [part_from(): lax.ppermute(parts, axes, [(d, d ^ row_bits * n_col + col_bits) for d in...]
    pallas_call x6, Pallas kernels: 7.68 us -> 6.61 us  [call(): pl.pallas_call(kernel, out_shape=out_shape, in_specs=[SMEM] * smem + [VME...]
    ppermute x2, starting transfers between devices: 4.13 us -> 3.22 us  [part_from(): lax.ppermute(parts, axes, [(d, d ^ row_bits * n_col + col_bits) for d in...]
    ppermute x4, starting transfers between devices: 0.92 us -> 0.59 us  [share(): return lax.ppermute(value, axes, [(d, d ^ 1) for d in range(n_devices)])]
  transfers between devices with their start and end apart: 13 -> 13, of which waited for: 6 -> 7; matrix products, arithmetic and copies ran while one was open for 0% -> 0% of each run, Pallas kernels for 23% -> 20%
where the time goes in v4:
time: 32.2 us; the launch traced here: 32.1 us
  starting transfers between devices  14.2 us (44%)
  waiting for transfers between devices  8.96 us (28%)
  Pallas kernels  6.61 us (21%)
  local copies, waits for them, and re-layouts  0.99 us (3%)
  between operations  0.71 us (2%)
  other arithmetic  0.63 us (2%)
    pallas_call x6, Pallas kernels, call(): pl.pallas_call(kernel, out_shape=out_shape, in_specs=[SMEM] * smem + [VME...  6.61 us
    ppermute x4, starting transfers between devices, chip_grid(): came = [lax.ppermute(density, axes, pairs) for pairs in first]  6.05 us
    ppermute x4, waiting for transfers between devices, chip_grid(): came = [lax.ppermute(density, axes, pairs) for pairs in first]  5.32 us
    ppermute x3, starting transfers between devices, chip_grid(): lax.ppermute(value, axes, pairs)  4.3 us
    ppermute x2, starting transfers between devices, part_from(): lax.ppermute(parts, axes, [(d, d ^ row_bits * n_col + col_bits) for d in...  3.22 us
    ppermute x2, waiting for transfers between devices, part_from(): lax.ppermute(parts, axes, [(d, d ^ row_bits * n_col + col_bits) for d in...  1.99 us
    ppermute x3, waiting for transfers between devices, chip_grid(): lax.ppermute(value, axes, pairs)  1.64 us
    unnamed x4, local copies, waits for them, and re-layouts  0.99 us
  transfers between devices with their start and end apart: 13, of which 7 were waited for; matrix products, arithmetic and copies ran while one was open for 0% of the time, Pallas kernels for 20%

profile of v4, /device:TPU:0, one launch (start us, length us, event | category | flops | bytes accessed | tf_op | source)
XLA Modules:
  0.0 32.1 jit_solution(16481381125181406330)
XLA Ops:
  0.6 3.0 %collective-permute-start = (bf16[512,256]{1,0:T(8,128)(2,1)}, bf16[512,256]{1,0:T(8,128)(2,1)S(1)}, u32[]{:S(2)}, u32[]{:S(2)}) collective-permute-start(bf16[512,256]{1,0:T(8,128)(2,1)} %source.1), channel_id=1, source_target_pairs={{0,2},{1,0},{2,4},{3,1},{4,6},{5,3},{6,7},{7,5},{8,10},{9,8},{10,1... | collective-permute-start | bytes 786440 | tf_op jit(solution)/shard_map/ppermute | solution.py:561
  3.7 0.0 collective-permute-start.1
  3.7 1.5 %collective-permute-start.2 = (bf16[512,256]{1,0:T(8,128)(2,1)}, bf16[512,256]{1,0:T(8,128)(2,1)S(1)}, u32[]{:S(2)}, u32[]{:S(2)}) collective-permute-start(bf16[512,256]{1,0:T(8,128)(2,1)} %source.1), channel_id=1, source_target_pairs={{0,8},{1,9},{2,10},{3,11},{4,12},{5,13},{6,14},{7,15},{8,0},{9,1},... | collective-permute-start | bytes 786440 | tf_op jit(solution)/shard_map/ppermute | solution.py:561
  5.2 1.5 %collective-permute-start.3 = (bf16[512,256]{1,0:T(8,128)(2,1)}, bf16[512,256]{1,0:T(8,128)(2,1)S(1)}, u32[]{:S(2)}, u32[]{:S(2)}) collective-permute-start(bf16[512,256]{1,0:T(8,128)(2,1)} %source.1), channel_id=1, source_target_pairs={{0,16},{1,17},{2,18},{3,19},{4,20},{5,21},{6,22},{7,23},{8,24},{9,... | collective-permute-start | bytes 786440 | tf_op jit(solution)/shard_map/ppermute | solution.py:561
  6.7 0.0 copy-start
  6.7 1.0 %copy-done = bf16[512,256]{1,0:T(8,128)(2,1)S(1)} copy-done((bf16[512,256]{1,0:T(8,128)(2,1)S(1)}, bf16[512,256]{1,0:T(8,128)(2,1)}, u32[]{:S(2)}) %copy-start) | copy-done | bytes 262168
  7.7 0.0 copy-start.1
  7.7 1.9 %collective-permute-done.refs_1_ = bf16[512,256]{1,0:T(8,128)(2,1)S(1)} collective-permute-done((bf16[512,256]{1,0:T(8,128)(2,1)}, bf16[512,256]{1,0:T(8,128)(2,1)S(1)}, u32[]{:S(2)}, u32[]{:S(2)}) %collective-permute-start) | collective-permute-done | bytes 262176 | tf_op jit(solution)/shard_map/ppermute | solution.py:561
  9.6 0.7 %collective-permute-done.1.refs_2_ = bf16[512,256]{1,0:T(8,128)(2,1)S(1)} collective-permute-done((bf16[512,256]{1,0:T(8,128)(2,1)}, bf16[512,256]{1,0:T(8,128)(2,1)S(1)}, u32[]{:S(2)}, u32[]{:S(2)}) %collective-permute-start.1) | collective-permute-done | bytes 262176 | tf_op jit(solution)/shard_map/ppermute | solution.py:561
  10.3 1.4 %collective-permute-done.2.refs_3_ = bf16[512,256]{1,0:T(8,128)(2,1)S(1)} collective-permute-done((bf16[512,256]{1,0:T(8,128)(2,1)}, bf16[512,256]{1,0:T(8,128)(2,1)S(1)}, u32[]{:S(2)}, u32[]{:S(2)}) %collective-permute-start.2) | collective-permute-done | bytes 262176 | tf_op jit(solution)/shard_map/ppermute | solution.py:561
  11.7 1.4 %collective-permute-done.3.refs_4_ = bf16[512,256]{1,0:T(8,128)(2,1)S(1)} collective-permute-done((bf16[512,256]{1,0:T(8,128)(2,1)}, bf16[512,256]{1,0:T(8,128)(2,1)S(1)}, u32[]{:S(2)}, u32[]{:S(2)}) %collective-permute-start.3) | collective-permute-done | bytes 262176 | tf_op jit(solution)/shard_map/ppermute | solution.py:561
  13.0 0.1 shard_map.42
  13.1 0.1 shard_map.43
  13.2 0.1 collective-permute-start.5
  13.3 2.9 %collective-permute-start.4 = (bf16[512,256]{1,0:T(8,128)(2,1)S(1)}, bf16[512,256]{1,0:T(8,128)(2,1)S(1)}, u32[]{:S(2)}, u32[]{:S(2)}) collective-permute-start(bf16[512,256]{1,0:T(8,128)(2,1)S(1)} %get-tuple-element.37), channel_id=1, source_target_pairs={{0,7},{2,0},{4,13},{5,1},{6,4},{7,23},{9,5},{12,14},{13,2},{14,20}... | collective-permute-start | bytes 786440 | tf_op jit(solution)/shard_map/ppermute | solution.py:567
  16.2 0.0 collective-permute-start.7
  16.2 1.4 %collective-permute-start.8 = (bf16[512,256]{1,0:T(8,128)(2,1)S(1)}, bf16[512,256]{1,0:T(8,128)(2,1)S(1)}, u32[]{:S(2)}, u32[]{:S(2)}) collective-permute-start(bf16[512,256]{1,0:T(8,128)(2,1)S(1)} %get-tuple-element.51), channel_id=1, source_target_pairs={{3,13},{4,12},{6,22},{7,2},{10,14},{11,3},{12,11},{14,6},{15,7},{2... | collective-permute-start | bytes 786440 | tf_op jit(solution)/shard_map/ppermute | solution.py:567
  17.6 0.0 collective-permute-done.5.refs_5_
  17.6 0.0 copy-done.1
  17.6 1.4 %shard_map.44 = f32[8,128]{1,0:T(8,128)S(1)} custom-call(s32[16,16]{1,0:T(8,128)S(1)} %copy-done.1, bf16[512,256]{1,0:T(8,128)(2,1)S(1)} %shard_map.41.refs_0_, bf16[512,256]{1,0:T(8,128)(2,1)S(1)} %collective-permute-done.refs_1_, bf16[512,256]{1,0:T(8,128)(2,1)S(1)} %collective-permute-done.1.refs_2_, bf16[512,256]{1,0:T(8,128)(2,1)S(1)} %collective-permute-done.2.refs_3_, ...), custom_call_target="tpu_custom_call" | custom-call | tf_op jit(solution)/shard_map/pallas_call | solution.py:544
  19.1 1.2 %collective-permute-start.6 = (f32[8,128]{1,0:T(8,128)S(1)}, f32[8,128]{1,0:T(8,128)S(1)}, u32[]{:S(2)}, u32[]{:S(2)}) collective-permute-start(f32[8,128]{1,0:T(8,128)S(1)} %shard_map.44), channel_id=1, source_target_pairs={{0,26},{1,27},{2,24},{3,25},{4,30},{5,31},{6,28},{7,29},{8,18},{9,... | collective-permute-start | bytes 12296 | tf_op jit(solution)/shard_map/ppermute | solution.py:559
  20.2 2.3 %shard_map.45 = (bf16[512,2048]{1,0:T(8,128)(2,1)S(1)}, bf16[2048,256]{1,0:T(8,128)(2,1)S(1)}, bf16[512,256]{1,0:T(8,128)(2,1)S(1)}) custom-call(s32[16,16]{1,0:T(8,128)S(1)} %copy-done.1, bf16[512,256]{1,0:T(8,128)(2,1)S(1)} %shard_map.41.refs_0_, bf16[512,256]{1,0:T(8,128)(2,1)S(1)} %collective-permute-done.refs_1_, ...), custom_call_target="tpu_custom_call" | custom-call | tf_op jit(solution)/shard_map/pallas_call | solution.py:544
  22.5 2.0 %collective-permute-done.6 = f32[8,128]{1,0:T(8,128)S(1)} collective-permute-done((f32[8,128]{1,0:T(8,128)S(1)}, f32[8,128]{1,0:T(8,128)S(1)}, u32[]{:S(2)}, u32[]{:S(2)}) %collective-permute-start.6) | collective-permute-done | bytes 4128 | tf_op jit(solution)/shard_map/ppermute | solution.py:559
  24.5 0.1 collective-permute-done.4.refs_0_
  24.6 1.5 %collective-permute-done.7.refs_1_ = bf16[512,256]{1,0:T(8,128)(2,1)S(1)} collective-permute-done((bf16[512,256]{1,0:T(8,128)(2,1)S(1)}, bf16[512,256]{1,0:T(8,128)(2,1)S(1)}, u32[]{:S(2)}, u32[]{:S(2)}) %collective-permute-start.7) | collective-permute-done | bytes 262176 | tf_op jit(solution)/shard_map/ppermute | solution.py:567
  26.2 0.0 collective-permute-done.8.refs_2_
  26.2 0.0 collective-permute-start.11
  26.2 0.5 %collective-permute-start.10 = (bf16[512,256]{1,0:T(8,128)(2,1)S(1)}, bf16[512,256]{1,0:T(8,128)(2,1)S(1)}, u32[]{:S(2)}, u32[]{:S(2)}) collective-permute-start(bf16[512,256]{1,0:T(8,128)(2,1)S(1)} %collective-permute-done.7.refs_1_), channel_id=1, source_target_pairs={{0,1},{1,0},{2,3},{3,2},{4,5},{5,4},{6,7},{7,6},{8,9},{9,8},{10,11... | collective-permute-start | bytes 786440 | tf_op jit(solution)/shard_map/ppermute | solution.py:556
  26.7 0.0 collective-permute-start.9
  26.7 2.0 %collective-permute-start.12 = (f32[8,128]{1,0:T(8,128)S(1)}, f32[8,128]{1,0:T(8,128)S(1)}, u32[]{:S(2)}, u32[]{:S(2)}) collective-permute-start(f32[8,128]{1,0:T(8,128)S(1)} %add.6), channel_id=1, source_target_pairs={{0,4},{1,5},{2,6},{3,7},{4,0},{5,1},{6,2},{7,3},{8,12},{9,13},{10,... | collective-permute-start | bytes 12296 | tf_op jit(solution)/shard_map/ppermute | solution.py:559
  28.7 0.0 collective-permute-done.11.refs_5_
  28.7 0.0 collective-permute-done.10.refs_4_
  28.7 0.0 collective-permute-done.9.refs_3_
  28.7 2.7 %shard_map.46 = (bf16[512,2048]{1,0:T(8,128)(2,1)S(1)}, bf16[2048,256]{1,0:T(8,128)(2,1)S(1)}, bf16[512,256]{1,0:T(8,128)(2,1)}) custom-call(bf16[512,256]{1,0:T(8,128)(2,1)S(1)} %collective-permute-done.4.refs_0_, bf16[512,256]{1,0:T(8,128)(2,1)S(1)} %collective-permute-done.7.refs_1_, ...), custom_call_target="tpu_custom_call", output_to_operand_aliasing={{0}: (7, {}), {1}: (8, {})} | custom-call | tf_op jit(solution)/shard_map/pallas_call | solution.py:544
  31.4 0.0 collective-permute-done.12
  31.4 0.6 %add_reduce_fusion = f32[2]{0:T(128)} fusion(f32[8,128]{1,0:T(8,128)S(1)} %collective-permute-done.12, f32[8,128]{1,0:T(8,128)S(1)} %add.6), kind=kLoop, calls=%fused_computation | loop fusion | flops 510 | bytes 2056 | tf_op jit(solution)/shard_map/reduce_sum | solution.py:598
  (2 shorter events, 0.0 us)
Async XLA Ops:
  0.6 8.9 %collective-permute-start = (bf16[512,256]{1,0:T(8,128)(2,1)}, bf16[512,256]{1,0:T(8,128)(2,1)S(1)}, u32[]{:S(2)}, u32[]{:S(2)}) collective-permute-start(bf16[512,256]{1,0:T(8,128)(2,1)} %source.1), channel_id=1, source_target_pairs={{0,2},{1,0},{2,4},{3,1},{4,6},{5,3},{6,7},{7,5},{8,10},{9,8},{10,1... | collective-permute-start | bytes 786440 | tf_op jit(solution)/shard_map/ppermute | solution.py:561
  3.7 6.6 %collective-permute-start.1 = (bf16[512,256]{1,0:T(8,128)(2,1)}, bf16[512,256]{1,0:T(8,128)(2,1)S(1)}, u32[]{:S(2)}, u32[]{:S(2)}) collective-permute-start(bf16[512,256]{1,0:T(8,128)(2,1)} %source.1), channel_id=1, source_target_pairs={{0,1},{1,3},{2,0},{3,5},{4,2},{5,7},{6,4},{7,6},{8,9},{9,11},{10,8... | collective-permute-start | bytes 786440 | tf_op jit(solution)/shard_map/ppermute | solution.py:561
  3.7 8.0 %collective-permute-start.2 = (bf16[512,256]{1,0:T(8,128)(2,1)}, bf16[512,256]{1,0:T(8,128)(2,1)S(1)}, u32[]{:S(2)}, u32[]{:S(2)}) collective-permute-start(bf16[512,256]{1,0:T(8,128)(2,1)} %source.1), channel_id=1, source_target_pairs={{0,8},{1,9},{2,10},{3,11},{4,12},{5,13},{6,14},{7,15},{8,0},{9,1},... | collective-permute-start | bytes 786440 | tf_op jit(solution)/shard_map/ppermute | solution.py:561
  5.2 7.9 %collective-permute-start.3 = (bf16[512,256]{1,0:T(8,128)(2,1)}, bf16[512,256]{1,0:T(8,128)(2,1)S(1)}, u32[]{:S(2)}, u32[]{:S(2)}) collective-permute-start(bf16[512,256]{1,0:T(8,128)(2,1)} %source.1), channel_id=1, source_target_pairs={{0,16},{1,17},{2,18},{3,19},{4,20},{5,21},{6,22},{7,23},{8,24},{9,... | collective-permute-start | bytes 786440 | tf_op jit(solution)/shard_map/ppermute | solution.py:561
  6.7 1.0 %copy-start = (bf16[512,256]{1,0:T(8,128)(2,1)S(1)}, bf16[512,256]{1,0:T(8,128)(2,1)}, u32[]{:S(2)}) copy-start(bf16[512,256]{1,0:T(8,128)(2,1)} %source.1) | copy-start | bytes 786436
  7.7 9.9 %copy-start.1 = (s32[16,16]{1,0:T(8,128)S(1)}, s32[16,16]{1,0:T(8,128)}, u32[]{:S(2)}) copy-start(s32[16,16]{1,0:T(8,128)} %pattern.3) | copy-start | bytes 3076
  13.2 4.4 %collective-permute-start.5 = (bf16[5,512,256]{2,1,0:T(8,128)(2,1)S(1)}, bf16[5,512,256]{2,1,0:T(8,128)(2,1)S(1)}, u32[]{:S(2)}, u32[]{:S(2)}) collective-permute-start(bf16[5,512,256]{2,1,0:T(8,128)(2,1)S(1)} %shard_map.43), channel_id=1, source_target_pairs={{0,1},{1,0},{2,3},{3,2},{4,5},{5,4},{6,7},{7,6},{8,9},{9,8},{10,11... | collective-permute-start | bytes 3932168 | tf_op jit(solution)/shard_map/ppermute | solution.py:556
  13.3 11.3 %collective-permute-start.4 = (bf16[512,256]{1,0:T(8,128)(2,1)S(1)}, bf16[512,256]{1,0:T(8,128)(2,1)S(1)}, u32[]{:S(2)}, u32[]{:S(2)}) collective-permute-start(bf16[512,256]{1,0:T(8,128)(2,1)S(1)} %get-tuple-element.37), channel_id=1, source_target_pairs={{0,7},{2,0},{4,13},{5,1},{6,4},{7,23},{9,5},{12,14},{13,2},{14,20}... | collective-permute-start | bytes 786440 | tf_op jit(solution)/shard_map/ppermute | solution.py:567
  16.2 9.9 %collective-permute-start.7 = (bf16[512,256]{1,0:T(8,128)(2,1)S(1)}, bf16[512,256]{1,0:T(8,128)(2,1)S(1)}, u32[]{:S(2)}, u32[]{:S(2)}) collective-permute-start(bf16[512,256]{1,0:T(8,128)(2,1)S(1)} %get-tuple-element.48), channel_id=1, source_target_pairs={{1,7},{4,0},{7,14},{11,15},{12,3},{14,22},{16,4},{18,6},{21,1},{22... | collective-permute-start | bytes 786440 | tf_op jit(solution)/shard_map/ppermute | solution.py:567
  16.2 9.9 %collective-permute-start.8 = (bf16[512,256]{1,0:T(8,128)(2,1)S(1)}, bf16[512,256]{1,0:T(8,128)(2,1)S(1)}, u32[]{:S(2)}, u32[]{:S(2)}) collective-permute-start(bf16[512,256]{1,0:T(8,128)(2,1)S(1)} %get-tuple-element.51), channel_id=1, source_target_pairs={{3,13},{4,12},{6,22},{7,2},{10,14},{11,3},{12,11},{14,6},{15,7},{2... | collective-permute-start | bytes 786440 | tf_op jit(solution)/shard_map/ppermute | solution.py:567
  19.1 5.5 %collective-permute-start.6 = (f32[8,128]{1,0:T(8,128)S(1)}, f32[8,128]{1,0:T(8,128)S(1)}, u32[]{:S(2)}, u32[]{:S(2)}) collective-permute-start(f32[8,128]{1,0:T(8,128)S(1)} %shard_map.44), channel_id=1, source_target_pairs={{0,26},{1,27},{2,24},{3,25},{4,30},{5,31},{6,28},{7,29},{8,18},{9,... | collective-permute-start | bytes 12296 | tf_op jit(solution)/shard_map/ppermute | solution.py:559
  26.2 2.6 %collective-permute-start.11 = (bf16[512,256]{1,0:T(8,128)(2,1)S(1)}, bf16[512,256]{1,0:T(8,128)(2,1)S(1)}, u32[]{:S(2)}, u32[]{:S(2)}) collective-permute-start(bf16[512,256]{1,0:T(8,128)(2,1)S(1)} %collective-permute-done.8.refs_2_), channel_id=1, source_target_pairs={{0,1},{1,0},{2,3},{3,2},{4,5},{5,4},{6,7},{7,6},{8,9},{9,8},{10,11... | collective-permute-start | bytes 786440 | tf_op jit(solution)/shard_map/ppermute | solution.py:556
  26.2 2.6 %collective-permute-start.10 = (bf16[512,256]{1,0:T(8,128)(2,1)S(1)}, bf16[512,256]{1,0:T(8,128)(2,1)S(1)}, u32[]{:S(2)}, u32[]{:S(2)}) collective-permute-start(bf16[512,256]{1,0:T(8,128)(2,1)S(1)} %collective-permute-done.7.refs_1_), channel_id=1, source_target_pairs={{0,1},{1,0},{2,3},{3,2},{4,5},{5,4},{6,7},{7,6},{8,9},{9,8},{10,11... | collective-permute-start | bytes 786440 | tf_op jit(solution)/shard_map/ppermute | solution.py:556
  26.7 2.1 %collective-permute-start.9 = (bf16[512,256]{1,0:T(8,128)(2,1)S(1)}, bf16[512,256]{1,0:T(8,128)(2,1)S(1)}, u32[]{:S(2)}, u32[]{:S(2)}) collective-permute-start(bf16[512,256]{1,0:T(8,128)(2,1)S(1)} %collective-permute-done.4.refs_0_), channel_id=1, source_target_pairs={{0,1},{1,0},{2,3},{3,2},{4,5},{5,4},{6,7},{7,6},{8,9},{9,8},{10,11... | collective-permute-start | bytes 786440 | tf_op jit(solution)/shard_map/ppermute | solution.py:556
  26.7 4.7 %collective-permute-start.12 = (f32[8,128]{1,0:T(8,128)S(1)}, f32[8,128]{1,0:T(8,128)S(1)}, u32[]{:S(2)}, u32[]{:S(2)}) collective-permute-start(f32[8,128]{1,0:T(8,128)S(1)} %add.6), channel_id=1, source_target_pairs={{0,4},{1,5},{2,6},{3,7},{4,0},{5,1},{6,2},{7,3},{8,12},{9,13},{10,... | collective-permute-start | bytes 12296 | tf_op jit(solution)/shard_map/ppermute | solution.py:559

commit v5 on v4

--- a/solution.py
+++ b/solution.py
@@ -154,49 +154,49 @@
 SEEN = ((), (0,), (1, 3), (2,))
 
 MESSAGES = (
-    (0, (0, 0), 0, (0, 0, 0), (0, 3, 1)),
-    (0, (0, 2), 0, (0, 1, 0), (0, 0, 0)),
-    (0, (2, 2), 0, (0, 2, 0), (1, 2, 1)),
+    (0, (0, 0), 1, (0, 0, 1), (0, 3, 1)),
+    (0, (0, 3), 0, (0, 2, 0), (0, 0, 0)),
     (0, (0, 3), 1, (0, 2, 1), (0, 0, 1)),
     (0, (2, 3), 0, (0, 3, 0), (0, 2, 0)),
     (0, (0, 2), 1, (0, 3, 1), (2, 3, 1)),
-    (0, (0, 0), 1, (1, 0, 1), (0, 2, 1)),
-    (0, (1, 1), 0, (1, 2, 0), (1, 3, 0)),
-    (0, (1, 3), 1, (1, 2, 1), (0, 1, 0)),
-    (0, (1, 2), 0, (1, 3, 0), (2, 2, 0)),
-    (0, (0, 1), 1, (2, 1, 1), (0, 3, 0)),
+    (0, (0, 1), 0, (1, 1, 0), (1, 3, 1)),
+    (0, (1, 2), 0, (1, 2, 0), (2, 2, 0)),
+    (0, (1, 3), 1, (1, 3, 1), (0, 1, 1)),
+    (0, (0, 0), 0, (2, 0, 0), (0, 2, 1)),
+    (0, (0, 1), 0, (2, 1, 0), (0, 3, 0)),
     (0, (0, 2), 0, (2, 2, 0), (2, 3, 0)),
-    (0, (0, 3), 0, (2, 3, 0), (0, 1, 1)),
-    (0, (1, 1), 1, (3, 1, 1), (1, 3, 1)),
-    (0, (2, 2), 1, (3, 2, 1), (1, 2, 0)),
-    (0, (1, 3), 1, (3, 3, 1), (1, 1, 1)),
-    (1, (0, 0), 1, (0, 0, 1), (0, 3, 1)),
-    (1, (0, 3), 0, (0, 2, 0), (0, 0, 0)),
+    (0, (0, 3), 0, (2, 3, 0), (0, 1, 0)),
+    (0, (1, 1), 1, (3, 1, 1), (1, 3, 0)),
+    (0, (2, 2), 0, (3, 2, 0), (1, 2, 0)),
+    (0, (2, 2), 1, (3, 2, 1), (1, 2, 1)),
+    (0, (1, 3), 1, (3, 3, 1), (1, 1, 0)),
+    (1, (0, 0), 0, (0, 0, 0), (0, 3, 1)),
+    (1, (0, 2), 0, (0, 1, 0), (0, 0, 0)),
+    (1, (0, 1), 1, (0, 2, 1), (1, 3, 1)),
+    (1, (2, 3), 0, (0, 3, 0), (1, 2, 0)),
     (1, (2, 3), 1, (0, 3, 1), (1, 3, 0)),
-    (1, (0, 1), 1, (1, 1, 1), (1, 3, 1)),
-    (1, (1, 3), 0, (1, 2, 0), (0, 1, 1)),
-    (1, (1, 2), 0, (1, 3, 0), (2, 3, 0)),
-    (1, (0, 0), 0, (2, 0, 0), (0, 2, 0)),
-    (1, (0, 1), 0, (2, 1, 0), (0, 3, 0)),
+    (1, (0, 0), 1, (1, 0, 1), (0, 2, 0)),
+    (1, (1, 3), 0, (1, 2, 0), (0, 1, 0)),
+    (1, (1, 2), 0, (1, 3, 0), (2, 3, 1)),
+    (1, (1, 2), 1, (1, 3, 1), (2, 3, 0)),
+    (1, (0, 1), 1, (2, 1, 1), (0, 3, 0)),
     (1, (0, 2), 1, (2, 2, 1), (0, 0, 1)),
-    (1, (0, 3), 0, (2, 3, 0), (3, 3, 1)),
-    (1, (1, 2), 0, (3, 2, 0), (0, 1, 0)),
-    (1, (1, 2), 1, (3, 2, 1), (2, 3, 1)),
-    (1, (2, 3), 0, (3, 3, 0), (1, 2, 0)),
+    (1, (0, 3), 0, (2, 3, 0), (3, 3, 0)),
+    (1, (1, 2), 0, (3, 2, 0), (0, 1, 1)),
     (1, (2, 3), 1, (3, 3, 1), (1, 2, 1)),
     (2, (0, 1), 1, (0, 1, 1), (1, 2, 1)),
     (2, (0, 1), 0, (0, 2, 0), (1, 2, 0)),
     (2, (1, 3), 0, (0, 3, 0), (2, 3, 0)),
-    (2, (0, 3), 1, (0, 3, 1), (0, 1, 0)),
-    (2, (0, 1), 0, (1, 1, 0), (1, 3, 0)),
-    (2, (1, 2), 1, (1, 1, 1), (0, 1, 1)),
+    (2, (0, 3), 1, (0, 3, 1), (0, 1, 1)),
+    (2, (1, 1), 0, (1, 1, 0), (1, 3, 1)),
+    (2, (1, 2), 1, (1, 1, 1), (0, 1, 0)),
     (2, (1, 3), 0, (1, 2, 0), (1, 1, 1)),
-    (2, (3, 3), 0, (1, 3, 0), (0, 3, 0)),
+    (2, (1, 2), 1, (1, 2, 1), (2, 2, 0)),
     (2, (3, 3), 1, (1, 3, 1), (0, 3, 1)),
     (2, (2, 3), 1, (2, 2, 1), (0, 2, 1)),
-    (2, (2, 3), 0, (2, 3, 0), (1, 3, 1)),
+    (2, (3, 3), 0, (2, 3, 0), (0, 3, 0)),
     (2, (0, 3), 1, (2, 3, 1), (3, 3, 0)),
-    (2, (1, 2), 1, (3, 2, 1), (2, 2, 0)),
+    (2, (2, 3), 0, (3, 3, 0), (1, 3, 0)),
     (2, (1, 3), 1, (3, 3, 1), (2, 3, 1)),
 )
 

time: 32.2 us -> 32.7 us (1.016); the launches traced: 32.1 us -> 32.1 us
  starting transfers between devices: 14.2 us -> 14.7 us
  waiting for transfers between devices: 8.96 us -> 8.53 us
    ppermute x2, starting transfers between devices: 3.22 us -> 3.81 us  [part_from(): lax.ppermute(parts, axes, [(d, d ^ row_bits * n_col + col_bits) for d in...]
    ppermute x3, waiting for transfers between devices: 1.64 us -> 1.29 us  [chip_grid(): lax.ppermute(value, axes, pairs)]
where the time goes in v5:
time: 32.7 us; the launch traced here: 32.1 us
  starting transfers between devices  14.7 us (45%)
  waiting for transfers between devices  8.53 us (26%)
  Pallas kernels  6.57 us (20%)
  local copies, waits for them, and re-layouts  0.99 us (3%)
  between operations  0.72 us (2%)
  other arithmetic  0.63 us (2%)
    pallas_call x6, Pallas kernels, call(): pl.pallas_call(kernel, out_shape=out_shape, in_specs=[SMEM] * smem + [VME...  6.57 us
    ppermute x4, starting transfers between devices, chip_grid(): came = [lax.ppermute(density, axes, pairs) for pairs in first]  6.05 us
    ppermute x4, waiting for transfers between devices, chip_grid(): came = [lax.ppermute(density, axes, pairs) for pairs in first]  5.32 us
    ppermute x3, starting transfers between devices, chip_grid(): lax.ppermute(value, axes, pairs)  4.22 us
    ppermute x2, starting transfers between devices, part_from(): lax.ppermute(parts, axes, [(d, d ^ row_bits * n_col + col_bits) for d in...  3.81 us
    ppermute x2, waiting for transfers between devices, part_from(): lax.ppermute(parts, axes, [(d, d ^ row_bits * n_col + col_bits) for d in...  1.91 us
    ppermute x3, waiting for transfers between devices, chip_grid(): lax.ppermute(value, axes, pairs)  1.29 us
    unnamed x4, local copies, waits for them, and re-layouts  0.99 us
  transfers between devices with their start and end apart: 13, of which 7 were waited for; matrix products, arithmetic and copies ran while one was open for 0% of the time, Pallas kernels for 20%

profile of v5, /device:TPU:0, one launch (start us, length us, event | category | flops | bytes accessed | tf_op | source)
XLA Modules:
  0.0 32.1 jit_solution(10073936220079917967)
XLA Ops:
  0.6 3.0 %collective-permute-start = (bf16[512,256]{1,0:T(8,128)(2,1)}, bf16[512,256]{1,0:T(8,128)(2,1)S(1)}, u32[]{:S(2)}, u32[]{:S(2)}) collective-permute-start(bf16[512,256]{1,0:T(8,128)(2,1)} %source.1), channel_id=1, source_target_pairs={{0,2},{1,0},{2,4},{3,1},{4,6},{5,3},{6,7},{7,5},{8,10},{9,8},{10,1... | collective-permute-start | bytes 786440 | tf_op jit(solution)/shard_map/ppermute | solution.py:561
  3.7 0.0 collective-permute-start.1
  3.7 1.5 %collective-permute-start.2 = (bf16[512,256]{1,0:T(8,128)(2,1)}, bf16[512,256]{1,0:T(8,128)(2,1)S(1)}, u32[]{:S(2)}, u32[]{:S(2)}) collective-permute-start(bf16[512,256]{1,0:T(8,128)(2,1)} %source.1), channel_id=1, source_target_pairs={{0,8},{1,9},{2,10},{3,11},{4,12},{5,13},{6,14},{7,15},{8,0},{9,1},... | collective-permute-start | bytes 786440 | tf_op jit(solution)/shard_map/ppermute | solution.py:561
  5.2 1.5 %collective-permute-start.3 = (bf16[512,256]{1,0:T(8,128)(2,1)}, bf16[512,256]{1,0:T(8,128)(2,1)S(1)}, u32[]{:S(2)}, u32[]{:S(2)}) collective-permute-start(bf16[512,256]{1,0:T(8,128)(2,1)} %source.1), channel_id=1, source_target_pairs={{0,16},{1,17},{2,18},{3,19},{4,20},{5,21},{6,22},{7,23},{8,24},{9,... | collective-permute-start | bytes 786440 | tf_op jit(solution)/shard_map/ppermute | solution.py:561
  6.7 0.0 copy-start
  6.7 1.0 %copy-done = bf16[512,256]{1,0:T(8,128)(2,1)S(1)} copy-done((bf16[512,256]{1,0:T(8,128)(2,1)S(1)}, bf16[512,256]{1,0:T(8,128)(2,1)}, u32[]{:S(2)}) %copy-start) | copy-done | bytes 262168
  7.7 0.0 copy-start.1
  7.7 1.9 %collective-permute-done.refs_1_ = bf16[512,256]{1,0:T(8,128)(2,1)S(1)} collective-permute-done((bf16[512,256]{1,0:T(8,128)(2,1)}, bf16[512,256]{1,0:T(8,128)(2,1)S(1)}, u32[]{:S(2)}, u32[]{:S(2)}) %collective-permute-start) | collective-permute-done | bytes 262176 | tf_op jit(solution)/shard_map/ppermute | solution.py:561
  9.6 0.7 %collective-permute-done.1.refs_2_ = bf16[512,256]{1,0:T(8,128)(2,1)S(1)} collective-permute-done((bf16[512,256]{1,0:T(8,128)(2,1)}, bf16[512,256]{1,0:T(8,128)(2,1)S(1)}, u32[]{:S(2)}, u32[]{:S(2)}) %collective-permute-start.1) | collective-permute-done | bytes 262176 | tf_op jit(solution)/shard_map/ppermute | solution.py:561
  10.3 1.4 %collective-permute-done.2.refs_3_ = bf16[512,256]{1,0:T(8,128)(2,1)S(1)} collective-permute-done((bf16[512,256]{1,0:T(8,128)(2,1)}, bf16[512,256]{1,0:T(8,128)(2,1)S(1)}, u32[]{:S(2)}, u32[]{:S(2)}) %collective-permute-start.2) | collective-permute-done | bytes 262176 | tf_op jit(solution)/shard_map/ppermute | solution.py:561
  11.7 1.4 %collective-permute-done.3.refs_4_ = bf16[512,256]{1,0:T(8,128)(2,1)S(1)} collective-permute-done((bf16[512,256]{1,0:T(8,128)(2,1)}, bf16[512,256]{1,0:T(8,128)(2,1)S(1)}, u32[]{:S(2)}, u32[]{:S(2)}) %collective-permute-start.3) | collective-permute-done | bytes 262176 | tf_op jit(solution)/shard_map/ppermute | solution.py:561
  13.0 0.1 shard_map.42
  13.1 0.1 shard_map.43
  13.2 0.1 collective-permute-start.5
  13.3 1.6 %collective-permute-start.4 = (bf16[512,256]{1,0:T(8,128)(2,1)S(1)}, bf16[512,256]{1,0:T(8,128)(2,1)S(1)}, u32[]{:S(2)}, u32[]{:S(2)}) collective-permute-start(bf16[512,256]{1,0:T(8,128)(2,1)S(1)} %get-tuple-element.37), channel_id=1, source_target_pairs={{1,7},{4,0},{5,1},{6,4},{7,23},{10,15},{12,20},{15,3},{16,5},{18,6... | collective-permute-start | bytes 786440 | tf_op jit(solution)/shard_map/ppermute | solution.py:567
  14.9 2.6 %collective-permute-start.7 = (bf16[512,256]{1,0:T(8,128)(2,1)S(1)}, bf16[512,256]{1,0:T(8,128)(2,1)S(1)}, u32[]{:S(2)}, u32[]{:S(2)}) collective-permute-start(bf16[512,256]{1,0:T(8,128)(2,1)S(1)} %get-tuple-element.48), channel_id=1, source_target_pairs={{0,7},{2,0},{5,15},{6,12},{7,14},{9,4},{12,2},{14,23},{15,22},{19,... | collective-permute-start | bytes 786440 | tf_op jit(solution)/shard_map/ppermute | solution.py:567
  17.5 0.0 collective-permute-start.8
  17.5 0.0 collective-permute-done.5.refs_5_
  17.5 0.0 copy-done.1
  17.5 1.4 %shard_map.44 = f32[8,128]{1,0:T(8,128)S(1)} custom-call(s32[16,16]{1,0:T(8,128)S(1)} %copy-done.1, bf16[512,256]{1,0:T(8,128)(2,1)S(1)} %shard_map.41.refs_0_, bf16[512,256]{1,0:T(8,128)(2,1)S(1)} %collective-permute-done.refs_1_, bf16[512,256]{1,0:T(8,128)(2,1)S(1)} %collective-permute-done.1.refs_2_, bf16[512,256]{1,0:T(8,128)(2,1)S(1)} %collective-permute-done.2.refs_3_, ...), custom_call_target="tpu_custom_call" | custom-call | tf_op jit(solution)/shard_map/pallas_call | solution.py:544
  19.0 1.3 %collective-permute-start.6 = (f32[8,128]{1,0:T(8,128)S(1)}, f32[8,128]{1,0:T(8,128)S(1)}, u32[]{:S(2)}, u32[]{:S(2)}) collective-permute-start(f32[8,128]{1,0:T(8,128)S(1)} %shard_map.44), channel_id=1, source_target_pairs={{0,26},{1,27},{2,24},{3,25},{4,30},{5,31},{6,28},{7,29},{8,18},{9,... | collective-permute-start | bytes 12296 | tf_op jit(solution)/shard_map/ppermute | solution.py:559
  20.2 2.3 %shard_map.45 = (bf16[512,2048]{1,0:T(8,128)(2,1)S(1)}, bf16[2048,256]{1,0:T(8,128)(2,1)S(1)}, bf16[512,256]{1,0:T(8,128)(2,1)S(1)}) custom-call(s32[16,16]{1,0:T(8,128)S(1)} %copy-done.1, bf16[512,256]{1,0:T(8,128)(2,1)S(1)} %shard_map.41.refs_0_, bf16[512,256]{1,0:T(8,128)(2,1)S(1)} %collective-permute-done.refs_1_, ...), custom_call_target="tpu_custom_call" | custom-call | tf_op jit(solution)/shard_map/pallas_call | solution.py:544
  22.5 1.9 %collective-permute-done.6 = f32[8,128]{1,0:T(8,128)S(1)} collective-permute-done((f32[8,128]{1,0:T(8,128)S(1)}, f32[8,128]{1,0:T(8,128)S(1)}, u32[]{:S(2)}, u32[]{:S(2)}) %collective-permute-start.6) | collective-permute-done | bytes 4128 | tf_op jit(solution)/shard_map/ppermute | solution.py:559
  24.5 0.1 collective-permute-done.4.refs_0_
  24.5 1.2 %collective-permute-done.7.refs_1_ = bf16[512,256]{1,0:T(8,128)(2,1)S(1)} collective-permute-done((bf16[512,256]{1,0:T(8,128)(2,1)S(1)}, bf16[512,256]{1,0:T(8,128)(2,1)S(1)}, u32[]{:S(2)}, u32[]{:S(2)}) %collective-permute-start.7) | collective-permute-done | bytes 262176 | tf_op jit(solution)/shard_map/ppermute | solution.py:567
  25.7 0.0 collective-permute-done.8.refs_2_
  25.7 0.0 collective-permute-start.11
  25.7 0.5 %collective-permute-start.10 = (bf16[512,256]{1,0:T(8,128)(2,1)S(1)}, bf16[512,256]{1,0:T(8,128)(2,1)S(1)}, u32[]{:S(2)}, u32[]{:S(2)}) collective-permute-start(bf16[512,256]{1,0:T(8,128)(2,1)S(1)} %collective-permute-done.7.refs_1_), channel_id=1, source_target_pairs={{0,1},{1,0},{2,3},{3,2},{4,5},{5,4},{6,7},{7,6},{8,9},{9,8},{10,11... | collective-permute-start | bytes 786440 | tf_op jit(solution)/shard_map/ppermute | solution.py:556
  26.3 0.0 collective-permute-start.9
  26.3 2.5 %collective-permute-start.12 = (f32[8,128]{1,0:T(8,128)S(1)}, f32[8,128]{1,0:T(8,128)S(1)}, u32[]{:S(2)}, u32[]{:S(2)}) collective-permute-start(f32[8,128]{1,0:T(8,128)S(1)} %add.6), channel_id=1, source_target_pairs={{0,4},{1,5},{2,6},{3,7},{4,0},{5,1},{6,2},{7,3},{8,12},{9,13},{10,... | collective-permute-start | bytes 12296 | tf_op jit(solution)/shard_map/ppermute | solution.py:559
  28.8 0.0 collective-permute-done.11.refs_5_
  28.8 0.0 collective-permute-done.10.refs_4_
  28.8 0.0 collective-permute-done.9.refs_3_
  28.8 2.7 %shard_map.46 = (bf16[512,2048]{1,0:T(8,128)(2,1)S(1)}, bf16[2048,256]{1,0:T(8,128)(2,1)S(1)}, bf16[512,256]{1,0:T(8,128)(2,1)}) custom-call(bf16[512,256]{1,0:T(8,128)(2,1)S(1)} %collective-permute-done.4.refs_0_, bf16[512,256]{1,0:T(8,128)(2,1)S(1)} %collective-permute-done.7.refs_1_, ...), custom_call_target="tpu_custom_call", output_to_operand_aliasing={{0}: (7, {}), {1}: (8, {})} | custom-call | tf_op jit(solution)/shard_map/pallas_call | solution.py:544
  31.5 0.0 collective-permute-done.12
  31.5 0.6 %add_reduce_fusion = f32[2]{0:T(128)} fusion(f32[8,128]{1,0:T(8,128)S(1)} %collective-permute-done.12, f32[8,128]{1,0:T(8,128)S(1)} %add.6), kind=kLoop, calls=%fused_computation | loop fusion | flops 510 | bytes 2056 | tf_op jit(solution)/shard_map/reduce_sum | solution.py:598
  (2 shorter events, 0.0 us)
Async XLA Ops:
  0.6 8.9 %collective-permute-start = (bf16[512,256]{1,0:T(8,128)(2,1)}, bf16[512,256]{1,0:T(8,128)(2,1)S(1)}, u32[]{:S(2)}, u32[]{:S(2)}) collective-permute-start(bf16[512,256]{1,0:T(8,128)(2,1)} %source.1), channel_id=1, source_target_pairs={{0,2},{1,0},{2,4},{3,1},{4,6},{5,3},{6,7},{7,5},{8,10},{9,8},{10,1... | collective-permute-start | bytes 786440 | tf_op jit(solution)/shard_map/ppermute | solution.py:561
  3.7 6.6 %collective-permute-start.1 = (bf16[512,256]{1,0:T(8,128)(2,1)}, bf16[512,256]{1,0:T(8,128)(2,1)S(1)}, u32[]{:S(2)}, u32[]{:S(2)}) collective-permute-start(bf16[512,256]{1,0:T(8,128)(2,1)} %source.1), channel_id=1, source_target_pairs={{0,1},{1,3},{2,0},{3,5},{4,2},{5,7},{6,4},{7,6},{8,9},{9,11},{10,8... | collective-permute-start | bytes 786440 | tf_op jit(solution)/shard_map/ppermute | solution.py:561
  3.7 8.0 %collective-permute-start.2 = (bf16[512,256]{1,0:T(8,128)(2,1)}, bf16[512,256]{1,0:T(8,128)(2,1)S(1)}, u32[]{:S(2)}, u32[]{:S(2)}) collective-permute-start(bf16[512,256]{1,0:T(8,128)(2,1)} %source.1), channel_id=1, source_target_pairs={{0,8},{1,9},{2,10},{3,11},{4,12},{5,13},{6,14},{7,15},{8,0},{9,1},... | collective-permute-start | bytes 786440 | tf_op jit(solution)/shard_map/ppermute | solution.py:561
  5.2 7.9 %collective-permute-start.3 = (bf16[512,256]{1,0:T(8,128)(2,1)}, bf16[512,256]{1,0:T(8,128)(2,1)S(1)}, u32[]{:S(2)}, u32[]{:S(2)}) collective-permute-start(bf16[512,256]{1,0:T(8,128)(2,1)} %source.1), channel_id=1, source_target_pairs={{0,16},{1,17},{2,18},{3,19},{4,20},{5,21},{6,22},{7,23},{8,24},{9,... | collective-permute-start | bytes 786440 | tf_op jit(solution)/shard_map/ppermute | solution.py:561
  6.7 1.0 %copy-start = (bf16[512,256]{1,0:T(8,128)(2,1)S(1)}, bf16[512,256]{1,0:T(8,128)(2,1)}, u32[]{:S(2)}) copy-start(bf16[512,256]{1,0:T(8,128)(2,1)} %source.1) | copy-start | bytes 786436
  7.7 9.8 %copy-start.1 = (s32[16,16]{1,0:T(8,128)S(1)}, s32[16,16]{1,0:T(8,128)}, u32[]{:S(2)}) copy-start(s32[16,16]{1,0:T(8,128)} %pattern.3) | copy-start | bytes 3076
  13.2 4.3 %collective-permute-start.5 = (bf16[5,512,256]{2,1,0:T(8,128)(2,1)S(1)}, bf16[5,512,256]{2,1,0:T(8,128)(2,1)S(1)}, u32[]{:S(2)}, u32[]{:S(2)}) collective-permute-start(bf16[5,512,256]{2,1,0:T(8,128)(2,1)S(1)} %shard_map.43), channel_id=1, source_target_pairs={{0,1},{1,0},{2,3},{3,2},{4,5},{5,4},{6,7},{7,6},{8,9},{9,8},{10,11... | collective-permute-start | bytes 3932168 | tf_op jit(solution)/shard_map/ppermute | solution.py:556
  13.3 11.2 %collective-permute-start.4 = (bf16[512,256]{1,0:T(8,128)(2,1)S(1)}, bf16[512,256]{1,0:T(8,128)(2,1)S(1)}, u32[]{:S(2)}, u32[]{:S(2)}) collective-permute-start(bf16[512,256]{1,0:T(8,128)(2,1)S(1)} %get-tuple-element.37), channel_id=1, source_target_pairs={{1,7},{4,0},{5,1},{6,4},{7,23},{10,15},{12,20},{15,3},{16,5},{18,6... | collective-permute-start | bytes 786440 | tf_op jit(solution)/shard_map/ppermute | solution.py:567
  14.9 10.8 %collective-permute-start.7 = (bf16[512,256]{1,0:T(8,128)(2,1)S(1)}, bf16[512,256]{1,0:T(8,128)(2,1)S(1)}, u32[]{:S(2)}, u32[]{:S(2)}) collective-permute-start(bf16[512,256]{1,0:T(8,128)(2,1)S(1)} %get-tuple-element.48), channel_id=1, source_target_pairs={{0,7},{2,0},{5,15},{6,12},{7,14},{9,4},{12,2},{14,23},{15,22},{19,... | collective-permute-start | bytes 786440 | tf_op jit(solution)/shard_map/ppermute | solution.py:567
  17.5 8.2 %collective-permute-start.8 = (bf16[512,256]{1,0:T(8,128)(2,1)S(1)}, bf16[512,256]{1,0:T(8,128)(2,1)S(1)}, u32[]{:S(2)}, u32[]{:S(2)}) collective-permute-start(bf16[512,256]{1,0:T(8,128)(2,1)S(1)} %get-tuple-element.51), channel_id=1, source_target_pairs={{3,13},{4,12},{6,22},{7,3},{10,15},{11,2},{12,11},{13,20},{15,7},{... | collective-permute-start | bytes 786440 | tf_op jit(solution)/shard_map/ppermute | solution.py:567
  19.0 5.5 %collective-permute-start.6 = (f32[8,128]{1,0:T(8,128)S(1)}, f32[8,128]{1,0:T(8,128)S(1)}, u32[]{:S(2)}, u32[]{:S(2)}) collective-permute-start(f32[8,128]{1,0:T(8,128)S(1)} %shard_map.44), channel_id=1, source_target_pairs={{0,26},{1,27},{2,24},{3,25},{4,30},{5,31},{6,28},{7,29},{8,18},{9,... | collective-permute-start | bytes 12296 | tf_op jit(solution)/shard_map/ppermute | solution.py:559
  25.7 3.1 %collective-permute-start.11 = (bf16[512,256]{1,0:T(8,128)(2,1)S(1)}, bf16[512,256]{1,0:T(8,128)(2,1)S(1)}, u32[]{:S(2)}, u32[]{:S(2)}) collective-permute-start(bf16[512,256]{1,0:T(8,128)(2,1)S(1)} %collective-permute-done.8.refs_2_), channel_id=1, source_target_pairs={{0,1},{1,0},{2,3},{3,2},{4,5},{5,4},{6,7},{7,6},{8,9},{9,8},{10,11... | collective-permute-start | bytes 786440 | tf_op jit(solution)/shard_map/ppermute | solution.py:556
  25.7 3.1 %collective-permute-start.10 = (bf16[512,256]{1,0:T(8,128)(2,1)S(1)}, bf16[512,256]{1,0:T(8,128)(2,1)S(1)}, u32[]{:S(2)}, u32[]{:S(2)}) collective-permute-start(bf16[512,256]{1,0:T(8,128)(2,1)S(1)} %collective-permute-done.7.refs_1_), channel_id=1, source_target_pairs={{0,1},{1,0},{2,3},{3,2},{4,5},{5,4},{6,7},{7,6},{8,9},{9,8},{10,11... | collective-permute-start | bytes 786440 | tf_op jit(solution)/shard_map/ppermute | solution.py:556
  26.3 2.5 %collective-permute-start.9 = (bf16[512,256]{1,0:T(8,128)(2,1)S(1)}, bf16[512,256]{1,0:T(8,128)(2,1)S(1)}, u32[]{:S(2)}, u32[]{:S(2)}) collective-permute-start(bf16[512,256]{1,0:T(8,128)(2,1)S(1)} %collective-permute-done.4.refs_0_), channel_id=1, source_target_pairs={{0,1},{1,0},{2,3},{3,2},{4,5},{5,4},{6,7},{7,6},{8,9},{9,8},{10,11... | collective-permute-start | bytes 786440 | tf_op jit(solution)/shard_map/ppermute | solution.py:556
  26.3 5.2 %collective-permute-start.12 = (f32[8,128]{1,0:T(8,128)S(1)}, f32[8,128]{1,0:T(8,128)S(1)}, u32[]{:S(2)}, u32[]{:S(2)}) collective-permute-start(f32[8,128]{1,0:T(8,128)S(1)} %add.6), channel_id=1, source_target_pairs={{0,4},{1,5},{2,6},{3,7},{4,0},{5,1},{6,2},{7,3},{8,12},{9,13},{10,... | collective-permute-start | bytes 12296 | tf_op jit(solution)/shard_map/ppermute | solution.py:559

commit v6 on v4

--- a/solution.py
+++ b/solution.py
@@ -151,8 +151,11 @@
 USES = 8
 FIRST = 5
 SECOND = 3
-SEEN = ((), (0,), (1, 3), (2,))
-
+HEARD = (
+    ((2, 0), (0, 3), (0, 1), (1, 3), (0, 2), (3, 0), (3, 2), (1, 0), (0, 0), (2, 3), (2, 1), (3, 3), (3, 1), (1, 1), (1, 2), (2, 2)),
+    ((3, 0), (3, 2), (2, 2), (1, 3), (0, 0), (1, 0), (0, 3), (1, 1), (2, 1), (1, 2), (0, 1), (0, 2), (3, 3), (2, 0), (2, 3), (3, 1)),
+)
+LAST_HEARD = ((0, 1), (0, 0), (0, 3), (0, 2), (3, 0), (1, 2), (1, 1), (3, 3), (2, 1), (2, 0), (2, 3), (2, 2), (1, 0), (3, 2), (3, 1), (1, 3))
 MESSAGES = (
     (0, (0, 0), 0, (0, 0, 0), (0, 3, 1)),
     (0, (0, 2), 0, (0, 1, 0), (0, 0, 0)),
@@ -256,6 +259,22 @@
     return pairs + [(ends[row_of[j] - 1], starts[j - 1]) for j in range(1, size + 1)]
 
 
+def trace_pairs():
+    chips = [(r, z) for r in range(4) for z in range(4)]
+
+    def near(c):
+        return {d for d in chips if abs(c[1] - d[1]) + bin(c[0] ^ d[0]).count("1") <= 1}
+
+    known = {c: near(c) | near(HEARD[0][i]) | near(HEARD[1][i]) for i, c in enumerate(chips)}
+    for i, c in enumerate(chips):
+        assert known[c] | known[LAST_HEARD[i]] >= {d for d in chips if d[0] <= d[1]}
+
+    def on_cores(sources):
+        return [(number((*sources[i], k)), number((*c, k))) for i, c in enumerate(chips) for k in range(2)]
+
+    return [on_cores(sources) for sources in HEARD], on_cores(LAST_HEARD)
+
+
 def schedule():
     devices = [(r, z, k) for r in range(4) for z in range(4) for k in range(2)]
     first = first_round(devices)
@@ -275,9 +294,8 @@
     uses = [[{} for _ in range(USES)] for _ in range(2)]
     for d in devices:
         r, z, k = d
-        added = {(r, z), (r ^ 1, z), (r ^ 2, z)} | {(r, j) for j in SEEN[z]}
         for s, (tile, half) in enumerate(held[d]):
-            if tile in added and half == k and (s == 0 or tile != (r, z)):
+            if half == k and (s == 0 or tile != (r, z)):
                 adds[s].add(number(d))
         for u, tile in enumerate(wanted(r, z)):
             for n, shards in enumerate((held, later)):
@@ -555,8 +573,8 @@
     def share(value):
         return lax.ppermute(value, axes, [(d, d ^ 1) for d in range(n_devices)])
 
-    def part_from(parts, row_bits, col_bits):
-        return lax.ppermute(parts, axes, [(d, d ^ (row_bits * n_col + col_bits)) for d in range(n_devices)])
+    def merge(parts, others):
+        return jnp.where(parts != 0, parts, others)
 
     came = [lax.ppermute(density, axes, pairs) for pairs in first]
     came[0], own = lax.optimization_barrier((came[0], call(copy_kernel, shard, 0, [density])))
@@ -573,13 +591,13 @@
         [pattern] + held + [packed],
     )
     packed, parts = lax.optimization_barrier((packed, parts))
-    received = part_from(parts, 3, 2)
+    early, late = trace_pairs()
+    received = [lax.ppermute(parts, axes, pairs) for pairs in early]
     left, right, keeps = call(
         functools.partial(panels_kernel, uses), panels + [shard], 1, [pattern] + held + [packed], [raw], [VMEM] * 3
     )
-    left, parts = lax.optimization_barrier((left, parts + received))
-    received = part_from(parts, 0, 4)
-    left, parts = lax.optimization_barrier((left, parts))
+    left, parts = lax.optimization_barrier((left, merge(parts, merge(*received))))
+    received = lax.ppermute(parts, axes, late)
     shared = []
     for i in range(SECOND):
         later[i], left = lax.optimization_barrier((later[i], left))
@@ -595,7 +613,7 @@
         {len(inputs) - 2: 0, len(inputs) - 1: 1},
     )[2]
     square, received = lax.optimization_barrier((square, received))
-    traces = jnp.sum(parts[:2] + received[:2], axis=1)
+    traces = jnp.sum(merge(parts[:2], received[:2]), axis=1)
     return (square, traces)
 
 

time: 32.2 us -> 32.6 us (1.012)
  waiting for transfers between devices: 8.96 us -> 6.17 us
  starting transfers between devices: 14.2 us -> 16.9 us
  Pallas kernels: 6.61 us -> 7.05 us
    ppermute x2 -> x3, starting transfers between devices: 3.22 us -> 5.8 us  [the longest x2 3.6 us: chip_grid(): received = [lax.ppermute(parts, axes, pairs) for pairs in early]]
    ppermute x2 -> x3, waiting for transfers between devices: 1.99 us -> 0.28 us  [the longest x2 0.28 us: chip_grid(): received = [lax.ppermute(parts, axes, pairs) for pairs in early]]
    ppermute x3, waiting for transfers between devices: 1.64 us -> 0.55 us  [chip_grid(): lax.ppermute(value, axes, pairs)]
    pallas_call x6, Pallas kernels: 6.61 us -> 7.05 us  [call(): pl.pallas_call(kernel, out_shape=out_shape, in_specs=[SMEM] * smem + [VME...]
  transfers between devices with their start and end apart: 13 -> 14, of which waited for: 7 -> 6; matrix products, arithmetic and copies ran while one was open for 0% -> 0% of each run, Pallas kernels for 20% -> 21%
where the time goes in v6:
time: 32.6 us; the launch traced here: 32.4 us
  starting transfers between devices  16.9 us (52%)
  Pallas kernels  7.05 us (22%)
  waiting for transfers between devices  6.17 us (19%)
  local copies, waits for them, and re-layouts  0.99 us (3%)
  between operations  0.73 us (2%)
  other arithmetic  0.63 us (2%)
    pallas_call x6, Pallas kernels, call(): pl.pallas_call(kernel, out_shape=out_shape, in_specs=[SMEM] * smem + [VME...  7.05 us
    ppermute x4, starting transfers between devices, chip_grid(): came = [lax.ppermute(density, axes, pairs) for pairs in first]  6.05 us
    ppermute x4, waiting for transfers between devices, chip_grid(): came = [lax.ppermute(density, axes, pairs) for pairs in first]  5.32 us
    ppermute x3, starting transfers between devices, chip_grid(): lax.ppermute(value, axes, pairs)  4.3 us
    ppermute x2, starting transfers between devices, chip_grid(): received = [lax.ppermute(parts, axes, pairs) for pairs in early]  3.6 us
    ppermute x1, starting transfers between devices, chip_grid(): received = lax.ppermute(parts, axes, late)  2.2 us
    unnamed x4, local copies, waits for them, and re-layouts  0.99 us
    ppermute x4, starting transfers between devices, share(): return lax.ppermute(value, axes, [(d, d ^ 1) for d in range(n_devices)])  0.71 us
  transfers between devices with their start and end apart: 14, of which 6 were waited for; matrix products, arithmetic and copies ran while one was open for 0% of the time, Pallas kernels for 21%

profile of v6, /device:TPU:0, one launch (start us, length us, event | category | flops | bytes accessed | tf_op | source)
XLA Modules:
  0.0 32.4 jit_solution(2659001635069359251)
XLA Ops:
  0.6 3.0 %collective-permute-start = (bf16[512,256]{1,0:T(8,128)(2,1)}, bf16[512,256]{1,0:T(8,128)(2,1)S(1)}, u32[]{:S(2)}, u32[]{:S(2)}) collective-permute-start(bf16[512,256]{1,0:T(8,128)(2,1)} %source.1), channel_id=1, source_target_pairs={{0,2},{1,0},{2,4},{3,1},{4,6},{5,3},{6,7},{7,5},{8,10},{9,8},{10,1... | collective-permute-start | bytes 786440 | tf_op jit(solution)/shard_map/ppermute | solution.py:579
  3.7 0.0 collective-permute-start.1
  3.7 1.5 %collective-permute-start.2 = (bf16[512,256]{1,0:T(8,128)(2,1)}, bf16[512,256]{1,0:T(8,128)(2,1)S(1)}, u32[]{:S(2)}, u32[]{:S(2)}) collective-permute-start(bf16[512,256]{1,0:T(8,128)(2,1)} %source.1), channel_id=1, source_target_pairs={{0,8},{1,9},{2,10},{3,11},{4,12},{5,13},{6,14},{7,15},{8,0},{9,1},... | collective-permute-start | bytes 786440 | tf_op jit(solution)/shard_map/ppermute | solution.py:579
  5.2 1.5 %collective-permute-start.3 = (bf16[512,256]{1,0:T(8,128)(2,1)}, bf16[512,256]{1,0:T(8,128)(2,1)S(1)}, u32[]{:S(2)}, u32[]{:S(2)}) collective-permute-start(bf16[512,256]{1,0:T(8,128)(2,1)} %source.1), channel_id=1, source_target_pairs={{0,16},{1,17},{2,18},{3,19},{4,20},{5,21},{6,22},{7,23},{8,24},{9,... | collective-permute-start | bytes 786440 | tf_op jit(solution)/shard_map/ppermute | solution.py:579
  6.7 0.0 copy-start
  6.7 1.0 %copy-done = bf16[512,256]{1,0:T(8,128)(2,1)S(1)} copy-done((bf16[512,256]{1,0:T(8,128)(2,1)S(1)}, bf16[512,256]{1,0:T(8,128)(2,1)}, u32[]{:S(2)}) %copy-start) | copy-done | bytes 262168
  7.7 0.0 copy-start.1
  7.7 1.9 %collective-permute-done.refs_1_ = bf16[512,256]{1,0:T(8,128)(2,1)S(1)} collective-permute-done((bf16[512,256]{1,0:T(8,128)(2,1)}, bf16[512,256]{1,0:T(8,128)(2,1)S(1)}, u32[]{:S(2)}, u32[]{:S(2)}) %collective-permute-start) | collective-permute-done | bytes 262176 | tf_op jit(solution)/shard_map/ppermute | solution.py:579
  9.6 0.7 %collective-permute-done.1.refs_2_ = bf16[512,256]{1,0:T(8,128)(2,1)S(1)} collective-permute-done((bf16[512,256]{1,0:T(8,128)(2,1)}, bf16[512,256]{1,0:T(8,128)(2,1)S(1)}, u32[]{:S(2)}, u32[]{:S(2)}) %collective-permute-start.1) | collective-permute-done | bytes 262176 | tf_op jit(solution)/shard_map/ppermute | solution.py:579
  10.3 1.4 %collective-permute-done.2.refs_3_ = bf16[512,256]{1,0:T(8,128)(2,1)S(1)} collective-permute-done((bf16[512,256]{1,0:T(8,128)(2,1)}, bf16[512,256]{1,0:T(8,128)(2,1)S(1)}, u32[]{:S(2)}, u32[]{:S(2)}) %collective-permute-start.2) | collective-permute-done | bytes 262176 | tf_op jit(solution)/shard_map/ppermute | solution.py:579
  11.7 1.4 %collective-permute-done.3.refs_4_ = bf16[512,256]{1,0:T(8,128)(2,1)S(1)} collective-permute-done((bf16[512,256]{1,0:T(8,128)(2,1)}, bf16[512,256]{1,0:T(8,128)(2,1)S(1)}, u32[]{:S(2)}, u32[]{:S(2)}) %collective-permute-start.3) | collective-permute-done | bytes 262176 | tf_op jit(solution)/shard_map/ppermute | solution.py:579
  13.0 0.1 shard_map.42
  13.1 0.1 shard_map.43
  13.2 0.1 collective-permute-start.5
  13.3 2.9 %collective-permute-start.4 = (bf16[512,256]{1,0:T(8,128)(2,1)S(1)}, bf16[512,256]{1,0:T(8,128)(2,1)S(1)}, u32[]{:S(2)}, u32[]{:S(2)}) collective-permute-start(bf16[512,256]{1,0:T(8,128)(2,1)S(1)} %get-tuple-element.36), channel_id=1, source_target_pairs={{0,7},{2,0},{4,13},{5,1},{6,4},{7,23},{9,5},{12,14},{13,2},{14,20}... | collective-permute-start | bytes 786440 | tf_op jit(solution)/shard_map/ppermute | solution.py:585
  16.2 0.0 collective-permute-start.8
  16.2 1.4 %collective-permute-start.9 = (bf16[512,256]{1,0:T(8,128)(2,1)S(1)}, bf16[512,256]{1,0:T(8,128)(2,1)S(1)}, u32[]{:S(2)}, u32[]{:S(2)}) collective-permute-start(bf16[512,256]{1,0:T(8,128)(2,1)S(1)} %get-tuple-element.50), channel_id=1, source_target_pairs={{3,13},{4,12},{6,22},{7,2},{10,14},{11,3},{12,11},{14,6},{15,7},{2... | collective-permute-start | bytes 786440 | tf_op jit(solution)/shard_map/ppermute | solution.py:585
  17.6 0.0 collective-permute-done.5.refs_5_
  17.6 0.0 copy-done.1
  17.6 1.9 %shard_map.44 = f32[8,128]{1,0:T(8,128)S(1)} custom-call(s32[16,16]{1,0:T(8,128)S(1)} %copy-done.1, bf16[512,256]{1,0:T(8,128)(2,1)S(1)} %shard_map.41.refs_0_, bf16[512,256]{1,0:T(8,128)(2,1)S(1)} %collective-permute-done.refs_1_, bf16[512,256]{1,0:T(8,128)(2,1)S(1)} %collective-permute-done.1.refs_2_, bf16[512,256]{1,0:T(8,128)(2,1)S(1)} %collective-permute-done.2.refs_3_, ...), custom_call_target="tpu_custom_call" | custom-call | tf_op jit(solution)/shard_map/pallas_call | solution.py:562
  19.5 0.1 collective-permute-start.6
  19.6 3.5 %collective-permute-start.7 = (f32[8,128]{1,0:T(8,128)S(1)}, f32[8,128]{1,0:T(8,128)S(1)}, u32[]{:S(2)}, u32[]{:S(2)}) collective-permute-start(f32[8,128]{1,0:T(8,128)S(1)} %shard_map.44), channel_id=1, source_target_pairs={{24,0},{25,1},{28,2},{29,3},{20,4},{21,5},{14,6},{15,7},{0,8},{1,9... | collective-permute-start | bytes 12296 | tf_op jit(solution)/shard_map/ppermute | solution.py:595
  23.1 2.3 %shard_map.45 = (bf16[512,2048]{1,0:T(8,128)(2,1)S(1)}, bf16[2048,256]{1,0:T(8,128)(2,1)S(1)}, bf16[512,256]{1,0:T(8,128)(2,1)S(1)}) custom-call(s32[16,16]{1,0:T(8,128)S(1)} %copy-done.1, bf16[512,256]{1,0:T(8,128)(2,1)S(1)} %shard_map.41.refs_0_, bf16[512,256]{1,0:T(8,128)(2,1)S(1)} %collective-permute-done.refs_1_, ...), custom_call_target="tpu_custom_call" | custom-call | tf_op jit(solution)/shard_map/pallas_call | solution.py:562
  25.4 0.0 collective-permute-done.6
  25.4 0.3 collective-permute-done.7
  25.7 0.0 collective-permute-done.4.refs_0_
  25.7 0.5 %collective-permute-done.8.refs_1_ = bf16[512,256]{1,0:T(8,128)(2,1)S(1)} collective-permute-done((bf16[512,256]{1,0:T(8,128)(2,1)S(1)}, bf16[512,256]{1,0:T(8,128)(2,1)S(1)}, u32[]{:S(2)}, u32[]{:S(2)}) %collective-permute-start.8) | collective-permute-done | bytes 262176 | tf_op jit(solution)/shard_map/ppermute | solution.py:585
  26.3 0.0 collective-permute-done.9.refs_2_
  26.3 0.1 collective-permute-start.12
  26.4 0.4 %collective-permute-start.11 = (bf16[512,256]{1,0:T(8,128)(2,1)S(1)}, bf16[512,256]{1,0:T(8,128)(2,1)S(1)}, u32[]{:S(2)}, u32[]{:S(2)}) collective-permute-start(bf16[512,256]{1,0:T(8,128)(2,1)S(1)} %collective-permute-done.8.refs_1_), channel_id=1, source_target_pairs={{0,1},{1,0},{2,3},{3,2},{4,5},{5,4},{6,7},{7,6},{8,9},{9,8},{10,11... | collective-permute-start | bytes 786440 | tf_op jit(solution)/shard_map/ppermute | solution.py:574
  26.8 0.1 collective-permute-start.10
  26.9 2.2 %collective-permute-start.13 = (f32[8,128]{1,0:T(8,128)S(1)}, f32[8,128]{1,0:T(8,128)S(1)}, u32[]{:S(2)}, u32[]{:S(2)}) collective-permute-start(f32[8,128]{1,0:T(8,128)S(1)} %compare_select_fusion.1), channel_id=1, source_target_pairs={{2,0},{3,1},{0,2},{1,3},{6,4},{7,5},{4,6},{5,7},{24,8},{25,9},{12,... | collective-permute-start | bytes 12296 | tf_op jit(solution)/shard_map/ppermute | solution.py:600
  29.1 0.0 collective-permute-done.12.refs_5_
  29.1 0.0 collective-permute-done.11.refs_4_
  29.1 0.0 collective-permute-done.10.refs_3_
  29.1 2.7 %shard_map.46 = (bf16[512,2048]{1,0:T(8,128)(2,1)S(1)}, bf16[2048,256]{1,0:T(8,128)(2,1)S(1)}, bf16[512,256]{1,0:T(8,128)(2,1)}) custom-call(bf16[512,256]{1,0:T(8,128)(2,1)S(1)} %collective-permute-done.4.refs_0_, bf16[512,256]{1,0:T(8,128)(2,1)S(1)} %collective-permute-done.8.refs_1_, ...), custom_call_target="tpu_custom_call", output_to_operand_aliasing={{0}: (7, {}), {1}: (8, {})} | custom-call | tf_op jit(solution)/shard_map/pallas_call | solution.py:562
  31.8 0.0 collective-permute-done.13
  31.8 0.6 %fusion = f32[2]{0:T(128)} fusion(f32[8,128]{1,0:T(8,128)S(1)} %collective-permute-done.13, f32[8,128]{1,0:T(8,128)S(1)} %compare_select_fusion.1), kind=kLoop, calls=%fused_computation.3 | loop fusion | flops 766 | bytes 2056 | tf_op jit(solution)/shard_map/reduce_sum | solution.py:616
  (2 shorter events, 0.0 us)
Async XLA Ops:
  0.6 8.9 %collective-permute-start = (bf16[512,256]{1,0:T(8,128)(2,1)}, bf16[512,256]{1,0:T(8,128)(2,1)S(1)}, u32[]{:S(2)}, u32[]{:S(2)}) collective-permute-start(bf16[512,256]{1,0:T(8,128)(2,1)} %source.1), channel_id=1, source_target_pairs={{0,2},{1,0},{2,4},{3,1},{4,6},{5,3},{6,7},{7,5},{8,10},{9,8},{10,1... | collective-permute-start | bytes 786440 | tf_op jit(solution)/shard_map/ppermute | solution.py:579
  3.7 6.6 %collective-permute-start.1 = (bf16[512,256]{1,0:T(8,128)(2,1)}, bf16[512,256]{1,0:T(8,128)(2,1)S(1)}, u32[]{:S(2)}, u32[]{:S(2)}) collective-permute-start(bf16[512,256]{1,0:T(8,128)(2,1)} %source.1), channel_id=1, source_target_pairs={{0,1},{1,3},{2,0},{3,5},{4,2},{5,7},{6,4},{7,6},{8,9},{9,11},{10,8... | collective-permute-start | bytes 786440 | tf_op jit(solution)/shard_map/ppermute | solution.py:579
  3.7 8.0 %collective-permute-start.2 = (bf16[512,256]{1,0:T(8,128)(2,1)}, bf16[512,256]{1,0:T(8,128)(2,1)S(1)}, u32[]{:S(2)}, u32[]{:S(2)}) collective-permute-start(bf16[512,256]{1,0:T(8,128)(2,1)} %source.1), channel_id=1, source_target_pairs={{0,8},{1,9},{2,10},{3,11},{4,12},{5,13},{6,14},{7,15},{8,0},{9,1},... | collective-permute-start | bytes 786440 | tf_op jit(solution)/shard_map/ppermute | solution.py:579
  5.2 7.9 %collective-permute-start.3 = (bf16[512,256]{1,0:T(8,128)(2,1)}, bf16[512,256]{1,0:T(8,128)(2,1)S(1)}, u32[]{:S(2)}, u32[]{:S(2)}) collective-permute-start(bf16[512,256]{1,0:T(8,128)(2,1)} %source.1), channel_id=1, source_target_pairs={{0,16},{1,17},{2,18},{3,19},{4,20},{5,21},{6,22},{7,23},{8,24},{9,... | collective-permute-start | bytes 786440 | tf_op jit(solution)/shard_map/ppermute | solution.py:579
  6.7 1.0 %copy-start = (bf16[512,256]{1,0:T(8,128)(2,1)S(1)}, bf16[512,256]{1,0:T(8,128)(2,1)}, u32[]{:S(2)}) copy-start(bf16[512,256]{1,0:T(8,128)(2,1)} %source.1) | copy-start | bytes 786436
  7.7 9.9 %copy-start.1 = (s32[16,16]{1,0:T(8,128)S(1)}, s32[16,16]{1,0:T(8,128)}, u32[]{:S(2)}) copy-start(s32[16,16]{1,0:T(8,128)} %pattern.3) | copy-start | bytes 3076
  13.2 4.4 %collective-permute-start.5 = (bf16[5,512,256]{2,1,0:T(8,128)(2,1)S(1)}, bf16[5,512,256]{2,1,0:T(8,128)(2,1)S(1)}, u32[]{:S(2)}, u32[]{:S(2)}) collective-permute-start(bf16[5,512,256]{2,1,0:T(8,128)(2,1)S(1)} %shard_map.43), channel_id=1, source_target_pairs={{0,1},{1,0},{2,3},{3,2},{4,5},{5,4},{6,7},{7,6},{8,9},{9,8},{10,11... | collective-permute-start | bytes 3932168 | tf_op jit(solution)/shard_map/ppermute | solution.py:574
  13.3 12.4 %collective-permute-start.4 = (bf16[512,256]{1,0:T(8,128)(2,1)S(1)}, bf16[512,256]{1,0:T(8,128)(2,1)S(1)}, u32[]{:S(2)}, u32[]{:S(2)}) collective-permute-start(bf16[512,256]{1,0:T(8,128)(2,1)S(1)} %get-tuple-element.36), channel_id=1, source_target_pairs={{0,7},{2,0},{4,13},{5,1},{6,4},{7,23},{9,5},{12,14},{13,2},{14,20}... | collective-permute-start | bytes 786440 | tf_op jit(solution)/shard_map/ppermute | solution.py:585
  16.2 10.0 %collective-permute-start.8 = (bf16[512,256]{1,0:T(8,128)(2,1)S(1)}, bf16[512,256]{1,0:T(8,128)(2,1)S(1)}, u32[]{:S(2)}, u32[]{:S(2)}) collective-permute-start(bf16[512,256]{1,0:T(8,128)(2,1)S(1)} %get-tuple-element.47), channel_id=1, source_target_pairs={{1,7},{4,0},{7,14},{11,15},{12,3},{14,22},{16,4},{18,6},{21,1},{22... | collective-permute-start | bytes 786440 | tf_op jit(solution)/shard_map/ppermute | solution.py:585
  16.2 10.0 %collective-permute-start.9 = (bf16[512,256]{1,0:T(8,128)(2,1)S(1)}, bf16[512,256]{1,0:T(8,128)(2,1)S(1)}, u32[]{:S(2)}, u32[]{:S(2)}) collective-permute-start(bf16[512,256]{1,0:T(8,128)(2,1)S(1)} %get-tuple-element.50), channel_id=1, source_target_pairs={{3,13},{4,12},{6,22},{7,2},{10,14},{11,3},{12,11},{14,6},{15,7},{2... | collective-permute-start | bytes 786440 | tf_op jit(solution)/shard_map/ppermute | solution.py:585
  19.5 5.9 %collective-permute-start.6 = (f32[8,128]{1,0:T(8,128)S(1)}, f32[8,128]{1,0:T(8,128)S(1)}, u32[]{:S(2)}, u32[]{:S(2)}) collective-permute-start(f32[8,128]{1,0:T(8,128)S(1)} %shard_map.44), channel_id=1, source_target_pairs={{16,0},{17,1},{6,2},{7,3},{2,4},{3,5},{14,6},{15,7},{4,8},{5,9},{2... | collective-permute-start | bytes 12296 | tf_op jit(solution)/shard_map/ppermute | solution.py:595
  19.6 6.1 %collective-permute-start.7 = (f32[8,128]{1,0:T(8,128)S(1)}, f32[8,128]{1,0:T(8,128)S(1)}, u32[]{:S(2)}, u32[]{:S(2)}) collective-permute-start(f32[8,128]{1,0:T(8,128)S(1)} %shard_map.44), channel_id=1, source_target_pairs={{24,0},{25,1},{28,2},{29,3},{20,4},{21,5},{14,6},{15,7},{0,8},{1,9... | collective-permute-start | bytes 12296 | tf_op jit(solution)/shard_map/ppermute | solution.py:595
  26.3 2.8 %collective-permute-start.12 = (bf16[512,256]{1,0:T(8,128)(2,1)S(1)}, bf16[512,256]{1,0:T(8,128)(2,1)S(1)}, u32[]{:S(2)}, u32[]{:S(2)}) collective-permute-start(bf16[512,256]{1,0:T(8,128)(2,1)S(1)} %collective-permute-done.9.refs_2_), channel_id=1, source_target_pairs={{0,1},{1,0},{2,3},{3,2},{4,5},{5,4},{6,7},{7,6},{8,9},{9,8},{10,11... | collective-permute-start | bytes 786440 | tf_op jit(solution)/shard_map/ppermute | solution.py:574
  26.4 2.7 %collective-permute-start.11 = (bf16[512,256]{1,0:T(8,128)(2,1)S(1)}, bf16[512,256]{1,0:T(8,128)(2,1)S(1)}, u32[]{:S(2)}, u32[]{:S(2)}) collective-permute-start(bf16[512,256]{1,0:T(8,128)(2,1)S(1)} %collective-permute-done.8.refs_1_), channel_id=1, source_target_pairs={{0,1},{1,0},{2,3},{3,2},{4,5},{5,4},{6,7},{7,6},{8,9},{9,8},{10,11... | collective-permute-start | bytes 786440 | tf_op jit(solution)/shard_map/ppermute | solution.py:574
  26.8 2.3 %collective-permute-start.10 = (bf16[512,256]{1,0:T(8,128)(2,1)S(1)}, bf16[512,256]{1,0:T(8,128)(2,1)S(1)}, u32[]{:S(2)}, u32[]{:S(2)}) collective-permute-start(bf16[512,256]{1,0:T(8,128)(2,1)S(1)} %collective-permute-done.4.refs_0_), channel_id=1, source_target_pairs={{0,1},{1,0},{2,3},{3,2},{4,5},{5,4},{6,7},{7,6},{8,9},{9,8},{10,11... | collective-permute-start | bytes 786440 | tf_op jit(solution)/shard_map/ppermute | solution.py:574
  26.9 4.9 %collective-permute-start.13 = (f32[8,128]{1,0:T(8,128)S(1)}, f32[8,128]{1,0:T(8,128)S(1)}, u32[]{:S(2)}, u32[]{:S(2)}) collective-permute-start(f32[8,128]{1,0:T(8,128)S(1)} %compare_select_fusion.1), channel_id=1, source_target_pairs={{2,0},{3,1},{0,2},{1,3},{6,4},{7,5},{4,6},{5,7},{24,8},{25,9},{12,... | collective-permute-start | bytes 12296 | tf_op jit(solution)/shard_map/ppermute | solution.py:600

commit v7 on v5

--- a/solution.py
+++ b/solution.py
@@ -154,50 +154,50 @@
 SEEN = ((), (0,), (1, 3), (2,))
 
 MESSAGES = (
+    (0, (0, 0), 0, (2, 0, 0), (0, 2, 0)),
     (0, (0, 0), 1, (0, 0, 1), (0, 3, 1)),
+    (0, (0, 1), 0, (2, 1, 0), (0, 3, 0)),
+    (0, (0, 1), 1, (1, 1, 1), (1, 3, 1)),
+    (0, (0, 2), 1, (2, 2, 1), (0, 0, 1)),
     (0, (0, 3), 0, (0, 2, 0), (0, 0, 0)),
-    (0, (0, 3), 1, (0, 2, 1), (0, 0, 1)),
-    (0, (2, 3), 0, (0, 3, 0), (0, 2, 0)),
-    (0, (0, 2), 1, (0, 3, 1), (2, 3, 1)),
-    (0, (0, 1), 0, (1, 1, 0), (1, 3, 1)),
-    (0, (1, 2), 0, (1, 2, 0), (2, 2, 0)),
-    (0, (1, 3), 1, (1, 3, 1), (0, 1, 1)),
-    (0, (0, 0), 0, (2, 0, 0), (0, 2, 1)),
-    (0, (0, 1), 0, (2, 1, 0), (0, 3, 0)),
-    (0, (0, 2), 0, (2, 2, 0), (2, 3, 0)),
-    (0, (0, 3), 0, (2, 3, 0), (0, 1, 0)),
-    (0, (1, 1), 1, (3, 1, 1), (1, 3, 0)),
-    (0, (2, 2), 0, (3, 2, 0), (1, 2, 0)),
-    (0, (2, 2), 1, (3, 2, 1), (1, 2, 1)),
-    (0, (1, 3), 1, (3, 3, 1), (1, 1, 0)),
+    (0, (0, 3), 0, (2, 3, 0), (3, 3, 1)),
+    (0, (1, 2), 0, (1, 3, 0), (2, 3, 0)),
+    (0, (1, 2), 0, (3, 2, 0), (0, 1, 0)),
+    (0, (1, 2), 1, (3, 2, 1), (2, 3, 1)),
+    (0, (1, 3), 0, (1, 2, 0), (0, 1, 1)),
+    (0, (2, 3), 0, (3, 3, 0), (1, 2, 0)),
+    (0, (2, 3), 1, (0, 3, 1), (1, 3, 0)),
+    (0, (2, 3), 1, (3, 3, 1), (1, 2, 1)),
     (1, (0, 0), 0, (0, 0, 0), (0, 3, 1)),
+    (1, (0, 0), 1, (1, 0, 1), (0, 2, 1)),
+    (1, (0, 1), 1, (2, 1, 1), (0, 3, 0)),
     (1, (0, 2), 0, (0, 1, 0), (0, 0, 0)),
-    (1, (0, 1), 1, (0, 2, 1), (1, 3, 1)),
-    (1, (2, 3), 0, (0, 3, 0), (1, 2, 0)),
-    (1, (2, 3), 1, (0, 3, 1), (1, 3, 0)),
-    (1, (0, 0), 1, (1, 0, 1), (0, 2, 0)),
-    (1, (1, 3), 0, (1, 2, 0), (0, 1, 0)),
-    (1, (1, 2), 0, (1, 3, 0), (2, 3, 1)),
-    (1, (1, 2), 1, (1, 3, 1), (2, 3, 0)),
-    (1, (0, 1), 1, (2, 1, 1), (0, 3, 0)),
-    (1, (0, 2), 1, (2, 2, 1), (0, 0, 1)),
-    (1, (0, 3), 0, (2, 3, 0), (3, 3, 0)),
-    (1, (1, 2), 0, (3, 2, 0), (0, 1, 1)),
-    (1, (2, 3), 1, (3, 3, 1), (1, 2, 1)),
+    (1, (0, 2), 0, (2, 2, 0), (2, 3, 0)),
+    (1, (0, 2), 1, (0, 3, 1), (2, 3, 1)),
+    (1, (0, 3), 0, (2, 3, 0), (0, 1, 1)),
+    (1, (0, 3), 1, (0, 2, 1), (0, 0, 1)),
+    (1, (1, 1), 0, (1, 2, 0), (1, 3, 0)),
+    (1, (1, 1), 1, (3, 1, 1), (1, 3, 1)),
+    (1, (1, 2), 0, (1, 3, 0), (2, 2, 0)),
+    (1, (1, 3), 1, (1, 2, 1), (0, 1, 0)),
+    (1, (1, 3), 1, (3, 3, 1), (1, 1, 1)),
+    (1, (2, 2), 0, (0, 2, 0), (1, 2, 1)),
+    (1, (2, 2), 1, (3, 2, 1), (1, 2, 0)),
+    (1, (2, 3), 0, (0, 3, 0), (0, 2, 0)),
+    (2, (0, 1), 0, (0, 2, 0), (1, 2, 0)),
+    (2, (0, 1), 0, (1, 1, 0), (1, 3, 0)),
     (2, (0, 1), 1, (0, 1, 1), (1, 2, 1)),
-    (2, (0, 1), 0, (0, 2, 0), (1, 2, 0)),
+    (2, (0, 3), 1, (0, 3, 1), (0, 1, 0)),
+    (2, (0, 3), 1, (2, 3, 1), (3, 3, 0)),
+    (2, (1, 2), 1, (1, 1, 1), (0, 1, 1)),
+    (2, (1, 2), 1, (3, 2, 1), (2, 2, 0)),
     (2, (1, 3), 0, (0, 3, 0), (2, 3, 0)),
-    (2, (0, 3), 1, (0, 3, 1), (0, 1, 1)),
-    (2, (1, 1), 0, (1, 1, 0), (1, 3, 1)),
-    (2, (1, 2), 1, (1, 1, 1), (0, 1, 0)),
     (2, (1, 3), 0, (1, 2, 0), (1, 1, 1)),
-    (2, (1, 2), 1, (1, 2, 1), (2, 2, 0)),
+    (2, (1, 3), 1, (3, 3, 1), (2, 3, 1)),
+    (2, (2, 3), 0, (2, 3, 0), (1, 3, 1)),
+    (2, (2, 3), 1, (2, 2, 1), (0, 2, 1)),
+    (2, (3, 3), 0, (1, 3, 0), (0, 3, 0)),
     (2, (3, 3), 1, (1, 3, 1), (0, 3, 1)),
-    (2, (2, 3), 1, (2, 2, 1), (0, 2, 1)),
-    (2, (3, 3), 0, (2, 3, 0), (0, 3, 0)),
-    (2, (0, 3), 1, (2, 3, 1), (3, 3, 0)),
-    (2, (2, 3), 0, (3, 3, 0), (1, 3, 0)),
-    (2, (1, 3), 1, (3, 3, 1), (2, 3, 1)),
 )
 
 

time: 32.7 us -> 32.6 us (level); the launches traced: 32.1 us -> 32.5 us
    ppermute x3, waiting for transfers between devices: 1.29 us -> 2.6 us  [chip_grid(): lax.ppermute(value, axes, pairs)]
    ppermute x2, waiting for transfers between devices: 1.91 us -> 0.62 us  [part_from(): lax.ppermute(parts, axes, [(d, d ^ row_bits * n_col + col_bits) for d in...]
    ppermute x2, starting transfers between devices: 3.81 us -> 5.08 us  [part_from(): lax.ppermute(parts, axes, [(d, d ^ row_bits * n_col + col_bits) for d in...]
    ppermute x3, starting transfers between devices: 4.22 us -> 3.21 us  [chip_grid(): lax.ppermute(value, axes, pairs)]
  transfers between devices with their start and end apart: 13 -> 13, of which waited for: 7 -> 6; matrix products, arithmetic and copies ran while one was open for 0% -> 0% of each run, Pallas kernels for 20% -> 20%
where the time goes in v7:
time: 32.6 us; the launch traced here: 32.5 us
  starting transfers between devices  15 us (46%)
  waiting for transfers between devices  8.55 us (26%)
  Pallas kernels  6.58 us (20%)
  local copies, waits for them, and re-layouts  0.99 us (3%)
  between operations  0.72 us (2%)
  other arithmetic  0.63 us (2%)
    pallas_call x6, Pallas kernels, call(): pl.pallas_call(kernel, out_shape=out_shape, in_specs=[SMEM] * smem + [VME...  6.58 us
    ppermute x4, starting transfers between devices, chip_grid(): came = [lax.ppermute(density, axes, pairs) for pairs in first]  6.05 us
    ppermute x4, waiting for transfers between devices, chip_grid(): came = [lax.ppermute(density, axes, pairs) for pairs in first]  5.32 us
    ppermute x2, starting transfers between devices, part_from(): lax.ppermute(parts, axes, [(d, d ^ row_bits * n_col + col_bits) for d in...  5.08 us
    ppermute x3, starting transfers between devices, chip_grid(): lax.ppermute(value, axes, pairs)  3.21 us
    ppermute x3, waiting for transfers between devices, chip_grid(): lax.ppermute(value, axes, pairs)  2.6 us
    unnamed x4, local copies, waits for them, and re-layouts  0.99 us
    ppermute x4, starting transfers between devices, share(): return lax.ppermute(value, axes, [(d, d ^ 1) for d in range(n_devices)])  0.65 us
  transfers between devices with their start and end apart: 13, of which 6 were waited for; matrix products, arithmetic and copies ran while one was open for 0% of the time, Pallas kernels for 20%

profile of v7, /device:TPU:0, one launch (start us, length us, event | category | flops | bytes accessed | tf_op | source)
XLA Modules:
  0.0 32.5 jit_solution(10245857310114020056)
XLA Ops:
  0.6 3.0 %collective-permute-start = (bf16[512,256]{1,0:T(8,128)(2,1)}, bf16[512,256]{1,0:T(8,128)(2,1)S(1)}, u32[]{:S(2)}, u32[]{:S(2)}) collective-permute-start(bf16[512,256]{1,0:T(8,128)(2,1)} %source.1), channel_id=1, source_target_pairs={{0,2},{1,0},{2,4},{3,1},{4,6},{5,3},{6,7},{7,5},{8,10},{9,8},{10,1... | collective-permute-start | bytes 786440 | tf_op jit(solution)/shard_map/ppermute | solution.py:561
  3.7 0.0 collective-permute-start.1
  3.7 1.5 %collective-permute-start.2 = (bf16[512,256]{1,0:T(8,128)(2,1)}, bf16[512,256]{1,0:T(8,128)(2,1)S(1)}, u32[]{:S(2)}, u32[]{:S(2)}) collective-permute-start(bf16[512,256]{1,0:T(8,128)(2,1)} %source.1), channel_id=1, source_target_pairs={{0,8},{1,9},{2,10},{3,11},{4,12},{5,13},{6,14},{7,15},{8,0},{9,1},... | collective-permute-start | bytes 786440 | tf_op jit(solution)/shard_map/ppermute | solution.py:561
  5.2 1.5 %collective-permute-start.3 = (bf16[512,256]{1,0:T(8,128)(2,1)}, bf16[512,256]{1,0:T(8,128)(2,1)S(1)}, u32[]{:S(2)}, u32[]{:S(2)}) collective-permute-start(bf16[512,256]{1,0:T(8,128)(2,1)} %source.1), channel_id=1, source_target_pairs={{0,16},{1,17},{2,18},{3,19},{4,20},{5,21},{6,22},{7,23},{8,24},{9,... | collective-permute-start | bytes 786440 | tf_op jit(solution)/shard_map/ppermute | solution.py:561
  6.7 0.0 copy-start
  6.7 1.0 %copy-done = bf16[512,256]{1,0:T(8,128)(2,1)S(1)} copy-done((bf16[512,256]{1,0:T(8,128)(2,1)S(1)}, bf16[512,256]{1,0:T(8,128)(2,1)}, u32[]{:S(2)}) %copy-start) | copy-done | bytes 262168
  7.7 0.0 copy-start.1
  7.7 1.9 %collective-permute-done.refs_1_ = bf16[512,256]{1,0:T(8,128)(2,1)S(1)} collective-permute-done((bf16[512,256]{1,0:T(8,128)(2,1)}, bf16[512,256]{1,0:T(8,128)(2,1)S(1)}, u32[]{:S(2)}, u32[]{:S(2)}) %collective-permute-start) | collective-permute-done | bytes 262176 | tf_op jit(solution)/shard_map/ppermute | solution.py:561
  9.6 0.7 %collective-permute-done.1.refs_2_ = bf16[512,256]{1,0:T(8,128)(2,1)S(1)} collective-permute-done((bf16[512,256]{1,0:T(8,128)(2,1)}, bf16[512,256]{1,0:T(8,128)(2,1)S(1)}, u32[]{:S(2)}, u32[]{:S(2)}) %collective-permute-start.1) | collective-permute-done | bytes 262176 | tf_op jit(solution)/shard_map/ppermute | solution.py:561
  10.3 1.4 %collective-permute-done.2.refs_3_ = bf16[512,256]{1,0:T(8,128)(2,1)S(1)} collective-permute-done((bf16[512,256]{1,0:T(8,128)(2,1)}, bf16[512,256]{1,0:T(8,128)(2,1)S(1)}, u32[]{:S(2)}, u32[]{:S(2)}) %collective-permute-start.2) | collective-permute-done | bytes 262176 | tf_op jit(solution)/shard_map/ppermute | solution.py:561
  11.7 1.4 %collective-permute-done.3.refs_4_ = bf16[512,256]{1,0:T(8,128)(2,1)S(1)} collective-permute-done((bf16[512,256]{1,0:T(8,128)(2,1)}, bf16[512,256]{1,0:T(8,128)(2,1)S(1)}, u32[]{:S(2)}, u32[]{:S(2)}) %collective-permute-start.3) | collective-permute-done | bytes 262176 | tf_op jit(solution)/shard_map/ppermute | solution.py:561
  13.0 0.1 shard_map.42
  13.1 0.1 shard_map.43
  13.2 0.1 collective-permute-start.5
  13.3 1.6 %collective-permute-start.4 = (bf16[512,256]{1,0:T(8,128)(2,1)S(1)}, bf16[512,256]{1,0:T(8,128)(2,1)S(1)}, u32[]{:S(2)}, u32[]{:S(2)}) collective-permute-start(bf16[512,256]{1,0:T(8,128)(2,1)S(1)} %get-tuple-element.37), channel_id=1, source_target_pairs={{16,4},{1,7},{18,6},{11,15},{21,1},{4,0},{22,31},{14,22},{28,2},{2... | collective-permute-start | bytes 786440 | tf_op jit(solution)/shard_map/ppermute | solution.py:567
  14.9 1.6 %collective-permute-start.7 = (bf16[512,256]{1,0:T(8,128)(2,1)S(1)}, bf16[512,256]{1,0:T(8,128)(2,1)S(1)}, u32[]{:S(2)}, u32[]{:S(2)}) collective-permute-start(bf16[512,256]{1,0:T(8,128)(2,1)S(1)} %get-tuple-element.48), channel_id=1, source_target_pairs={{0,7},{9,5},{19,6},{2,0},{20,22},{7,23},{22,3},{5,1},{12,14},{27,1... | collective-permute-start | bytes 786440 | tf_op jit(solution)/shard_map/ppermute | solution.py:567
  16.5 0.0 collective-permute-start.8
  16.5 0.0 collective-permute-done.5.refs_5_
  16.5 0.0 copy-done.1
  16.5 1.4 %shard_map.44 = f32[8,128]{1,0:T(8,128)S(1)} custom-call(s32[16,16]{1,0:T(8,128)S(1)} %copy-done.1, bf16[512,256]{1,0:T(8,128)(2,1)S(1)} %shard_map.41.refs_0_, bf16[512,256]{1,0:T(8,128)(2,1)S(1)} %collective-permute-done.refs_1_, bf16[512,256]{1,0:T(8,128)(2,1)S(1)} %collective-permute-done.1.refs_2_, bf16[512,256]{1,0:T(8,128)(2,1)S(1)} %collective-permute-done.2.refs_3_, ...), custom_call_target="tpu_custom_call" | custom-call | tf_op jit(solution)/shard_map/pallas_call | solution.py:544
  18.0 2.6 %collective-permute-start.6 = (f32[8,128]{1,0:T(8,128)S(1)}, f32[8,128]{1,0:T(8,128)S(1)}, u32[]{:S(2)}, u32[]{:S(2)}) collective-permute-start(f32[8,128]{1,0:T(8,128)S(1)} %shard_map.44), channel_id=1, source_target_pairs={{0,26},{1,27},{2,24},{3,25},{4,30},{5,31},{6,28},{7,29},{8,18},{9,... | collective-permute-start | bytes 12296 | tf_op jit(solution)/shard_map/ppermute | solution.py:559
  20.5 2.3 %shard_map.45 = (bf16[512,2048]{1,0:T(8,128)(2,1)S(1)}, bf16[2048,256]{1,0:T(8,128)(2,1)S(1)}, bf16[512,256]{1,0:T(8,128)(2,1)S(1)}) custom-call(s32[16,16]{1,0:T(8,128)S(1)} %copy-done.1, bf16[512,256]{1,0:T(8,128)(2,1)S(1)} %shard_map.41.refs_0_, bf16[512,256]{1,0:T(8,128)(2,1)S(1)} %collective-permute-done.refs_1_, ...), custom_call_target="tpu_custom_call" | custom-call | tf_op jit(solution)/shard_map/pallas_call | solution.py:544
  22.8 0.6 %collective-permute-done.6 = f32[8,128]{1,0:T(8,128)S(1)} collective-permute-done((f32[8,128]{1,0:T(8,128)S(1)}, f32[8,128]{1,0:T(8,128)S(1)}, u32[]{:S(2)}, u32[]{:S(2)}) %collective-permute-start.6) | collective-permute-done | bytes 4128 | tf_op jit(solution)/shard_map/ppermute | solution.py:559
  23.4 0.0 collective-permute-done.4.refs_0_
  23.4 2.6 %collective-permute-done.7.refs_1_ = bf16[512,256]{1,0:T(8,128)(2,1)S(1)} collective-permute-done((bf16[512,256]{1,0:T(8,128)(2,1)S(1)}, bf16[512,256]{1,0:T(8,128)(2,1)S(1)}, u32[]{:S(2)}, u32[]{:S(2)}) %collective-permute-start.7) | collective-permute-done | bytes 262176 | tf_op jit(solution)/shard_map/ppermute | solution.py:567
  26.0 0.0 collective-permute-done.8.refs_2_
  26.0 0.1 collective-permute-start.11
  26.1 0.4 %collective-permute-start.10 = (bf16[512,256]{1,0:T(8,128)(2,1)S(1)}, bf16[512,256]{1,0:T(8,128)(2,1)S(1)}, u32[]{:S(2)}, u32[]{:S(2)}) collective-permute-start(bf16[512,256]{1,0:T(8,128)(2,1)S(1)} %collective-permute-done.7.refs_1_), channel_id=1, source_target_pairs={{0,1},{1,0},{2,3},{3,2},{4,5},{5,4},{6,7},{7,6},{8,9},{9,8},{10,11... | collective-permute-start | bytes 786440 | tf_op jit(solution)/shard_map/ppermute | solution.py:556
  26.5 0.1 collective-permute-start.9
  26.6 2.5 %collective-permute-start.12 = (f32[8,128]{1,0:T(8,128)S(1)}, f32[8,128]{1,0:T(8,128)S(1)}, u32[]{:S(2)}, u32[]{:S(2)}) collective-permute-start(f32[8,128]{1,0:T(8,128)S(1)} %add.6), channel_id=1, source_target_pairs={{0,4},{1,5},{2,6},{3,7},{4,0},{5,1},{6,2},{7,3},{8,12},{9,13},{10,... | collective-permute-start | bytes 12296 | tf_op jit(solution)/shard_map/ppermute | solution.py:559
  29.1 0.0 collective-permute-done.11.refs_5_
  29.1 0.0 collective-permute-done.10.refs_4_
  29.2 0.0 collective-permute-done.9.refs_3_
  29.2 2.7 %shard_map.46 = (bf16[512,2048]{1,0:T(8,128)(2,1)S(1)}, bf16[2048,256]{1,0:T(8,128)(2,1)S(1)}, bf16[512,256]{1,0:T(8,128)(2,1)}) custom-call(bf16[512,256]{1,0:T(8,128)(2,1)S(1)} %collective-permute-done.4.refs_0_, bf16[512,256]{1,0:T(8,128)(2,1)S(1)} %collective-permute-done.7.refs_1_, ...), custom_call_target="tpu_custom_call", output_to_operand_aliasing={{0}: (7, {}), {1}: (8, {})} | custom-call | tf_op jit(solution)/shard_map/pallas_call | solution.py:544
  31.8 0.0 collective-permute-done.12
  31.8 0.6 %add_reduce_fusion = f32[2]{0:T(128)} fusion(f32[8,128]{1,0:T(8,128)S(1)} %collective-permute-done.12, f32[8,128]{1,0:T(8,128)S(1)} %add.6), kind=kLoop, calls=%fused_computation | loop fusion | flops 510 | bytes 2056 | tf_op jit(solution)/shard_map/reduce_sum | solution.py:598
  (2 shorter events, 0.0 us)
Async XLA Ops:
  0.6 8.9 %collective-permute-start = (bf16[512,256]{1,0:T(8,128)(2,1)}, bf16[512,256]{1,0:T(8,128)(2,1)S(1)}, u32[]{:S(2)}, u32[]{:S(2)}) collective-permute-start(bf16[512,256]{1,0:T(8,128)(2,1)} %source.1), channel_id=1, source_target_pairs={{0,2},{1,0},{2,4},{3,1},{4,6},{5,3},{6,7},{7,5},{8,10},{9,8},{10,1... | collective-permute-start | bytes 786440 | tf_op jit(solution)/shard_map/ppermute | solution.py:561
  3.7 6.6 %collective-permute-start.1 = (bf16[512,256]{1,0:T(8,128)(2,1)}, bf16[512,256]{1,0:T(8,128)(2,1)S(1)}, u32[]{:S(2)}, u32[]{:S(2)}) collective-permute-start(bf16[512,256]{1,0:T(8,128)(2,1)} %source.1), channel_id=1, source_target_pairs={{0,1},{1,3},{2,0},{3,5},{4,2},{5,7},{6,4},{7,6},{8,9},{9,11},{10,8... | collective-permute-start | bytes 786440 | tf_op jit(solution)/shard_map/ppermute | solution.py:561
  3.7 8.0 %collective-permute-start.2 = (bf16[512,256]{1,0:T(8,128)(2,1)}, bf16[512,256]{1,0:T(8,128)(2,1)S(1)}, u32[]{:S(2)}, u32[]{:S(2)}) collective-permute-start(bf16[512,256]{1,0:T(8,128)(2,1)} %source.1), channel_id=1, source_target_pairs={{0,8},{1,9},{2,10},{3,11},{4,12},{5,13},{6,14},{7,15},{8,0},{9,1},... | collective-permute-start | bytes 786440 | tf_op jit(solution)/shard_map/ppermute | solution.py:561
  5.2 7.9 %collective-permute-start.3 = (bf16[512,256]{1,0:T(8,128)(2,1)}, bf16[512,256]{1,0:T(8,128)(2,1)S(1)}, u32[]{:S(2)}, u32[]{:S(2)}) collective-permute-start(bf16[512,256]{1,0:T(8,128)(2,1)} %source.1), channel_id=1, source_target_pairs={{0,16},{1,17},{2,18},{3,19},{4,20},{5,21},{6,22},{7,23},{8,24},{9,... | collective-permute-start | bytes 786440 | tf_op jit(solution)/shard_map/ppermute | solution.py:561
  6.7 1.0 %copy-start = (bf16[512,256]{1,0:T(8,128)(2,1)S(1)}, bf16[512,256]{1,0:T(8,128)(2,1)}, u32[]{:S(2)}) copy-start(bf16[512,256]{1,0:T(8,128)(2,1)} %source.1) | copy-start | bytes 786436
  7.7 8.8 %copy-start.1 = (s32[16,16]{1,0:T(8,128)S(1)}, s32[16,16]{1,0:T(8,128)}, u32[]{:S(2)}) copy-start(s32[16,16]{1,0:T(8,128)} %pattern.3) | copy-start | bytes 3076
  13.2 3.3 %collective-permute-start.5 = (bf16[5,512,256]{2,1,0:T(8,128)(2,1)S(1)}, bf16[5,512,256]{2,1,0:T(8,128)(2,1)S(1)}, u32[]{:S(2)}, u32[]{:S(2)}) collective-permute-start(bf16[5,512,256]{2,1,0:T(8,128)(2,1)S(1)} %shard_map.43), channel_id=1, source_target_pairs={{0,1},{1,0},{2,3},{3,2},{4,5},{5,4},{6,7},{7,6},{8,9},{9,8},{10,11... | collective-permute-start | bytes 3932168 | tf_op jit(solution)/shard_map/ppermute | solution.py:556
  13.3 10.2 %collective-permute-start.4 = (bf16[512,256]{1,0:T(8,128)(2,1)S(1)}, bf16[512,256]{1,0:T(8,128)(2,1)S(1)}, u32[]{:S(2)}, u32[]{:S(2)}) collective-permute-start(bf16[512,256]{1,0:T(8,128)(2,1)S(1)} %get-tuple-element.37), channel_id=1, source_target_pairs={{16,4},{1,7},{18,6},{11,15},{21,1},{4,0},{22,31},{14,22},{28,2},{2... | collective-permute-start | bytes 786440 | tf_op jit(solution)/shard_map/ppermute | solution.py:567
  14.9 11.1 %collective-permute-start.7 = (bf16[512,256]{1,0:T(8,128)(2,1)S(1)}, bf16[512,256]{1,0:T(8,128)(2,1)S(1)}, u32[]{:S(2)}, u32[]{:S(2)}) collective-permute-start(bf16[512,256]{1,0:T(8,128)(2,1)S(1)} %get-tuple-element.48), channel_id=1, source_target_pairs={{0,7},{9,5},{19,6},{2,0},{20,22},{7,23},{22,3},{5,1},{12,14},{27,1... | collective-permute-start | bytes 786440 | tf_op jit(solution)/shard_map/ppermute | solution.py:567
  16.5 9.5 %collective-permute-start.8 = (bf16[512,256]{1,0:T(8,128)(2,1)S(1)}, bf16[512,256]{1,0:T(8,128)(2,1)S(1)}, u32[]{:S(2)}, u32[]{:S(2)}) collective-permute-start(bf16[512,256]{1,0:T(8,128)(2,1)S(1)} %get-tuple-element.51), channel_id=1, source_target_pairs={{4,12},{10,14},{3,13},{7,2},{23,30},{11,3},{29,20},{6,22},{12,11},... | collective-permute-start | bytes 786440 | tf_op jit(solution)/shard_map/ppermute | solution.py:567
  18.0 5.5 %collective-permute-start.6 = (f32[8,128]{1,0:T(8,128)S(1)}, f32[8,128]{1,0:T(8,128)S(1)}, u32[]{:S(2)}, u32[]{:S(2)}) collective-permute-start(f32[8,128]{1,0:T(8,128)S(1)} %shard_map.44), channel_id=1, source_target_pairs={{0,26},{1,27},{2,24},{3,25},{4,30},{5,31},{6,28},{7,29},{8,18},{9,... | collective-permute-start | bytes 12296 | tf_op jit(solution)/shard_map/ppermute | solution.py:559
  26.0 3.1 %collective-permute-start.11 = (bf16[512,256]{1,0:T(8,128)(2,1)S(1)}, bf16[512,256]{1,0:T(8,128)(2,1)S(1)}, u32[]{:S(2)}, u32[]{:S(2)}) collective-permute-start(bf16[512,256]{1,0:T(8,128)(2,1)S(1)} %collective-permute-done.8.refs_2_), channel_id=1, source_target_pairs={{0,1},{1,0},{2,3},{3,2},{4,5},{5,4},{6,7},{7,6},{8,9},{9,8},{10,11... | collective-permute-start | bytes 786440 | tf_op jit(solution)/shard_map/ppermute | solution.py:556
  26.1 3.1 %collective-permute-start.10 = (bf16[512,256]{1,0:T(8,128)(2,1)S(1)}, bf16[512,256]{1,0:T(8,128)(2,1)S(1)}, u32[]{:S(2)}, u32[]{:S(2)}) collective-permute-start(bf16[512,256]{1,0:T(8,128)(2,1)S(1)} %collective-permute-done.7.refs_1_), channel_id=1, source_target_pairs={{0,1},{1,0},{2,3},{3,2},{4,5},{5,4},{6,7},{7,6},{8,9},{9,8},{10,11... | collective-permute-start | bytes 786440 | tf_op jit(solution)/shard_map/ppermute | solution.py:556
  26.5 2.6 %collective-permute-start.9 = (bf16[512,256]{1,0:T(8,128)(2,1)S(1)}, bf16[512,256]{1,0:T(8,128)(2,1)S(1)}, u32[]{:S(2)}, u32[]{:S(2)}) collective-permute-start(bf16[512,256]{1,0:T(8,128)(2,1)S(1)} %collective-permute-done.4.refs_0_), channel_id=1, source_target_pairs={{0,1},{1,0},{2,3},{3,2},{4,5},{5,4},{6,7},{7,6},{8,9},{9,8},{10,11... | collective-permute-start | bytes 786440 | tf_op jit(solution)/shard_map/ppermute | solution.py:556
  26.6 5.2 %collective-permute-start.12 = (f32[8,128]{1,0:T(8,128)S(1)}, f32[8,128]{1,0:T(8,128)S(1)}, u32[]{:S(2)}, u32[]{:S(2)}) collective-permute-start(f32[8,128]{1,0:T(8,128)S(1)} %add.6), channel_id=1, source_target_pairs={{0,4},{1,5},{2,6},{3,7},{4,0},{5,1},{6,2},{7,3},{8,12},{9,13},{10,... | collective-permute-start | bytes 12296 | tf_op jit(solution)/shard_map/ppermute | solution.py:559

commit v8 on v4

--- a/solution.py
+++ b/solution.py
@@ -154,7 +154,7 @@
 SEEN = ((), (0,), (1, 3), (2,))
 
 MESSAGES = (
-    (0, (0, 0), 0, (0, 0, 0), (0, 3, 1)),
+    (0, (0, 0), 1, (0, 0, 1), (0, 3, 1)),
     (0, (0, 2), 0, (0, 1, 0), (0, 0, 0)),
     (0, (2, 2), 0, (0, 2, 0), (1, 2, 1)),
     (0, (0, 3), 1, (0, 2, 1), (0, 0, 1)),
@@ -170,7 +170,7 @@
     (0, (1, 1), 1, (3, 1, 1), (1, 3, 1)),
     (0, (2, 2), 1, (3, 2, 1), (1, 2, 0)),
     (0, (1, 3), 1, (3, 3, 1), (1, 1, 1)),
-    (1, (0, 0), 1, (0, 0, 1), (0, 3, 1)),
+    (1, (0, 0), 0, (0, 1, 0), (0, 3, 1)),
     (1, (0, 3), 0, (0, 2, 0), (0, 0, 0)),
     (1, (2, 3), 1, (0, 3, 1), (1, 3, 0)),
     (1, (0, 1), 1, (1, 1, 1), (1, 3, 1)),

time: 32.2 us -> 32.1 us (level)
  waiting for transfers between devices: 8.96 us -> 8.08 us
  starting transfers between devices: 14.2 us -> 15 us
    ppermute x2, starting transfers between devices: 3.22 us -> 4.87 us  [part_from(): lax.ppermute(parts, axes, [(d, d ^ row_bits * n_col + col_bits) for d in...]
    ppermute x2, waiting for transfers between devices: 1.99 us -> 0.76 us  [part_from(): lax.ppermute(parts, axes, [(d, d ^ row_bits * n_col + col_bits) for d in...]
    ppermute x3, starting transfers between devices: 4.3 us -> 3.16 us  [chip_grid(): lax.ppermute(value, axes, pairs)]
    ppermute x4, starting transfers between devices: 0.59 us -> 0.95 us  [share(): return lax.ppermute(value, axes, [(d, d ^ 1) for d in range(n_devices)])]
    ppermute x3, waiting for transfers between devices: 1.64 us -> 1.99 us  [chip_grid(): lax.ppermute(value, axes, pairs)]
  transfers between devices with their start and end apart: 13 -> 13, of which waited for: 7 -> 6; matrix products, arithmetic and copies ran while one was open for 0% -> 0% of each run, Pallas kernels for 20% -> 20%
where the time goes in v8:
time: 32.1 us; the launch traced here: 31.9 us
  starting transfers between devices  15 us (47%)
  waiting for transfers between devices  8.08 us (25%)
  Pallas kernels  6.5 us (20%)
  local copies, waits for them, and re-layouts  0.99 us (3%)
  between operations  0.7 us (2%)
  other arithmetic  0.63 us (2%)
    pallas_call x6, Pallas kernels, call(): pl.pallas_call(kernel, out_shape=out_shape, in_specs=[SMEM] * smem + [VME...  6.5 us
    ppermute x4, starting transfers between devices, chip_grid(): came = [lax.ppermute(density, axes, pairs) for pairs in first]  6.05 us
    ppermute x4, waiting for transfers between devices, chip_grid(): came = [lax.ppermute(density, axes, pairs) for pairs in first]  5.32 us
    ppermute x2, starting transfers between devices, part_from(): lax.ppermute(parts, axes, [(d, d ^ row_bits * n_col + col_bits) for d in...  4.87 us
    ppermute x3, starting transfers between devices, chip_grid(): lax.ppermute(value, axes, pairs)  3.16 us
    ppermute x3, waiting for transfers between devices, chip_grid(): lax.ppermute(value, axes, pairs)  1.99 us
    unnamed x4, local copies, waits for them, and re-layouts  0.99 us
    ppermute x4, starting transfers between devices, share(): return lax.ppermute(value, axes, [(d, d ^ 1) for d in range(n_devices)])  0.95 us
  transfers between devices with their start and end apart: 13, of which 6 were waited for; matrix products, arithmetic and copies ran while one was open for 0% of the time, Pallas kernels for 20%

profile of v8, /device:TPU:0, one launch (start us, length us, event | category | flops | bytes accessed | tf_op | source)
XLA Modules:
  0.0 31.9 jit_solution(6239635764379028682)
XLA Ops:
  0.6 3.0 %collective-permute-start = (bf16[512,256]{1,0:T(8,128)(2,1)}, bf16[512,256]{1,0:T(8,128)(2,1)S(1)}, u32[]{:S(2)}, u32[]{:S(2)}) collective-permute-start(bf16[512,256]{1,0:T(8,128)(2,1)} %source.1), channel_id=1, source_target_pairs={{0,2},{1,0},{2,4},{3,1},{4,6},{5,3},{6,7},{7,5},{8,10},{9,8},{10,1... | collective-permute-start | bytes 786440 | tf_op jit(solution)/shard_map/ppermute | solution.py:561
  3.7 0.0 collective-permute-start.1
  3.7 1.5 %collective-permute-start.2 = (bf16[512,256]{1,0:T(8,128)(2,1)}, bf16[512,256]{1,0:T(8,128)(2,1)S(1)}, u32[]{:S(2)}, u32[]{:S(2)}) collective-permute-start(bf16[512,256]{1,0:T(8,128)(2,1)} %source.1), channel_id=1, source_target_pairs={{0,8},{1,9},{2,10},{3,11},{4,12},{5,13},{6,14},{7,15},{8,0},{9,1},... | collective-permute-start | bytes 786440 | tf_op jit(solution)/shard_map/ppermute | solution.py:561
  5.2 1.5 %collective-permute-start.3 = (bf16[512,256]{1,0:T(8,128)(2,1)}, bf16[512,256]{1,0:T(8,128)(2,1)S(1)}, u32[]{:S(2)}, u32[]{:S(2)}) collective-permute-start(bf16[512,256]{1,0:T(8,128)(2,1)} %source.1), channel_id=1, source_target_pairs={{0,16},{1,17},{2,18},{3,19},{4,20},{5,21},{6,22},{7,23},{8,24},{9,... | collective-permute-start | bytes 786440 | tf_op jit(solution)/shard_map/ppermute | solution.py:561
  6.7 0.0 copy-start
  6.7 1.0 %copy-done = bf16[512,256]{1,0:T(8,128)(2,1)S(1)} copy-done((bf16[512,256]{1,0:T(8,128)(2,1)S(1)}, bf16[512,256]{1,0:T(8,128)(2,1)}, u32[]{:S(2)}) %copy-start) | copy-done | bytes 262168
  7.7 0.0 copy-start.1
  7.7 1.9 %collective-permute-done.refs_1_ = bf16[512,256]{1,0:T(8,128)(2,1)S(1)} collective-permute-done((bf16[512,256]{1,0:T(8,128)(2,1)}, bf16[512,256]{1,0:T(8,128)(2,1)S(1)}, u32[]{:S(2)}, u32[]{:S(2)}) %collective-permute-start) | collective-permute-done | bytes 262176 | tf_op jit(solution)/shard_map/ppermute | solution.py:561
  9.6 0.7 %collective-permute-done.1.refs_2_ = bf16[512,256]{1,0:T(8,128)(2,1)S(1)} collective-permute-done((bf16[512,256]{1,0:T(8,128)(2,1)}, bf16[512,256]{1,0:T(8,128)(2,1)S(1)}, u32[]{:S(2)}, u32[]{:S(2)}) %collective-permute-start.1) | collective-permute-done | bytes 262176 | tf_op jit(solution)/shard_map/ppermute | solution.py:561
  10.3 1.4 %collective-permute-done.2.refs_3_ = bf16[512,256]{1,0:T(8,128)(2,1)S(1)} collective-permute-done((bf16[512,256]{1,0:T(8,128)(2,1)}, bf16[512,256]{1,0:T(8,128)(2,1)S(1)}, u32[]{:S(2)}, u32[]{:S(2)}) %collective-permute-start.2) | collective-permute-done | bytes 262176 | tf_op jit(solution)/shard_map/ppermute | solution.py:561
  11.7 1.4 %collective-permute-done.3.refs_4_ = bf16[512,256]{1,0:T(8,128)(2,1)S(1)} collective-permute-done((bf16[512,256]{1,0:T(8,128)(2,1)}, bf16[512,256]{1,0:T(8,128)(2,1)S(1)}, u32[]{:S(2)}, u32[]{:S(2)}) %collective-permute-start.3) | collective-permute-done | bytes 262176 | tf_op jit(solution)/shard_map/ppermute | solution.py:561
  13.0 0.1 shard_map.43
  13.1 0.1 collective-permute-start.5
  13.2 0.5 %collective-permute-start.4 = (bf16[512,256]{1,0:T(8,128)(2,1)S(1)}, bf16[512,256]{1,0:T(8,128)(2,1)S(1)}, u32[]{:S(2)}, u32[]{:S(2)}) collective-permute-start(bf16[512,256]{1,0:T(8,128)(2,1)S(1)} %get-tuple-element.37), channel_id=1, source_target_pairs={{1,7},{2,0},{4,13},{5,1},{6,4},{7,23},{9,5},{12,14},{13,2},{14,20}... | collective-permute-start | bytes 786440 | tf_op jit(solution)/shard_map/ppermute | solution.py:567
  13.6 1.3 %collective-permute-start.7 = (bf16[512,256]{1,0:T(8,128)(2,1)S(1)}, bf16[512,256]{1,0:T(8,128)(2,1)S(1)}, u32[]{:S(2)}, u32[]{:S(2)}) collective-permute-start(bf16[512,256]{1,0:T(8,128)(2,1)S(1)} %get-tuple-element.48), channel_id=1, source_target_pairs={{2,7},{4,0},{7,14},{11,15},{12,3},{14,22},{16,4},{18,6},{21,1},{22... | collective-permute-start | bytes 786440 | tf_op jit(solution)/shard_map/ppermute | solution.py:567
  14.9 1.4 %collective-permute-start.8 = (bf16[512,256]{1,0:T(8,128)(2,1)S(1)}, bf16[512,256]{1,0:T(8,128)(2,1)S(1)}, u32[]{:S(2)}, u32[]{:S(2)}) collective-permute-start(bf16[512,256]{1,0:T(8,128)(2,1)S(1)} %get-tuple-element.51), channel_id=1, source_target_pairs={{3,13},{4,12},{6,22},{7,2},{10,14},{11,3},{12,11},{14,6},{15,7},{2... | collective-permute-start | bytes 786440 | tf_op jit(solution)/shard_map/ppermute | solution.py:567
  16.4 0.0 collective-permute-done.5.refs_5_
  16.4 0.0 copy-done.1
  16.4 1.4 %shard_map.44 = f32[8,128]{1,0:T(8,128)S(1)} custom-call(s32[16,16]{1,0:T(8,128)S(1)} %copy-done.1, bf16[512,256]{1,0:T(8,128)(2,1)S(1)} %shard_map.41.refs_0_, bf16[512,256]{1,0:T(8,128)(2,1)S(1)} %collective-permute-done.refs_1_, bf16[512,256]{1,0:T(8,128)(2,1)S(1)} %collective-permute-done.1.refs_2_, bf16[512,256]{1,0:T(8,128)(2,1)S(1)} %collective-permute-done.2.refs_3_, ...), custom_call_target="tpu_custom_call" | custom-call | tf_op jit(solution)/shard_map/pallas_call | solution.py:544
  17.8 2.4 %collective-permute-start.6 = (f32[8,128]{1,0:T(8,128)S(1)}, f32[8,128]{1,0:T(8,128)S(1)}, u32[]{:S(2)}, u32[]{:S(2)}) collective-permute-start(f32[8,128]{1,0:T(8,128)S(1)} %shard_map.44), channel_id=1, source_target_pairs={{0,26},{1,27},{2,24},{3,25},{4,30},{5,31},{6,28},{7,29},{8,18},{9,... | collective-permute-start | bytes 12296 | tf_op jit(solution)/shard_map/ppermute | solution.py:559
  20.2 2.3 %shard_map.45 = (bf16[512,2048]{1,0:T(8,128)(2,1)S(1)}, bf16[2048,256]{1,0:T(8,128)(2,1)S(1)}, bf16[512,256]{1,0:T(8,128)(2,1)S(1)}) custom-call(s32[16,16]{1,0:T(8,128)S(1)} %copy-done.1, bf16[512,256]{1,0:T(8,128)(2,1)S(1)} %shard_map.41.refs_0_, bf16[512,256]{1,0:T(8,128)(2,1)S(1)} %collective-permute-done.refs_1_, ...), custom_call_target="tpu_custom_call" | custom-call | tf_op jit(solution)/shard_map/pallas_call | solution.py:544
  22.5 0.8 %collective-permute-done.6 = f32[8,128]{1,0:T(8,128)S(1)} collective-permute-done((f32[8,128]{1,0:T(8,128)S(1)}, f32[8,128]{1,0:T(8,128)S(1)}, u32[]{:S(2)}, u32[]{:S(2)}) %collective-permute-start.6) | collective-permute-done | bytes 4128 | tf_op jit(solution)/shard_map/ppermute | solution.py:559
  23.3 2.0 %collective-permute-done.4.refs_0_ = bf16[512,256]{1,0:T(8,128)(2,1)S(1)} collective-permute-done((bf16[512,256]{1,0:T(8,128)(2,1)S(1)}, bf16[512,256]{1,0:T(8,128)(2,1)S(1)}, u32[]{:S(2)}, u32[]{:S(2)}) %collective-permute-start.4) | collective-permute-done | bytes 262176 | tf_op jit(solution)/shard_map/ppermute | solution.py:567
  25.3 0.0 collective-permute-done.7.refs_1_
  25.3 0.0 collective-permute-done.8.refs_2_
  25.3 0.4 %collective-permute-start.11 = (bf16[512,256]{1,0:T(8,128)(2,1)S(1)}, bf16[512,256]{1,0:T(8,128)(2,1)S(1)}, u32[]{:S(2)}, u32[]{:S(2)}) collective-permute-start(bf16[512,256]{1,0:T(8,128)(2,1)S(1)} %collective-permute-done.8.refs_2_), channel_id=1, source_target_pairs={{0,1},{1,0},{2,3},{3,2},{4,5},{5,4},{6,7},{7,6},{8,9},{9,8},{10,11... | collective-permute-start | bytes 786440 | tf_op jit(solution)/shard_map/ppermute | solution.py:556
  25.7 0.1 collective-permute-start.10
  25.8 0.4 %collective-permute-start.9 = (bf16[512,256]{1,0:T(8,128)(2,1)S(1)}, bf16[512,256]{1,0:T(8,128)(2,1)S(1)}, u32[]{:S(2)}, u32[]{:S(2)}) collective-permute-start(bf16[512,256]{1,0:T(8,128)(2,1)S(1)} %collective-permute-done.4.refs_0_), channel_id=1, source_target_pairs={{0,1},{1,0},{2,3},{3,2},{4,5},{5,4},{6,7},{7,6},{8,9},{9,8},{10,11... | collective-permute-start | bytes 786440 | tf_op jit(solution)/shard_map/ppermute | solution.py:556
  26.2 2.4 %collective-permute-start.12 = (f32[8,128]{1,0:T(8,128)S(1)}, f32[8,128]{1,0:T(8,128)S(1)}, u32[]{:S(2)}, u32[]{:S(2)}) collective-permute-start(f32[8,128]{1,0:T(8,128)S(1)} %add.6), channel_id=1, source_target_pairs={{0,4},{1,5},{2,6},{3,7},{4,0},{5,1},{6,2},{7,3},{8,12},{9,13},{10,... | collective-permute-start | bytes 12296 | tf_op jit(solution)/shard_map/ppermute | solution.py:559
  28.6 0.0 collective-permute-done.11.refs_5_
  28.6 0.0 collective-permute-done.10.refs_4_
  28.6 0.0 collective-permute-done.9.refs_3_
  28.6 2.7 %shard_map.46 = (bf16[512,2048]{1,0:T(8,128)(2,1)S(1)}, bf16[2048,256]{1,0:T(8,128)(2,1)S(1)}, bf16[512,256]{1,0:T(8,128)(2,1)}) custom-call(bf16[512,256]{1,0:T(8,128)(2,1)S(1)} %collective-permute-done.4.refs_0_, bf16[512,256]{1,0:T(8,128)(2,1)S(1)} %collective-permute-done.7.refs_1_, ...), custom_call_target="tpu_custom_call", output_to_operand_aliasing={{0}: (7, {}), {1}: (8, {})} | custom-call | tf_op jit(solution)/shard_map/pallas_call | solution.py:544
  31.3 0.0 collective-permute-done.12
  31.3 0.6 %add_reduce_fusion = f32[2]{0:T(128)} fusion(f32[8,128]{1,0:T(8,128)S(1)} %collective-permute-done.12, f32[8,128]{1,0:T(8,128)S(1)} %add.6), kind=kLoop, calls=%fused_computation | loop fusion | flops 510 | bytes 2056 | tf_op jit(solution)/shard_map/reduce_sum | solution.py:598
  (3 shorter events, 0.0 us)
Async XLA Ops:
  0.6 8.9 %collective-permute-start = (bf16[512,256]{1,0:T(8,128)(2,1)}, bf16[512,256]{1,0:T(8,128)(2,1)S(1)}, u32[]{:S(2)}, u32[]{:S(2)}) collective-permute-start(bf16[512,256]{1,0:T(8,128)(2,1)} %source.1), channel_id=1, source_target_pairs={{0,2},{1,0},{2,4},{3,1},{4,6},{5,3},{6,7},{7,5},{8,10},{9,8},{10,1... | collective-permute-start | bytes 786440 | tf_op jit(solution)/shard_map/ppermute | solution.py:561
  3.7 6.6 %collective-permute-start.1 = (bf16[512,256]{1,0:T(8,128)(2,1)}, bf16[512,256]{1,0:T(8,128)(2,1)S(1)}, u32[]{:S(2)}, u32[]{:S(2)}) collective-permute-start(bf16[512,256]{1,0:T(8,128)(2,1)} %source.1), channel_id=1, source_target_pairs={{0,1},{1,3},{2,0},{3,5},{4,2},{5,7},{6,4},{7,6},{8,9},{9,11},{10,8... | collective-permute-start | bytes 786440 | tf_op jit(solution)/shard_map/ppermute | solution.py:561
  3.7 8.0 %collective-permute-start.2 = (bf16[512,256]{1,0:T(8,128)(2,1)}, bf16[512,256]{1,0:T(8,128)(2,1)S(1)}, u32[]{:S(2)}, u32[]{:S(2)}) collective-permute-start(bf16[512,256]{1,0:T(8,128)(2,1)} %source.1), channel_id=1, source_target_pairs={{0,8},{1,9},{2,10},{3,11},{4,12},{5,13},{6,14},{7,15},{8,0},{9,1},... | collective-permute-start | bytes 786440 | tf_op jit(solution)/shard_map/ppermute | solution.py:561
  5.2 7.9 %collective-permute-start.3 = (bf16[512,256]{1,0:T(8,128)(2,1)}, bf16[512,256]{1,0:T(8,128)(2,1)S(1)}, u32[]{:S(2)}, u32[]{:S(2)}) collective-permute-start(bf16[512,256]{1,0:T(8,128)(2,1)} %source.1), channel_id=1, source_target_pairs={{0,16},{1,17},{2,18},{3,19},{4,20},{5,21},{6,22},{7,23},{8,24},{9,... | collective-permute-start | bytes 786440 | tf_op jit(solution)/shard_map/ppermute | solution.py:561
  6.7 1.0 %copy-start = (bf16[512,256]{1,0:T(8,128)(2,1)S(1)}, bf16[512,256]{1,0:T(8,128)(2,1)}, u32[]{:S(2)}) copy-start(bf16[512,256]{1,0:T(8,128)(2,1)} %source.1) | copy-start | bytes 786436
  7.7 8.7 %copy-start.1 = (s32[16,16]{1,0:T(8,128)S(1)}, s32[16,16]{1,0:T(8,128)}, u32[]{:S(2)}) copy-start(s32[16,16]{1,0:T(8,128)} %pattern.3) | copy-start | bytes 3076
  13.1 3.2 %collective-permute-start.5 = (bf16[5,512,256]{2,1,0:T(8,128)(2,1)S(1)}, bf16[5,512,256]{2,1,0:T(8,128)(2,1)S(1)}, u32[]{:S(2)}, u32[]{:S(2)}) collective-permute-start(bf16[5,512,256]{2,1,0:T(8,128)(2,1)S(1)} %shard_map.43), channel_id=1, source_target_pairs={{0,1},{1,0},{2,3},{3,2},{4,5},{5,4},{6,7},{7,6},{8,9},{9,8},{10,11... | collective-permute-start | bytes 3932168 | tf_op jit(solution)/shard_map/ppermute | solution.py:556
  13.2 12.1 %collective-permute-start.4 = (bf16[512,256]{1,0:T(8,128)(2,1)S(1)}, bf16[512,256]{1,0:T(8,128)(2,1)S(1)}, u32[]{:S(2)}, u32[]{:S(2)}) collective-permute-start(bf16[512,256]{1,0:T(8,128)(2,1)S(1)} %get-tuple-element.37), channel_id=1, source_target_pairs={{1,7},{2,0},{4,13},{5,1},{6,4},{7,23},{9,5},{12,14},{13,2},{14,20}... | collective-permute-start | bytes 786440 | tf_op jit(solution)/shard_map/ppermute | solution.py:567
  13.6 11.6 %collective-permute-start.7 = (bf16[512,256]{1,0:T(8,128)(2,1)S(1)}, bf16[512,256]{1,0:T(8,128)(2,1)S(1)}, u32[]{:S(2)}, u32[]{:S(2)}) collective-permute-start(bf16[512,256]{1,0:T(8,128)(2,1)S(1)} %get-tuple-element.48), channel_id=1, source_target_pairs={{2,7},{4,0},{7,14},{11,15},{12,3},{14,22},{16,4},{18,6},{21,1},{22... | collective-permute-start | bytes 786440 | tf_op jit(solution)/shard_map/ppermute | solution.py:567
  14.9 10.3 %collective-permute-start.8 = (bf16[512,256]{1,0:T(8,128)(2,1)S(1)}, bf16[512,256]{1,0:T(8,128)(2,1)S(1)}, u32[]{:S(2)}, u32[]{:S(2)}) collective-permute-start(bf16[512,256]{1,0:T(8,128)(2,1)S(1)} %get-tuple-element.51), channel_id=1, source_target_pairs={{3,13},{4,12},{6,22},{7,2},{10,14},{11,3},{12,11},{14,6},{15,7},{2... | collective-permute-start | bytes 786440 | tf_op jit(solution)/shard_map/ppermute | solution.py:567
  17.8 5.5 %collective-permute-start.6 = (f32[8,128]{1,0:T(8,128)S(1)}, f32[8,128]{1,0:T(8,128)S(1)}, u32[]{:S(2)}, u32[]{:S(2)}) collective-permute-start(f32[8,128]{1,0:T(8,128)S(1)} %shard_map.44), channel_id=1, source_target_pairs={{0,26},{1,27},{2,24},{3,25},{4,30},{5,31},{6,28},{7,29},{8,18},{9,... | collective-permute-start | bytes 12296 | tf_op jit(solution)/shard_map/ppermute | solution.py:559
  25.3 3.3 %collective-permute-start.11 = (bf16[512,256]{1,0:T(8,128)(2,1)S(1)}, bf16[512,256]{1,0:T(8,128)(2,1)S(1)}, u32[]{:S(2)}, u32[]{:S(2)}) collective-permute-start(bf16[512,256]{1,0:T(8,128)(2,1)S(1)} %collective-permute-done.8.refs_2_), channel_id=1, source_target_pairs={{0,1},{1,0},{2,3},{3,2},{4,5},{5,4},{6,7},{7,6},{8,9},{9,8},{10,11... | collective-permute-start | bytes 786440 | tf_op jit(solution)/shard_map/ppermute | solution.py:556
  25.7 3.0 %collective-permute-start.10 = (bf16[512,256]{1,0:T(8,128)(2,1)S(1)}, bf16[512,256]{1,0:T(8,128)(2,1)S(1)}, u32[]{:S(2)}, u32[]{:S(2)}) collective-permute-start(bf16[512,256]{1,0:T(8,128)(2,1)S(1)} %collective-permute-done.7.refs_1_), channel_id=1, source_target_pairs={{0,1},{1,0},{2,3},{3,2},{4,5},{5,4},{6,7},{7,6},{8,9},{9,8},{10,11... | collective-permute-start | bytes 786440 | tf_op jit(solution)/shard_map/ppermute | solution.py:556
  25.8 2.8 %collective-permute-start.9 = (bf16[512,256]{1,0:T(8,128)(2,1)S(1)}, bf16[512,256]{1,0:T(8,128)(2,1)S(1)}, u32[]{:S(2)}, u32[]{:S(2)}) collective-permute-start(bf16[512,256]{1,0:T(8,128)(2,1)S(1)} %collective-permute-done.4.refs_0_), channel_id=1, source_target_pairs={{0,1},{1,0},{2,3},{3,2},{4,5},{5,4},{6,7},{7,6},{8,9},{9,8},{10,11... | collective-permute-start | bytes 786440 | tf_op jit(solution)/shard_map/ppermute | solution.py:556
  26.2 5.1 %collective-permute-start.12 = (f32[8,128]{1,0:T(8,128)S(1)}, f32[8,128]{1,0:T(8,128)S(1)}, u32[]{:S(2)}, u32[]{:S(2)}) collective-permute-start(f32[8,128]{1,0:T(8,128)S(1)} %add.6), channel_id=1, source_target_pairs={{0,4},{1,5},{2,6},{3,7},{4,0},{5,1},{6,2},{7,3},{8,12},{9,13},{10,... | collective-permute-start | bytes 12296 | tf_op jit(solution)/shard_map/ppermute | solution.py:559

commit v9 on v6

--- a/solution.py
+++ b/solution.py
@@ -157,7 +157,7 @@
 )
 LAST_HEARD = ((0, 1), (0, 0), (0, 3), (0, 2), (3, 0), (1, 2), (1, 1), (3, 3), (2, 1), (2, 0), (2, 3), (2, 2), (1, 0), (3, 2), (3, 1), (1, 3))
 MESSAGES = (
-    (0, (0, 0), 0, (0, 0, 0), (0, 3, 1)),
+    (0, (0, 0), 1, (0, 0, 1), (0, 3, 1)),
     (0, (0, 2), 0, (0, 1, 0), (0, 0, 0)),
     (0, (2, 2), 0, (0, 2, 0), (1, 2, 1)),
     (0, (0, 3), 1, (0, 2, 1), (0, 0, 1)),
@@ -173,7 +173,7 @@
     (0, (1, 1), 1, (3, 1, 1), (1, 3, 1)),
     (0, (2, 2), 1, (3, 2, 1), (1, 2, 0)),
     (0, (1, 3), 1, (3, 3, 1), (1, 1, 1)),
-    (1, (0, 0), 1, (0, 0, 1), (0, 3, 1)),
+    (1, (0, 0), 0, (0, 1, 0), (0, 3, 1)),
     (1, (0, 3), 0, (0, 2, 0), (0, 0, 0)),
     (1, (2, 3), 1, (0, 3, 1), (1, 3, 0)),
     (1, (0, 1), 1, (1, 1, 1), (1, 3, 1)),

time: 32.6 us -> 32.5 us (level)
  starting transfers between devices: 16.9 us -> 17.4 us
  waiting for transfers between devices: 6.17 us -> 5.67 us
    ppermute x2, starting transfers between devices: 3.6 us -> 4.87 us  [chip_grid(): received = [lax.ppermute(parts, axes, pairs) for pairs in early]]
    ppermute x3, starting transfers between devices: 4.3 us -> 3.16 us  [chip_grid(): lax.ppermute(value, axes, pairs)]
    ppermute x3, waiting for transfers between devices: 0.55 us -> 0.01 us  [chip_grid(): lax.ppermute(value, axes, pairs)]
    ppermute x4, starting transfers between devices: 0.71 us -> 1.19 us  [share(): return lax.ppermute(value, axes, [(d, d ^ 1) for d in range(n_devices)])]
  transfers between devices with their start and end apart: 14 -> 14, of which waited for: 6 -> 5; matrix products, arithmetic and copies ran while one was open for 0% -> 0% of each run, Pallas kernels for 21% -> 21%
where the time goes in v9:
time: 32.5 us; the launch traced here: 32.3 us
  starting transfers between devices  17.4 us (54%)
  Pallas kernels  6.95 us (21%)
  waiting for transfers between devices  5.67 us (17%)
  local copies, waits for them, and re-layouts  0.99 us (3%)
  between operations  0.72 us (2%)
  other arithmetic  0.63 us (2%)
    pallas_call x6, Pallas kernels, call(): pl.pallas_call(kernel, out_shape=out_shape, in_specs=[SMEM] * smem + [VME...  6.95 us
    ppermute x4, starting transfers between devices, chip_grid(): came = [lax.ppermute(density, axes, pairs) for pairs in first]  6.05 us
    ppermute x4, waiting for transfers between devices, chip_grid(): came = [lax.ppermute(density, axes, pairs) for pairs in first]  5.32 us
    ppermute x2, starting transfers between devices, chip_grid(): received = [lax.ppermute(parts, axes, pairs) for pairs in early]  4.87 us
    ppermute x3, starting transfers between devices, chip_grid(): lax.ppermute(value, axes, pairs)  3.16 us
    ppermute x1, starting transfers between devices, chip_grid(): received = lax.ppermute(parts, axes, late)  2.09 us
    ppermute x4, starting transfers between devices, share(): return lax.ppermute(value, axes, [(d, d ^ 1) for d in range(n_devices)])  1.19 us
    unnamed x4, local copies, waits for them, and re-layouts  0.99 us
  transfers between devices with their start and end apart: 14, of which 5 were waited for; matrix products, arithmetic and copies ran while one was open for 0% of the time, Pallas kernels for 21%

profile of v9, /device:TPU:0, one launch (start us, length us, event | category | flops | bytes accessed | tf_op | source)
XLA Modules:
  0.0 32.3 jit_solution(4036154045761553479)
XLA Ops:
  0.6 3.0 %collective-permute-start = (bf16[512,256]{1,0:T(8,128)(2,1)}, bf16[512,256]{1,0:T(8,128)(2,1)S(1)}, u32[]{:S(2)}, u32[]{:S(2)}) collective-permute-start(bf16[512,256]{1,0:T(8,128)(2,1)} %source.1), channel_id=1, source_target_pairs={{0,2},{1,0},{2,4},{3,1},{4,6},{5,3},{6,7},{7,5},{8,10},{9,8},{10,1... | collective-permute-start | bytes 786440 | tf_op jit(solution)/shard_map/ppermute | solution.py:579
  3.7 0.0 collective-permute-start.1
  3.7 1.5 %collective-permute-start.2 = (bf16[512,256]{1,0:T(8,128)(2,1)}, bf16[512,256]{1,0:T(8,128)(2,1)S(1)}, u32[]{:S(2)}, u32[]{:S(2)}) collective-permute-start(bf16[512,256]{1,0:T(8,128)(2,1)} %source.1), channel_id=1, source_target_pairs={{0,8},{1,9},{2,10},{3,11},{4,12},{5,13},{6,14},{7,15},{8,0},{9,1},... | collective-permute-start | bytes 786440 | tf_op jit(solution)/shard_map/ppermute | solution.py:579
  5.2 1.5 %collective-permute-start.3 = (bf16[512,256]{1,0:T(8,128)(2,1)}, bf16[512,256]{1,0:T(8,128)(2,1)S(1)}, u32[]{:S(2)}, u32[]{:S(2)}) collective-permute-start(bf16[512,256]{1,0:T(8,128)(2,1)} %source.1), channel_id=1, source_target_pairs={{0,16},{1,17},{2,18},{3,19},{4,20},{5,21},{6,22},{7,23},{8,24},{9,... | collective-permute-start | bytes 786440 | tf_op jit(solution)/shard_map/ppermute | solution.py:579
  6.7 0.0 copy-start
  6.7 1.0 %copy-done = bf16[512,256]{1,0:T(8,128)(2,1)S(1)} copy-done((bf16[512,256]{1,0:T(8,128)(2,1)S(1)}, bf16[512,256]{1,0:T(8,128)(2,1)}, u32[]{:S(2)}) %copy-start) | copy-done | bytes 262168
  7.7 0.0 copy-start.1
  7.7 1.9 %collective-permute-done.refs_1_ = bf16[512,256]{1,0:T(8,128)(2,1)S(1)} collective-permute-done((bf16[512,256]{1,0:T(8,128)(2,1)}, bf16[512,256]{1,0:T(8,128)(2,1)S(1)}, u32[]{:S(2)}, u32[]{:S(2)}) %collective-permute-start) | collective-permute-done | bytes 262176 | tf_op jit(solution)/shard_map/ppermute | solution.py:579
  9.6 0.7 %collective-permute-done.1.refs_2_ = bf16[512,256]{1,0:T(8,128)(2,1)S(1)} collective-permute-done((bf16[512,256]{1,0:T(8,128)(2,1)}, bf16[512,256]{1,0:T(8,128)(2,1)S(1)}, u32[]{:S(2)}, u32[]{:S(2)}) %collective-permute-start.1) | collective-permute-done | bytes 262176 | tf_op jit(solution)/shard_map/ppermute | solution.py:579
  10.3 1.4 %collective-permute-done.2.refs_3_ = bf16[512,256]{1,0:T(8,128)(2,1)S(1)} collective-permute-done((bf16[512,256]{1,0:T(8,128)(2,1)}, bf16[512,256]{1,0:T(8,128)(2,1)S(1)}, u32[]{:S(2)}, u32[]{:S(2)}) %collective-permute-start.2) | collective-permute-done | bytes 262176 | tf_op jit(solution)/shard_map/ppermute | solution.py:579
  11.7 1.4 %collective-permute-done.3.refs_4_ = bf16[512,256]{1,0:T(8,128)(2,1)S(1)} collective-permute-done((bf16[512,256]{1,0:T(8,128)(2,1)}, bf16[512,256]{1,0:T(8,128)(2,1)S(1)}, u32[]{:S(2)}, u32[]{:S(2)}) %collective-permute-start.3) | collective-permute-done | bytes 262176 | tf_op jit(solution)/shard_map/ppermute | solution.py:579
  13.0 0.1 shard_map.43
  13.1 0.1 collective-permute-start.5
  13.2 0.5 %collective-permute-start.4 = (bf16[512,256]{1,0:T(8,128)(2,1)S(1)}, bf16[512,256]{1,0:T(8,128)(2,1)S(1)}, u32[]{:S(2)}, u32[]{:S(2)}) collective-permute-start(bf16[512,256]{1,0:T(8,128)(2,1)S(1)} %get-tuple-element.36), channel_id=1, source_target_pairs={{1,7},{2,0},{4,13},{5,1},{6,4},{7,23},{9,5},{12,14},{13,2},{14,20}... | collective-permute-start | bytes 786440 | tf_op jit(solution)/shard_map/ppermute | solution.py:585
  13.6 1.3 %collective-permute-start.8 = (bf16[512,256]{1,0:T(8,128)(2,1)S(1)}, bf16[512,256]{1,0:T(8,128)(2,1)S(1)}, u32[]{:S(2)}, u32[]{:S(2)}) collective-permute-start(bf16[512,256]{1,0:T(8,128)(2,1)S(1)} %get-tuple-element.47), channel_id=1, source_target_pairs={{2,7},{4,0},{7,14},{11,15},{12,3},{14,22},{16,4},{18,6},{21,1},{22... | collective-permute-start | bytes 786440 | tf_op jit(solution)/shard_map/ppermute | solution.py:585
  14.9 1.4 %collective-permute-start.9 = (bf16[512,256]{1,0:T(8,128)(2,1)S(1)}, bf16[512,256]{1,0:T(8,128)(2,1)S(1)}, u32[]{:S(2)}, u32[]{:S(2)}) collective-permute-start(bf16[512,256]{1,0:T(8,128)(2,1)S(1)} %get-tuple-element.50), channel_id=1, source_target_pairs={{3,13},{4,12},{6,22},{7,2},{10,14},{11,3},{12,11},{14,6},{15,7},{2... | collective-permute-start | bytes 786440 | tf_op jit(solution)/shard_map/ppermute | solution.py:585
  16.4 0.0 collective-permute-done.5.refs_5_
  16.4 0.0 copy-done.1
  16.4 1.9 %shard_map.44 = f32[8,128]{1,0:T(8,128)S(1)} custom-call(s32[16,16]{1,0:T(8,128)S(1)} %copy-done.1, bf16[512,256]{1,0:T(8,128)(2,1)S(1)} %shard_map.41.refs_0_, bf16[512,256]{1,0:T(8,128)(2,1)S(1)} %collective-permute-done.refs_1_, bf16[512,256]{1,0:T(8,128)(2,1)S(1)} %collective-permute-done.1.refs_2_, bf16[512,256]{1,0:T(8,128)(2,1)S(1)} %collective-permute-done.2.refs_3_, ...), custom_call_target="tpu_custom_call" | custom-call | tf_op jit(solution)/shard_map/pallas_call | solution.py:562
  18.3 1.3 %collective-permute-start.6 = (f32[8,128]{1,0:T(8,128)S(1)}, f32[8,128]{1,0:T(8,128)S(1)}, u32[]{:S(2)}, u32[]{:S(2)}) collective-permute-start(f32[8,128]{1,0:T(8,128)S(1)} %shard_map.44), channel_id=1, source_target_pairs={{16,0},{17,1},{6,2},{7,3},{2,4},{3,5},{14,6},{15,7},{4,8},{5,9},{2... | collective-permute-start | bytes 12296 | tf_op jit(solution)/shard_map/ppermute | solution.py:595
  19.5 3.6 %collective-permute-start.7 = (f32[8,128]{1,0:T(8,128)S(1)}, f32[8,128]{1,0:T(8,128)S(1)}, u32[]{:S(2)}, u32[]{:S(2)}) collective-permute-start(f32[8,128]{1,0:T(8,128)S(1)} %shard_map.44), channel_id=1, source_target_pairs={{24,0},{25,1},{28,2},{29,3},{20,4},{21,5},{14,6},{15,7},{0,8},{1,9... | collective-permute-start | bytes 12296 | tf_op jit(solution)/shard_map/ppermute | solution.py:595
  23.1 2.3 %shard_map.45 = (bf16[512,2048]{1,0:T(8,128)(2,1)S(1)}, bf16[2048,256]{1,0:T(8,128)(2,1)S(1)}, bf16[512,256]{1,0:T(8,128)(2,1)S(1)}) custom-call(s32[16,16]{1,0:T(8,128)S(1)} %copy-done.1, bf16[512,256]{1,0:T(8,128)(2,1)S(1)} %shard_map.41.refs_0_, bf16[512,256]{1,0:T(8,128)(2,1)S(1)} %collective-permute-done.refs_1_, ...), custom_call_target="tpu_custom_call" | custom-call | tf_op jit(solution)/shard_map/pallas_call | solution.py:562
  25.4 0.0 collective-permute-done.6
  25.4 0.3 collective-permute-done.7
  25.8 0.0 collective-permute-done.4.refs_0_
  25.8 0.0 collective-permute-done.8.refs_1_
  25.8 0.0 collective-permute-done.9.refs_2_
  25.8 0.6 %collective-permute-start.12 = (bf16[512,256]{1,0:T(8,128)(2,1)S(1)}, bf16[512,256]{1,0:T(8,128)(2,1)S(1)}, u32[]{:S(2)}, u32[]{:S(2)}) collective-permute-start(bf16[512,256]{1,0:T(8,128)(2,1)S(1)} %collective-permute-done.9.refs_2_), channel_id=1, source_target_pairs={{0,1},{1,0},{2,3},{3,2},{4,5},{5,4},{6,7},{7,6},{8,9},{9,8},{10,11... | collective-permute-start | bytes 786440 | tf_op jit(solution)/shard_map/ppermute | solution.py:574
  26.4 0.1 collective-permute-start.11
  26.5 0.4 %collective-permute-start.10 = (bf16[512,256]{1,0:T(8,128)(2,1)S(1)}, bf16[512,256]{1,0:T(8,128)(2,1)S(1)}, u32[]{:S(2)}, u32[]{:S(2)}) collective-permute-start(bf16[512,256]{1,0:T(8,128)(2,1)S(1)} %collective-permute-done.4.refs_0_), channel_id=1, source_target_pairs={{0,1},{1,0},{2,3},{3,2},{4,5},{5,4},{6,7},{7,6},{8,9},{9,8},{10,11... | collective-permute-start | bytes 786440 | tf_op jit(solution)/shard_map/ppermute | solution.py:574
  26.9 2.1 %collective-permute-start.13 = (f32[8,128]{1,0:T(8,128)S(1)}, f32[8,128]{1,0:T(8,128)S(1)}, u32[]{:S(2)}, u32[]{:S(2)}) collective-permute-start(f32[8,128]{1,0:T(8,128)S(1)} %compare_select_fusion.1), channel_id=1, source_target_pairs={{2,0},{3,1},{0,2},{1,3},{6,4},{7,5},{4,6},{5,7},{24,8},{25,9},{12,... | collective-permute-start | bytes 12296 | tf_op jit(solution)/shard_map/ppermute | solution.py:600
  29.0 0.0 collective-permute-done.12.refs_5_
  29.0 0.0 collective-permute-done.11.refs_4_
  29.0 0.0 collective-permute-done.10.refs_3_
  29.0 2.7 %shard_map.46 = (bf16[512,2048]{1,0:T(8,128)(2,1)S(1)}, bf16[2048,256]{1,0:T(8,128)(2,1)S(1)}, bf16[512,256]{1,0:T(8,128)(2,1)}) custom-call(bf16[512,256]{1,0:T(8,128)(2,1)S(1)} %collective-permute-done.4.refs_0_, bf16[512,256]{1,0:T(8,128)(2,1)S(1)} %collective-permute-done.8.refs_1_, ...), custom_call_target="tpu_custom_call", output_to_operand_aliasing={{0}: (7, {}), {1}: (8, {})} | custom-call | tf_op jit(solution)/shard_map/pallas_call | solution.py:562
  31.7 0.0 collective-permute-done.13
  31.7 0.6 %fusion = f32[2]{0:T(128)} fusion(f32[8,128]{1,0:T(8,128)S(1)} %collective-permute-done.13, f32[8,128]{1,0:T(8,128)S(1)} %compare_select_fusion.1), kind=kLoop, calls=%fused_computation.3 | loop fusion | flops 766 | bytes 2056 | tf_op jit(solution)/shard_map/reduce_sum | solution.py:616
  (3 shorter events, 0.0 us)
Async XLA Ops:
  0.6 8.9 %collective-permute-start = (bf16[512,256]{1,0:T(8,128)(2,1)}, bf16[512,256]{1,0:T(8,128)(2,1)S(1)}, u32[]{:S(2)}, u32[]{:S(2)}) collective-permute-start(bf16[512,256]{1,0:T(8,128)(2,1)} %source.1), channel_id=1, source_target_pairs={{0,2},{1,0},{2,4},{3,1},{4,6},{5,3},{6,7},{7,5},{8,10},{9,8},{10,1... | collective-permute-start | bytes 786440 | tf_op jit(solution)/shard_map/ppermute | solution.py:579
  3.7 6.6 %collective-permute-start.1 = (bf16[512,256]{1,0:T(8,128)(2,1)}, bf16[512,256]{1,0:T(8,128)(2,1)S(1)}, u32[]{:S(2)}, u32[]{:S(2)}) collective-permute-start(bf16[512,256]{1,0:T(8,128)(2,1)} %source.1), channel_id=1, source_target_pairs={{0,1},{1,3},{2,0},{3,5},{4,2},{5,7},{6,4},{7,6},{8,9},{9,11},{10,8... | collective-permute-start | bytes 786440 | tf_op jit(solution)/shard_map/ppermute | solution.py:579
  3.7 8.0 %collective-permute-start.2 = (bf16[512,256]{1,0:T(8,128)(2,1)}, bf16[512,256]{1,0:T(8,128)(2,1)S(1)}, u32[]{:S(2)}, u32[]{:S(2)}) collective-permute-start(bf16[512,256]{1,0:T(8,128)(2,1)} %source.1), channel_id=1, source_target_pairs={{0,8},{1,9},{2,10},{3,11},{4,12},{5,13},{6,14},{7,15},{8,0},{9,1},... | collective-permute-start | bytes 786440 | tf_op jit(solution)/shard_map/ppermute | solution.py:579
  5.2 7.9 %collective-permute-start.3 = (bf16[512,256]{1,0:T(8,128)(2,1)}, bf16[512,256]{1,0:T(8,128)(2,1)S(1)}, u32[]{:S(2)}, u32[]{:S(2)}) collective-permute-start(bf16[512,256]{1,0:T(8,128)(2,1)} %source.1), channel_id=1, source_target_pairs={{0,16},{1,17},{2,18},{3,19},{4,20},{5,21},{6,22},{7,23},{8,24},{9,... | collective-permute-start | bytes 786440 | tf_op jit(solution)/shard_map/ppermute | solution.py:579
  6.7 1.0 %copy-start = (bf16[512,256]{1,0:T(8,128)(2,1)S(1)}, bf16[512,256]{1,0:T(8,128)(2,1)}, u32[]{:S(2)}) copy-start(bf16[512,256]{1,0:T(8,128)(2,1)} %source.1) | copy-start | bytes 786436
  7.7 8.7 %copy-start.1 = (s32[16,16]{1,0:T(8,128)S(1)}, s32[16,16]{1,0:T(8,128)}, u32[]{:S(2)}) copy-start(s32[16,16]{1,0:T(8,128)} %pattern.3) | copy-start | bytes 3076
  13.1 3.2 %collective-permute-start.5 = (bf16[5,512,256]{2,1,0:T(8,128)(2,1)S(1)}, bf16[5,512,256]{2,1,0:T(8,128)(2,1)S(1)}, u32[]{:S(2)}, u32[]{:S(2)}) collective-permute-start(bf16[5,512,256]{2,1,0:T(8,128)(2,1)S(1)} %shard_map.43), channel_id=1, source_target_pairs={{0,1},{1,0},{2,3},{3,2},{4,5},{5,4},{6,7},{7,6},{8,9},{9,8},{10,11... | collective-permute-start | bytes 3932168 | tf_op jit(solution)/shard_map/ppermute | solution.py:574
  13.2 12.6 %collective-permute-start.4 = (bf16[512,256]{1,0:T(8,128)(2,1)S(1)}, bf16[512,256]{1,0:T(8,128)(2,1)S(1)}, u32[]{:S(2)}, u32[]{:S(2)}) collective-permute-start(bf16[512,256]{1,0:T(8,128)(2,1)S(1)} %get-tuple-element.36), channel_id=1, source_target_pairs={{1,7},{2,0},{4,13},{5,1},{6,4},{7,23},{9,5},{12,14},{13,2},{14,20}... | collective-permute-start | bytes 786440 | tf_op jit(solution)/shard_map/ppermute | solution.py:585
  13.6 12.1 %collective-permute-start.8 = (bf16[512,256]{1,0:T(8,128)(2,1)S(1)}, bf16[512,256]{1,0:T(8,128)(2,1)S(1)}, u32[]{:S(2)}, u32[]{:S(2)}) collective-permute-start(bf16[512,256]{1,0:T(8,128)(2,1)S(1)} %get-tuple-element.47), channel_id=1, source_target_pairs={{2,7},{4,0},{7,14},{11,15},{12,3},{14,22},{16,4},{18,6},{21,1},{22... | collective-permute-start | bytes 786440 | tf_op jit(solution)/shard_map/ppermute | solution.py:585
  14.9 10.8 %collective-permute-start.9 = (bf16[512,256]{1,0:T(8,128)(2,1)S(1)}, bf16[512,256]{1,0:T(8,128)(2,1)S(1)}, u32[]{:S(2)}, u32[]{:S(2)}) collective-permute-start(bf16[512,256]{1,0:T(8,128)(2,1)S(1)} %get-tuple-element.50), channel_id=1, source_target_pairs={{3,13},{4,12},{6,22},{7,2},{10,14},{11,3},{12,11},{14,6},{15,7},{2... | collective-permute-start | bytes 786440 | tf_op jit(solution)/shard_map/ppermute | solution.py:585
  18.3 7.2 %collective-permute-start.6 = (f32[8,128]{1,0:T(8,128)S(1)}, f32[8,128]{1,0:T(8,128)S(1)}, u32[]{:S(2)}, u32[]{:S(2)}) collective-permute-start(f32[8,128]{1,0:T(8,128)S(1)} %shard_map.44), channel_id=1, source_target_pairs={{16,0},{17,1},{6,2},{7,3},{2,4},{3,5},{14,6},{15,7},{4,8},{5,9},{2... | collective-permute-start | bytes 12296 | tf_op jit(solution)/shard_map/ppermute | solution.py:595
  19.5 6.2 %collective-permute-start.7 = (f32[8,128]{1,0:T(8,128)S(1)}, f32[8,128]{1,0:T(8,128)S(1)}, u32[]{:S(2)}, u32[]{:S(2)}) collective-permute-start(f32[8,128]{1,0:T(8,128)S(1)} %shard_map.44), channel_id=1, source_target_pairs={{24,0},{25,1},{28,2},{29,3},{20,4},{21,5},{14,6},{15,7},{0,8},{1,9... | collective-permute-start | bytes 12296 | tf_op jit(solution)/shard_map/ppermute | solution.py:595
  25.8 3.2 %collective-permute-start.12 = (bf16[512,256]{1,0:T(8,128)(2,1)S(1)}, bf16[512,256]{1,0:T(8,128)(2,1)S(1)}, u32[]{:S(2)}, u32[]{:S(2)}) collective-permute-start(bf16[512,256]{1,0:T(8,128)(2,1)S(1)} %collective-permute-done.9.refs_2_), channel_id=1, source_target_pairs={{0,1},{1,0},{2,3},{3,2},{4,5},{5,4},{6,7},{7,6},{8,9},{9,8},{10,11... | collective-permute-start | bytes 786440 | tf_op jit(solution)/shard_map/ppermute | solution.py:574
  26.4 2.6 %collective-permute-start.11 = (bf16[512,256]{1,0:T(8,128)(2,1)S(1)}, bf16[512,256]{1,0:T(8,128)(2,1)S(1)}, u32[]{:S(2)}, u32[]{:S(2)}) collective-permute-start(bf16[512,256]{1,0:T(8,128)(2,1)S(1)} %collective-permute-done.8.refs_1_), channel_id=1, source_target_pairs={{0,1},{1,0},{2,3},{3,2},{4,5},{5,4},{6,7},{7,6},{8,9},{9,8},{10,11... | collective-permute-start | bytes 786440 | tf_op jit(solution)/shard_map/ppermute | solution.py:574
  26.5 2.5 %collective-permute-start.10 = (bf16[512,256]{1,0:T(8,128)(2,1)S(1)}, bf16[512,256]{1,0:T(8,128)(2,1)S(1)}, u32[]{:S(2)}, u32[]{:S(2)}) collective-permute-start(bf16[512,256]{1,0:T(8,128)(2,1)S(1)} %collective-permute-done.4.refs_0_), channel_id=1, source_target_pairs={{0,1},{1,0},{2,3},{3,2},{4,5},{5,4},{6,7},{7,6},{8,9},{9,8},{10,11... | collective-permute-start | bytes 786440 | tf_op jit(solution)/shard_map/ppermute | solution.py:574
  26.9 4.8 %collective-permute-start.13 = (f32[8,128]{1,0:T(8,128)S(1)}, f32[8,128]{1,0:T(8,128)S(1)}, u32[]{:S(2)}, u32[]{:S(2)}) collective-permute-start(f32[8,128]{1,0:T(8,128)S(1)} %compare_select_fusion.1), channel_id=1, source_target_pairs={{2,0},{3,1},{0,2},{1,3},{6,4},{7,5},{4,6},{5,7},{24,8},{25,9},{12,... | collective-permute-start | bytes 12296 | tf_op jit(solution)/shard_map/ppermute | solution.py:600
